TPU v7x, 32 devices: a whole 2x2x4 slice. The times are simulated.
32 devices in a mesh: runs: 2 (over y), tm: 2 (over x), cells: 4 (over z), feat: 2 (over core).
Axes of the slice: x: 2, y: 2, z: 4, core: 2. Of those that a mesh axis runs over, the one named last changes fastest.
Arguments:
- principal_coordinates: bfloat16 [4, 64, 8192], P(('runs', 'tm'), None, ('cells', 'feat')), parts along dimension 0, may hold values from -6 to 6
- present_potentials: float32 [4, 8192], P(('runs', 'tm'), ('cells', 'feat')), parts along dimension 0, may hold values from 0.25 to 4
- destination_tiles: int32 [4, 32, 8], P(('runs', 'tm'), ('cells', 'feat')), parts along dimension 0, may hold values from 0 to 31, as said below
- living_totals: int32 [4], P('runs'), parts along dimension 0, may hold values from 4096 to 8192, as said below
Outputs:
- renewed_potentials: float32 [4, 8192], P(('runs', 'tm'), ('cells', 'feat')), parts along dimension 0
- prior_projections: float32 [4, 8192], P(('runs', 'tm'), ('cells', 'feat')), parts along dimension 0
There are 2 independent parts, one for each index of `runs`. A program takes and returns all parts, laid end to end along the dimension named above; each array names one. Nothing has to cross between parts.
Inputs may be any that keep to these rules, and one draw needn't show every extreme that they name: `destination_tiles`: row b of time t lists 8 distinct blocks: 4 distinct values c below 16, b modulo 32/2 among them, each together with c + 16. The lists of the last time point are not used. The live cells of time t are its first living_totals[t] cells; in every draw one time point is full.
All inputs are finite; a program needn't handle non-finite values.
Results may differ from a plain program's by a relative error of at most 0.0003.
Values may be sent and summed in bfloat16 or wider, within the bound.
No kernel may reach another device: no remote copies, remote signals or barrier semaphores. Data moves between devices by JAX's collectives and lax.ppermute only.
A program may use at most 64 MiB of HBM per device.

v0:
```python
import jax
import jax.numpy as jnp
from jax import lax
from jax.sharding import PartitionSpec as P

spread = 0.5
highest = lax.Precision.HIGHEST


def shifted(block, axis, distance):
    devices = range(lax.axis_size(axis))
    route = [(i - distance, i) for i in devices if i - distance in devices]
    return lax.ppermute(block, axis, route)


def extended(cells, sides, width):
    for axis, dim in sides:
        count = lax.axis_size(axis)
        ends = count - 1
        head = lax.slice_in_dim(cells, 0, width, axis=dim)
        tail = lax.slice_in_dim(cells, cells.shape[dim] - width, cells.shape[dim], axis=dim)
        cells = jnp.concatenate(
            [
                lax.ppermute(tail, axis, [(i, (i + 1) % count) for i in range(ends)]),
                cells,
                lax.ppermute(head, axis, [((i + 1) % count, i) for i in range(ends)]),
            ],
            axis=dim,
        )
    return cells


def build_tiles(own_feats, later_feats, block_lists):
    feat_count, row_count = own_feats.shape
    source_count, list_len = block_lists.shape
    block_len = row_count // source_count
    block_total = later_feats.shape[1] // block_len
    sources = own_feats.reshape(feat_count, source_count, block_len)
    chosen = later_feats.reshape(feat_count, block_total, block_len)[:, block_lists]
    inner_prod = jnp.einsum("dsi,dsnj->snij", sources, chosen, preferred_element_type=jnp.float32)
    source_sq = jnp.sum(jnp.square(sources.astype(jnp.float32)), axis=0)
    target_sq = jnp.sum(jnp.square(chosen.astype(jnp.float32)), axis=0)
    distance = (
        source_sq[:, None, :, None] + target_sq[:, :, None, :] - 2.0 * inner_prod
    ) / feat_count
    return jnp.exp((2.0 - distance) / spread) / (2 * list_len * block_len)


def on_device(principal_coordinates, present_potentials, destination_tiles, living_totals):
    own_feats = principal_coordinates[0]
    dual_potentials = present_potentials[0]
    block_lists = destination_tiles[0]
    feat_count, row_count = own_feats.shape
    source_count, list_len = block_lists.shape
    block_len = row_count // source_count
    group_size = lax.axis_size(("cells", "feat"))
    block_total = source_count * group_size
    cell_total = block_total * block_len
    time_count = lax.axis_size("tm")
    time_here = lax.axis_index("tm")
    later_shard = shifted(own_feats, "tm", -1)
    later_feats = lax.all_gather(later_shard, ("cells", "feat"), axis=1, tiled=True)
    positions = lax.axis_index(("cells", "feat")) * row_count + lax.broadcasted_iota(
        jnp.int32, (row_count,), 0
    )
    time_ids = lax.broadcasted_iota(jnp.int32, living_totals.shape, 0)
    count_here = jnp.sum(jnp.where(time_ids == time_here, living_totals, 0))
    living_sample_flags = (positions < count_here).astype(jnp.float32)
    block_ids = lax.broadcasted_iota(jnp.int32, (1, block_total), 1)
    selector = (block_lists.reshape(-1)[:, None] == block_ids).astype(jnp.float32)

    def advance(sweep_index, state):
        rightward_belief, leftward_belief = state
        kernel_tiles = build_tiles(own_feats, later_feats, block_lists)
        sending = dual_potentials * leftward_belief * living_sample_flags
        running_belief = (dual_potentials * rightward_belief * living_sample_flags).reshape(
            source_count, block_len
        )
        pushed = jnp.einsum("snij,si->snj", kernel_tiles, running_belief, precision=highest)
        scattered = jnp.einsum(
            "ka,kj->aj",
            selector,
            pushed.reshape(source_count * list_len, block_len),
            precision=highest,
        )
        forward_share = lax.psum_scatter(
            scattered.reshape(cell_total), ("cells", "feat"), scatter_dimension=0, tiled=True
        )
        neighbours = extended(jnp.stack([forward_share, sending])[None], (("tm", 0),), 1)
        forward_from = neighbours[0, 0]
        successor_kernel = lax.all_gather(neighbours[2, 1], ("cells", "feat"), axis=0, tiled=True)
        picked = jnp.dot(
            selector, successor_kernel.reshape(block_total, block_len), precision=highest
        )
        pulled = jnp.einsum(
            "snij,snj->si",
            kernel_tiles,
            picked.reshape(source_count, list_len, block_len),
            precision=highest,
        )
        forward_next = jnp.where(time_here == 0, 1.0, forward_from)
        backward_next = jnp.where(time_here == time_count - 1, 1.0, pulled.reshape(row_count))
        return (forward_next, backward_next)

    unit_msg = jnp.ones((row_count,), jnp.float32)
    rightward_belief, leftward_belief = lax.fori_loop(
        0, time_count - 1, advance, (unit_msg, unit_msg)
    )
    prior_projections = dual_potentials * rightward_belief * leftward_belief * living_sample_flags
    wanted_density = living_sample_flags * cell_total / count_here.astype(jnp.float32)
    safe_multiplied = jnp.where(living_sample_flags > 0, prior_projections, 1.0)
    new_scales = jnp.where(
        living_sample_flags > 0, dual_potentials * jnp.sqrt(wanted_density / safe_multiplied), 0.0
    )
    return (new_scales[None], prior_projections[None])


def solution(mesh):
    in_specs = (
        P(("runs", "tm"), None, ("cells", "feat")),
        P(("runs", "tm"), ("cells", "feat")),
        P(("runs", "tm"), ("cells", "feat"), None),
        P("runs"),
    )
    out_specs = (P(("runs", "tm"), ("cells", "feat")), P(("runs", "tm"), ("cells", "feat")))
    return jax.shard_map(
        on_device, mesh=mesh, in_specs=in_specs, out_specs=out_specs, check_vma=False
    )
```

profile of v0, /device:TPU:0, one launch (start us, length us, event | category | flops | bytes accessed | tf_op | source)
XLA Modules:
  0.0 119.0 jit_solution(4175739387812048912)
XLA Ops:
  7.2 0.0 all-gather.3.cloned.1.call-start
  7.2 1.3 %collective-permute-start = (bf16[64,1024]{1,0:T(8,128)(2,1)}, bf16[64,1024]{1,0:T(8,128)(2,1)S(1)}, u32[]{:S(2)}, u32[]{:S(2)}) collective-permute-start(bf16[64,1024]{1,0:T(8,128)(2,1)} %bitcast.76), channel_id=1, source_target_pairs={{8,0},{9,1},{10,2},{11,3},{12,4},{13,5},{14,6},{15,7},{24,16},{25,... | collective-permute-start | bytes 393224 | tf_op jit(solution)/shard_map/ppermute | solution.py:13
  8.5 6.7 %collective-permute-done = bf16[64,1024]{1,0:T(8,128)(2,1)S(1)} collective-permute-done((bf16[64,1024]{1,0:T(8,128)(2,1)}, bf16[64,1024]{1,0:T(8,128)(2,1)S(1)}, u32[]{:S(2)}, u32[]{:S(2)}) %collective-permute-start) | collective-permute-done | bytes 131104 | tf_op jit(solution)/shard_map/ppermute | solution.py:13
  15.2 0.0 copy-start.1
  15.2 0.6 copy-done.1
  15.8 0.0 all-gather.3.cloned.1.call-update
  15.8 1.0 reshape_squeeze.4
  16.8 0.8 eq.56
  17.6 0.7 compare_select_fusion.2
  18.3 0.1 reshape.139
  18.4 0.9 multiply_reduce_fusion.1
  19.3 1.3 %fusion.38 = s32[]{:T(128)} fusion(s32[2]{0:T(128)} %param.7, s32[]{:T(128)S(6)} %axis_index.38), kind=kLoop, calls=%fused_computation.56 | loop fusion | flops 5 | bytes 16 | tf_op jit(solution)/shard_map/reduce_sum | solution.py:67
  20.6 0.5 broadcast.218
  21.1 1.9 %fusion.46 = (f32[1024]{0:T(1024)S(1)}, f32[1,1024]{1,0:T(1,128)S(1)}) fusion(f32[1,1024]{1,0:T(1,128)} %param.5, f32[]{:T(128)} %broadcast.218, s32[]{:T(128)} %fusion.38, s32[]{:T(128)S(6)} %mul.49), kind=kLoop, calls=%fused_computation.63 | loop fusion | flops 3072 | bytes 12300 | tf_op args[1]
  23.1 1.2 %dynamic-slice = u32[1]{0:T(128)} dynamic-slice(u32[32]{0:T(128)} %constant.63, u32[]{:T(128)S(6)} %add.78), dynamic_slice_sizes={1} | dynamic-slice | bytes 12
  25.0 0.6 select_bitcast_fusion
  25.6 13.8 %all-gather.3.cloned.1.call-done = bf16[64,8192]{1,0:T(8,128)(2,1)} async-done(((bf16[64,1024]{1,0:T(8,128)(2,1)}), bf16[64,8192]{1,0:T(8,128)(2,1)}) %all-gather.3.cloned.1.call-update) | async-done | bytes 1048592 | tf_op jit(solution)/shard_map/all_gather | solution.py:62
  39.3 1.3 %copy.44 = bf16[8,32,8,256]{3,2,0,1:T(8,128)(2,1)S(1)} copy(bf16[8,32,8,256]{3,2,1,0:T(8,128)(2,1)} %bitcast.74) | data formatting | bytes 2097152 | tf_op jit(solution)/shard_map/while/body/eval_jaxpr/reshape | solution.py:39
  40.7 0.6 gather_fusion
  41.3 0.3 multiply_reduce_fusion
  41.6 1.3 %fusion.21 = f32[4,8,256,256]{3,2,1,0:T(8,128)S(1)} fusion(bf16[64,4,8,256]{3,0,2,1:T(8,128)(2,1)S(1)} %bitcast.72, bf16[64,4,256,1]{2,1,0,3:T(4,128)(2,1)S(1)} %bitcast.75), kind=kOutput, calls=%fused_computation.26 | convolution fusion | flops 268435456 | bytes 9568256 | tf_op jit(solution)/shard_map/while/body/eval_jaxpr/dsi,dsnj->snij/dot_general | solution.py:40
  42.9 0.0 copy-start
  42.9 0.0 copy-start.2
  42.9 10.3 %fusion.7 = f32[4,1,8,256]{3,1,2,0:T(1,128)S(1)} fusion(f32[4,8,256,256]{3,2,1,0:T(8,128)S(1)} %fusion.21, f32[4,8,256]{2,1,0:T(8,128)S(1)} %multiply_reduce_fusion, f32[4,256]{1,0:T(4,128)S(1)} %add.70, f32[4,256,1,1]{1,0,2,3:T(4,128)S(1)} %select_bitcast_fusion), kind=kOutput, calls=%fused_computation.8 | convolution fusion | flops 39845888 | bytes 8462336 | tf_op jit(solution)/shard_map/while/body/eval_jaxpr/snij,si->snj/dot_general | solution.py:79
  53.2 0.0 copy-done
  53.2 0.3 convolution_bitcast_fusion.1
  53.5 27.5 %all-reduce = f32[8192]{0:T(1024)S(1)} all-reduce(f32[8192]{0:T(1024)S(1)} %bitcast.77), channel_id=3, replica_groups=mesh['runs'=2,'tm'=2,'cells'=4,'feat'=2] {'cells','feat'}, use_global_device_ids=true, to_apply=%region_3.0.clone | all-reduce | flops 8192 | bytes 65536
  81.0 1.3 %collective-permute-start.2 = (f32[1,2,1024]{2,1,0:T(2,128)S(1)}, f32[1,2,1024]{2,1,0:T(2,128)S(1)}, u32[]{:S(2)}, u32[]{:S(2)}) collective-permute-start(f32[1,2,1024]{2,1,0:T(2,128)S(1)} %maximum_bitcast_fusion), channel_id=1, source_target_pairs={{8,0},{9,1},{10,2},{11,3},{12,4},{13,5},{14,6},{15,7},{24,16},{25,... | collective-permute-start | bytes 24584 | tf_op jit(solution)/shard_map/while/body/eval_jaxpr/ppermute | solution.py:26
  82.9 4.5 %collective-permute-start.1 = (f32[1,2,1024]{2,1,0:T(2,128)S(1)}, f32[1,2,1024]{2,1,0:T(2,128)S(1)}, u32[]{:S(2)}, u32[]{:S(2)}) collective-permute-start(f32[1,2,1024]{2,1,0:T(2,128)S(1)} %maximum_bitcast_fusion), channel_id=1, source_target_pairs={{0,8},{1,9},{2,10},{3,11},{4,12},{5,13},{6,14},{7,15},{16,24},{17,... | collective-permute-start | bytes 24584 | tf_op jit(solution)/shard_map/while/body/eval_jaxpr/ppermute | solution.py:24
  87.4 0.0 collective-permute-done.2
  87.4 14.0 %all-gather = f32[1,1,8192]{2,1,0:T(1,128)S(1)} all-gather(f32[1,1,1024]{2,1,0:T(1,128)S(1)} %slice.13), channel_id=2, replica_groups=mesh['runs'=2,'tm'=2,'cells'=4,'feat'=2] {'cells','feat'}, dimensions={2}, use_global_device_ids=true | all-gather | bytes 36864 | tf_op jit(solution)/shard_map/while/body/eval_jaxpr/all_gather | solution.py:91
  101.5 0.0 copy-done.2
  101.5 0.2 convolution_bitcast_fusion
  101.7 0.0 copy-start.3
  101.7 9.3 %fusion.5 = f32[4,1,256,1]{2,1,3,0:T(1,128)S(1)} fusion(f32[4,8,256,256]{3,2,1,0:T(8,128)} %copy-done, f32[4,8,256]{2,1,0:T(8,128)S(1)} %multiply_reduce_fusion, f32[4,256]{1,0:T(4,128)S(1)} %add.70, f32[4,8,256,1]{2,1,0,3:T(8,128)S(1)} %convolution_bitcast_fusion), kind=kOutput, calls=%fused_computation.7 | convolution fusion | flops 39845888 | bytes 8462336 | tf_op jit(solution)/shard_map/while/body/eval_jaxpr/snij,snj->si/dot_general | solution.py:95
  111.0 0.0 collective-permute-done.1
  111.0 0.0 copy-done.3
  111.0 1.2 %compare_select_fusion = (f32[1,1024]{1,0:T(1,128)}, f32[1,1024]{1,0:T(1,128)}) fusion(f32[1,1024]{1,0:T(1,128)S(1)} %copy-done.3, f32[]{:T(128)S(6)} %convert_element_type.24, s32[]{:T(128)} %fusion.38, s32[]{:T(128)S(6)} %mul.49, f32[1,1024]{1,0:T(1,128)S(1)} %bitcast.80, f32[1,2,1024]{2,1,0:T(2,128)S(1)} %collective-permute-done.1, pred[]{:T(512)S(6)} %eq.55), kind=kLoop, calls=%fused_computation.34 | loop fusion | flops 14336 | bytes 20493 | tf_op jit(solution)/shard_map/jit(_where)/select_n | solution.py:112
  (9 shorter events, 0.1 us)
Async XLA Ops:
  7.2 32.2 %all-gather.3.cloned.1.call-start = ((), (), s32[]{:S(2)}) async-start(), calls=%async_computation | async-start | bytes 1179648 | tf_op jit(solution)/shard_map/all_gather | solution.py:62
  7.2 8.0 %collective-permute-start = (bf16[64,1024]{1,0:T(8,128)(2,1)}, bf16[64,1024]{1,0:T(8,128)(2,1)S(1)}, u32[]{:S(2)}, u32[]{:S(2)}) collective-permute-start(bf16[64,1024]{1,0:T(8,128)(2,1)} %bitcast.76), channel_id=1, source_target_pairs={{8,0},{9,1},{10,2},{11,3},{12,4},{13,5},{14,6},{15,7},{24,16},{25,... | collective-permute-start | bytes 393224 | tf_op jit(solution)/shard_map/ppermute | solution.py:13
  15.2 0.6 copy-start.1
  42.9 10.3 %copy-start = (f32[4,8,256,256]{3,2,1,0:T(8,128)}, f32[4,8,256,256]{3,2,1,0:T(8,128)S(1)}, u32[]{:S(2)}) copy-start(f32[4,8,256,256]{3,2,1,0:T(8,128)S(1)} %fusion.21) | copy-start | bytes 25165828
  42.9 58.6 %copy-start.2 = (s32[1,4,8]{2,1,0:T(4,128)S(1)}, s32[1,4,8]{2,1,0:T(4,128)}, u32[]{:S(2)}) copy-start(s32[1,4,8]{2,1,0:T(4,128)} %param.6) | copy-start | bytes 388
  81.0 6.4 %collective-permute-start.2 = (f32[1,2,1024]{2,1,0:T(2,128)S(1)}, f32[1,2,1024]{2,1,0:T(2,128)S(1)}, u32[]{:S(2)}, u32[]{:S(2)}) collective-permute-start(f32[1,2,1024]{2,1,0:T(2,128)S(1)} %maximum_bitcast_fusion), channel_id=1, source_target_pairs={{8,0},{9,1},{10,2},{11,3},{12,4},{13,5},{14,6},{15,7},{24,16},{25,... | collective-permute-start | bytes 24584 | tf_op jit(solution)/shard_map/while/body/eval_jaxpr/ppermute | solution.py:26
  82.9 28.1 %collective-permute-start.1 = (f32[1,2,1024]{2,1,0:T(2,128)S(1)}, f32[1,2,1024]{2,1,0:T(2,128)S(1)}, u32[]{:S(2)}, u32[]{:S(2)}) collective-permute-start(f32[1,2,1024]{2,1,0:T(2,128)S(1)} %maximum_bitcast_fusion), channel_id=1, source_target_pairs={{0,8},{1,9},{2,10},{3,11},{4,12},{5,13},{6,14},{7,15},{16,24},{17,... | collective-permute-start | bytes 24584 | tf_op jit(solution)/shard_map/while/body/eval_jaxpr/ppermute | solution.py:24
  101.7 9.3 %copy-start.3 = (f32[1,1024]{1,0:T(1,128)S(1)}, f32[1,1024]{1,0:T(1,128)}, u32[]{:S(2)}) copy-start(f32[1,1024]{1,0:T(1,128)} %param.5) | copy-start | bytes 12292
Sparse Core Ops, SparseCore 0:
  16.0 23.3 all-gather.2
where the time goes:
time: 119 us
  blocking collectives  41.5 us (35%)
  matrix products  21.3 us (18%)
  waiting for transfers between devices  20.5 us (17%)
  between operations  15.5 us (13%)
  starting transfers between devices  7.16 us (6%)
  other arithmetic  6.87 us (6%)
  local copies, waits for them, and re-layouts  6.26 us (5%)
    unnamed x1, blocking collectives  27.5 us
    all_gather x1, blocking collectives, advance(): lax.all_gather(neighbours[2, 1], ('cells', 'feat'), axis=0, tiled=True)  14 us
    all_gather x1, waiting for transfers between devices, on_device(): lax.all_gather(later_shard, ('cells', 'feat'), axis=1, tiled=True)  13.8 us
    dot_general x1, matrix products, advance(): jnp.einsum('snij,si->snj', kernel_tiles, running_belief, precision=highest)  10.3 us
    dot_general x1, matrix products, advance(): jnp.einsum('snij,snj->si', kernel_tiles, picked.reshape(source_count, lis...  9.25 us
    ppermute x1, waiting for transfers between devices, shifted(): return lax.ppermute(block, axis, route)  6.66 us
    ppermute x1, starting transfers between devices, extended(): lax.ppermute(tail, axis, [(i, (i + 1) % count) for i in range(ends)])  4.54 us
    unnamed x13, local copies, waits for them, and re-layouts  2.44 us
  transfers between devices with their start and end apart: 4, of which 2 were waited for; matrix products, arithmetic and copies ran while one was open for 16% of the time, Pallas kernels for 0%

commit v1 on v0

v1 whole, which is shorter than its diff:
```python
import functools
import math

import jax
import jax.numpy as jnp
from jax import lax
from jax.experimental import pallas as pl
from jax.experimental.pallas import tpu as pltpu
from jax.sharding import PartitionSpec as P

spread = 0.5
dead_exponent = -32768.0
vmem_bytes = 32 * 1024 * 1024


def pieces(value):
    high = value.astype(jnp.bfloat16).astype(jnp.float32)
    rest = value - high
    mid = rest.astype(jnp.bfloat16).astype(jnp.float32)
    return high, mid, (rest - mid).astype(jnp.bfloat16).astype(jnp.float32)


def stacked_rows(rows, width):
    row_ids = lax.broadcasted_iota(jnp.int32, (8, width), 0)
    block = jnp.zeros((8, width), jnp.float32)
    for place, row in enumerate(rows):
        block = jnp.where(row_ids == place, row, block)
    return block


def first_cell(row_count):
    group = lax.axis_index("cells") * lax.axis_size("feat") + lax.axis_index("feat")
    return group * row_count


def pack_kernel(offset, totals_ref, feats_ref, weights_ref, lists_ref, out_ref):
    feats = feats_ref[0]
    feat_count, row_count = feats.shape
    _, source_count, list_len = lists_ref.shape
    wide = feats.astype(jnp.float32)
    squares = jnp.sum(wide * wide, axis=0, keepdims=True)
    positions = first_cell(row_count) + lax.broadcasted_iota(jnp.int32, (1, row_count), 1)
    weights = weights_ref[...]
    used = (positions < totals_ref[lax.axis_index("tm")]) & (weights > 1e-37)
    share = offset - squares / (spread * feat_count) + jnp.log(jnp.where(used, weights, 1.0))
    high, mid, low = pieces(jnp.where(used, share, dead_exponent))
    lists = lists_ref[0].astype(jnp.float32)
    listed = jnp.concatenate(
        [lists[place : place + 1] for place in range(source_count)]
        + [jnp.full((1, row_count - source_count * list_len), -1.0, jnp.float32)],
        axis=1,
    )
    tail = stacked_rows([high, mid, low, 1.0, 1.0, 1.0, listed], row_count)
    out_ref[...] = jnp.concatenate([feats, tail.astype(jnp.bfloat16)], axis=0)


def own_kernel(feats_ref, out_ref):
    feats = feats_ref[0].astype(jnp.float32)
    feat_count, row_count = feats.shape
    squares = jnp.sum(feats * feats, axis=0, keepdims=True)
    high, mid, low = pieces(-squares / (spread * feat_count))
    tail = stacked_rows([1.0, 1.0, 1.0, high, mid, low], row_count)
    scaled = feats * (2.0 / (spread * feat_count))
    fill = jnp.zeros((out_ref.shape[1] - feat_count - 8, row_count), jnp.float32)
    columns = jnp.concatenate([scaled, tail, fill], axis=0)
    out_ref[...] = columns.T.astype(jnp.bfloat16)


def updated(alive, potentials, message):
    _, row_count = potentials.shape
    positions = first_cell(row_count) + lax.broadcasted_iota(jnp.int32, (1, row_count), 1)
    live = positions < alive
    prior = jnp.where(live, potentials * message, 0.0)
    cell_total = row_count * lax.axis_size("cells") * lax.axis_size("feat")
    wanted = cell_total / alive.astype(jnp.float32)
    scales = potentials * jnp.sqrt(wanted / jnp.where(live, prior, 1.0))
    return jnp.where(live, scales, 0.0), prior


def sum_kernel(groups, forward, closing, totals_ref, own_ref, lists_ref, weights_ref, *refs):
    shards, (scales_ref, prior_ref, acc_ref) = refs[:-3], refs[-3:]
    depth, row_count = shards[0].shape
    _, source_count, list_len = lists_ref.shape
    block_len = row_count // source_count
    time_here = lax.axis_index("tm")
    by_sender = time_here > 0 if forward is None else jnp.bool_(forward)
    here = lax.axis_index("cells") * lax.axis_size("feat") + lax.axis_index("feat")
    lists = lists_ref[0].astype(jnp.float32)
    lane = lax.broadcasted_iota(jnp.int32, (1, 128), 1)
    lister = lane // list_len
    own_lists = jnp.concatenate(
        [lists[place : place + 1] for place in range(source_count)]
        + [jnp.full((1, 128 - source_count * list_len), -1.0, jnp.float32)],
        axis=1,
    )
    acc_ref[...] = jnp.zeros_like(acc_ref)
    for shard_ref, group_of in zip(shards, groups):
        there = group_of()
        sent_lists = shard_ref[depth - 8 :, :128].astype(jnp.float32)[6:7]
        values = jnp.where(by_sender, sent_lists, own_lists)
        wanted = jnp.where(by_sender, here, there) * source_count
        mask = jnp.zeros((1, 128), jnp.int32)
        for place in range(source_count):
            bit = jnp.where(by_sender, place * source_count + lister, lister * source_count + place)
            hit = values == (wanted + place).astype(jnp.float32)
            mask = mask + jnp.where(hit, jnp.left_shift(1, bit), 0)
        pairs = jnp.sum(mask)

        def pair(index, carry, shard_ref=shard_ref, pairs=pairs):
            @pl.when(jnp.bitwise_and(jnp.right_shift(pairs, index), 1) == 1)
            def _():
                row = pl.multiple_of(index // source_count * block_len, block_len)
                column = pl.multiple_of(index % source_count * block_len, block_len)
                exponents = jnp.dot(
                    own_ref[pl.ds(row, block_len), :depth],
                    shard_ref[:, pl.ds(column, block_len)],
                    preferred_element_type=jnp.float32,
                )
                values = jnp.exp(exponents)
                total = values[:, :128]
                for start in range(128, block_len, 128):
                    total = total + values[:, start : start + 128]
                acc_ref[pl.ds(row, block_len), :] += total

            return carry

        lax.fori_loop(0, source_count * source_count, pair, 0)
    message = jnp.sum(acc_ref[...].T, axis=0, keepdims=True)
    if not closing:
        scales_ref[...] = message
        prior_ref[...] = message
        return
    scales_ref[...], prior_ref[...] = updated(totals_ref[time_here], weights_ref[...], message)


def call(kernel, out_shapes, operands, scratch=(), scalars=1):
    specs = [pl.BlockSpec(memory_space=pltpu.SMEM)] * scalars
    specs += [pl.BlockSpec(memory_space=pltpu.VMEM)] * (len(operands) - scalars)
    return pl.pallas_call(
        kernel,
        out_shape=out_shapes,
        in_specs=specs,
        out_specs=jax.tree.map(lambda _: pl.BlockSpec(memory_space=pltpu.VMEM), out_shapes),
        scratch_shapes=scratch,
        compiler_params=pltpu.CompilerParams(vmem_limit_bytes=vmem_bytes),
    )(*operands)


def collected(payload, step):
    times, count, cores = lax.axis_size("tm"), lax.axis_size("cells"), lax.axis_size("feat")
    xor = count & (count - 1) == 0

    def partner(place, distance):
        return place ^ distance if xor else (place + distance) % count

    arrived, groups = [], []
    for distance in reversed(range(count)):
        route = [
            ((time * count + place) * cores + core, ((time + move) * count + partner(place, distance)) * cores + core)
            for time in range(times)
            for move in ((1, -1) if step is None else (step,))
            if 0 <= time + move < times
            for place in range(count)
            for core in range(cores)
        ]
        shard = lax.ppermute(payload, ("tm", "cells", "feat"), route)
        for swap in range(cores):
            if swap:
                twin = [(core, (core + swap) % cores) for core in range(cores)]
                shard_here = lax.ppermute(shard, "feat", twin)
            else:
                shard_here = shard

            def group_of(distance=distance, swap=swap):
                place, core = lax.axis_index("cells"), lax.axis_index("feat")
                if xor:
                    source = jnp.bitwise_xor(place, distance)
                else:
                    source = lax.rem(place + count - distance, count)
                return source * cores + lax.rem(core + cores - swap, cores)

            arrived.append(shard_here)
            groups.append(group_of)
    return arrived, groups


def on_device(principal_coordinates, present_potentials, destination_tiles, living_totals):
    _, feat_count, row_count = principal_coordinates.shape
    _, source_count, list_len = destination_tiles.shape
    block_len = row_count // source_count
    offset = 2.0 / spread - math.log(2 * list_len * block_len)
    row = jax.ShapeDtypeStruct((1, row_count), jnp.float32)
    payload_shape = jax.ShapeDtypeStruct((feat_count + 8, row_count), jnp.bfloat16)
    own_shape = jax.ShapeDtypeStruct((row_count, 128), jnp.bfloat16)
    scratch = [pltpu.VMEM((row_count, 128), jnp.float32)]
    times = lax.axis_size("tm")

    def packed(weights):
        operands = (living_totals, principal_coordinates, weights, destination_tiles)
        return call(functools.partial(pack_kernel, offset), payload_shape, operands)

    def summed(payload, step, weights):
        arrived, groups = collected(payload, step)
        forward = None if step is None else step > 0
        operands = (living_totals, own_cells, destination_tiles, weights, *arrived)
        kernel = functools.partial(sum_kernel, groups, forward, step is None)
        return call(kernel, (row, row), operands, scratch)

    own_cells = call(own_kernel, own_shape, (principal_coordinates,), scalars=0)
    if times == 2:
        return tuple(summed(packed(present_potentials), None, present_potentials))

    time_here = lax.axis_index("tm")

    def advance(_, state):
        forward, backward = state
        pushed, _ = summed(packed(present_potentials * forward), 1, present_potentials)
        pulled, _ = summed(packed(present_potentials * backward), -1, present_potentials)
        return (
            jnp.where(time_here == 0, 1.0, pushed),
            jnp.where(time_here == times - 1, 1.0, pulled),
        )

    unit = jnp.ones((1, row_count), jnp.float32)
    forward, backward = lax.fori_loop(0, times - 1, advance, (unit, unit))
    return updated(living_totals[time_here], present_potentials, forward * backward)


def solution(mesh):
    in_specs = (
        P(("runs", "tm"), None, ("cells", "feat")),
        P(("runs", "tm"), ("cells", "feat")),
        P(("runs", "tm"), ("cells", "feat"), None),
        P("runs"),
    )
    out_specs = (P(("runs", "tm"), ("cells", "feat")), P(("runs", "tm"), ("cells", "feat")))
    return jax.shard_map(
        on_device, mesh=mesh, in_specs=in_specs, out_specs=out_specs, check_vma=False
    )
```

time: 119 us -> 35 us (0.29)
  blocking collectives: 41.5 us -> 0 us
  matrix products: 21.3 us -> 0 us
  between operations: 15.5 us -> 0.67 us
  Pallas kernels: 0 us -> 10.6 us
  waiting for transfers between devices: 20.5 us -> 11.4 us
  other arithmetic: 6.87 us -> 0 us
  local copies, waits for them, and re-layouts: 6.26 us -> 2.92 us
  starting transfers between devices: 7.16 us -> 9.08 us
    unnamed x1 -> x0, blocking collectives: 27.5 us -> none
    dot_general x5 -> x0, matrix products: 21.3 us -> none  [the longest x1 10.3 us: advance(): jnp.einsum('snij,si->snj', kernel_tiles, running_belief, precision=highest)]
    all_gather x1 -> x0, blocking collectives: 14 us -> none  [advance(): lax.all_gather(neighbours[2, 1], ('cells', 'feat'), axis=0, tiled=True)]
    all_gather x1 -> x0, waiting for transfers between devices: 13.8 us -> none  [on_device(): lax.all_gather(later_shard, ('cells', 'feat'), axis=1, tiled=True)]
    pallas_call x0 -> x3, Pallas kernels: none -> 10.6 us  [call(): pl.pallas_call(kernel, out_shape=out_shapes, in_specs=specs, out_specs=ja...]
    ppermute x3 -> x8, waiting for transfers between devices: 6.67 us -> 11.4 us  [the longest x4 10.5 us: collected(): shard = lax.ppermute(payload, ('tm', 'cells', 'feat'), route)]
    reduce_sum x3 -> x0, other arithmetic: 2.47 us -> none  [the longest x1 1.27 us: on_device(): count_here = jnp.sum(jnp.where(time_ids == time_here, living_totals, 0))]
    ppermute x3 -> x8, starting transfers between devices: 7.13 us -> 9.08 us  [the longest x4 8.06 us: collected(): shard = lax.ppermute(payload, ('tm', 'cells', 'feat'), route)]
  transfers between devices with their start and end apart: 4 -> 8, of which waited for: 2 -> 4; matrix products, arithmetic and copies ran while one was open for 16% -> 0% of each run, Pallas kernels for 0% -> 0%
where the time goes in v1:
time: 35 us; the launch traced here: 34.6 us
  waiting for transfers between devices  11.4 us (33%)
  Pallas kernels  10.6 us (30%)
  starting transfers between devices  9.08 us (26%)
  local copies, waits for them, and re-layouts  2.92 us (8%)
  between operations  0.67 us (2%)
    pallas_call x3, Pallas kernels, call(): pl.pallas_call(kernel, out_shape=out_shapes, in_specs=specs, out_specs=ja...  10.6 us
    ppermute x4, waiting for transfers between devices, collected(): shard = lax.ppermute(payload, ('tm', 'cells', 'feat'), route)  10.5 us
    ppermute x4, starting transfers between devices, collected(): shard = lax.ppermute(payload, ('tm', 'cells', 'feat'), route)  8.06 us
    unnamed x8, local copies, waits for them, and re-layouts  2.92 us
    ppermute x4, starting transfers between devices, collected(): shard_here = lax.ppermute(shard, 'feat', twin)  1.02 us
    ppermute x4, waiting for transfers between devices, collected(): shard_here = lax.ppermute(shard, 'feat', twin)  0.9 us
  transfers between devices with their start and end apart: 8, of which 4 were waited for; matrix products, arithmetic and copies ran while one was open for 0% of the time, Pallas kernels for 0%

profile of v1, /device:TPU:0, one launch (start us, length us, event | category | flops | bytes accessed | tf_op | source)
XLA Modules:
  0.0 34.6 jit_solution(13649816753172845592)
XLA Ops:
  0.6 0.0 copy-start
  0.6 0.9 %copy-done = bf16[1,64,1024]{2,1,0:T(8,128)(2,1)S(1)} copy-done((bf16[1,64,1024]{2,1,0:T(8,128)(2,1)S(1)}, bf16[1,64,1024]{2,1,0:T(8,128)(2,1)}, u32[]{:S(2)}) %copy-start) | copy-done | bytes 131096
  1.5 0.0 copy-start.1
  1.5 0.7 %copy-done.1 = f32[1,1024]{1,0:T(1,128)S(1)} copy-done((f32[1,1024]{1,0:T(1,128)S(1)}, f32[1,1024]{1,0:T(1,128)}, u32[]{:S(2)}) %copy-start.1) | copy-done | bytes 4120
  2.2 0.0 copy-start.2
  2.2 0.7 %copy-done.2 = s32[1,4,8]{2,1,0:T(4,128)S(1)} copy-done((s32[1,4,8]{2,1,0:T(4,128)S(1)}, s32[1,4,8]{2,1,0:T(4,128)}, u32[]{:S(2)}) %copy-start.2) | copy-done | bytes 152
  2.9 0.0 copy-start.3
  2.9 0.7 %copy-done.3 = s32[2]{0:T(128)S(1)} copy-done((s32[2]{0:T(128)S(1)}, s32[2]{0:T(128)}, u32[]{:S(2)}) %copy-start.3) | copy-done | bytes 32
  3.6 0.6 %shard_map.60 = bf16[72,1024]{1,0:T(8,128)(2,1)S(1)} custom-call(s32[2]{0:T(128)S(1)} %copy-done.3, bf16[1,64,1024]{2,1,0:T(8,128)(2,1)S(1)} %copy-done, f32[1,1024]{1,0:T(1,128)S(1)} %copy-done.1, s32[1,4,8]{2,1,0:T(4,128)S(1)} %copy-done.2), custom_call_target="tpu_custom_call" | custom-call | tf_op jit(solution)/shard_map/pallas_call | solution.py:139
  4.2 3.0 %collective-permute-start.6 = (bf16[72,1024]{1,0:T(8,128)(2,1)S(1)}, bf16[72,1024]{1,0:T(8,128)(2,1)S(1)}, u32[]{:S(2)}, u32[]{:S(2)}) collective-permute-start(bf16[72,1024]{1,0:T(8,128)(2,1)S(1)} %shard_map.60), channel_id=1, source_target_pairs={{0,8},{1,9},{2,10},{3,11},{4,12},{5,13},{6,14},{7,15},{8,0},{9,1},... | collective-permute-start | bytes 442376 | tf_op jit(solution)/shard_map/ppermute | solution.py:166
  7.2 1.5 %collective-permute-start.4 = (bf16[72,1024]{1,0:T(8,128)(2,1)S(1)}, bf16[72,1024]{1,0:T(8,128)(2,1)S(1)}, u32[]{:S(2)}, u32[]{:S(2)}) collective-permute-start(bf16[72,1024]{1,0:T(8,128)(2,1)S(1)} %shard_map.60), channel_id=1, source_target_pairs={{0,10},{1,11},{2,8},{3,9},{4,14},{5,15},{6,12},{7,13},{8,2},{9,3},... | collective-permute-start | bytes 442376 | tf_op jit(solution)/shard_map/ppermute | solution.py:166
  8.7 3.5 %collective-permute-start.2 = (bf16[72,1024]{1,0:T(8,128)(2,1)S(1)}, bf16[72,1024]{1,0:T(8,128)(2,1)S(1)}, u32[]{:S(2)}, u32[]{:S(2)}) collective-permute-start(bf16[72,1024]{1,0:T(8,128)(2,1)S(1)} %shard_map.60), channel_id=1, source_target_pairs={{0,12},{1,13},{2,14},{3,15},{4,8},{5,9},{6,10},{7,11},{8,4},{9,5},... | collective-permute-start | bytes 442376 | tf_op jit(solution)/shard_map/ppermute | solution.py:166
  12.2 0.0 collective-permute-start
  12.2 4.3 %collective-permute-done.6.refs_6_ = bf16[72,1024]{1,0:T(8,128)(2,1)S(1)} collective-permute-done((bf16[72,1024]{1,0:T(8,128)(2,1)S(1)}, bf16[72,1024]{1,0:T(8,128)(2,1)S(1)}, u32[]{:S(2)}, u32[]{:S(2)}) %collective-permute-start.6) | collective-permute-done | bytes 147488 | tf_op jit(solution)/shard_map/ppermute | solution.py:166
  16.5 0.0 collective-permute-start.7
  16.5 0.0 collective-permute-done.4.refs_4_
  16.5 0.5 %collective-permute-start.5 = (bf16[72,1024]{1,0:T(8,128)(2,1)S(1)}, bf16[72,1024]{1,0:T(8,128)(2,1)S(1)}, u32[]{:S(2)}, u32[]{:S(2)}) collective-permute-start(bf16[72,1024]{1,0:T(8,128)(2,1)S(1)} %collective-permute-done.4.refs_4_), channel_id=1, source_target_pairs={{0,1},{1,0},{2,3},{3,2},{4,5},{5,4},{6,7},{7,6},{8,9},{9,8},{10,11... | collective-permute-start | bytes 442376 | tf_op jit(solution)/shard_map/ppermute | solution.py:170
  17.0 6.3 %collective-permute-done.2.refs_2_ = bf16[72,1024]{1,0:T(8,128)(2,1)S(1)} collective-permute-done((bf16[72,1024]{1,0:T(8,128)(2,1)S(1)}, bf16[72,1024]{1,0:T(8,128)(2,1)S(1)}, u32[]{:S(2)}, u32[]{:S(2)}) %collective-permute-start.2) | collective-permute-done | bytes 147488 | tf_op jit(solution)/shard_map/ppermute | solution.py:166
  23.3 0.0 collective-permute-start.3
  23.3 0.0 collective-permute-done.refs_0_
  23.3 0.5 %collective-permute-start.1 = (bf16[72,1024]{1,0:T(8,128)(2,1)S(1)}, bf16[72,1024]{1,0:T(8,128)(2,1)S(1)}, u32[]{:S(2)}, u32[]{:S(2)}) collective-permute-start(bf16[72,1024]{1,0:T(8,128)(2,1)S(1)} %collective-permute-done.refs_0_), channel_id=1, source_target_pairs={{0,1},{1,0},{2,3},{3,2},{4,5},{5,4},{6,7},{7,6},{8,9},{9,8},{10,11... | collective-permute-start | bytes 442376 | tf_op jit(solution)/shard_map/ppermute | solution.py:170
  23.8 0.1 shard_map.59.own_ref
  23.9 0.0 collective-permute-done.7.refs_7_
  23.9 0.0 collective-permute-done.5.refs_5_
  24.0 0.7 %collective-permute-done.3.refs_3_ = bf16[72,1024]{1,0:T(8,128)(2,1)S(1)} collective-permute-done((bf16[72,1024]{1,0:T(8,128)(2,1)S(1)}, bf16[72,1024]{1,0:T(8,128)(2,1)S(1)}, u32[]{:S(2)}, u32[]{:S(2)}) %collective-permute-start.3) | collective-permute-done | bytes 147488 | tf_op jit(solution)/shard_map/ppermute | solution.py:170
  24.6 0.2 collective-permute-done.1.refs_1_
  24.9 9.8 %shard_map.61 = (f32[1,1024]{1,0:T(1,128)}, f32[1,1024]{1,0:T(1,128)}) custom-call(s32[2]{0:T(128)S(1)} %copy-done.3, bf16[1024,128]{1,0:T(8,128)(2,1)S(1)} %shard_map.59.own_ref, s32[1,4,8]{2,1,0:T(4,128)S(1)} %copy-done.2, f32[1,1024]{1,0:T(1,128)S(1)} %copy-done.1, bf16[72,1024]{1,0:T(8,128)(2,1)S(1)} %collective-permute-done.refs_0_, ...), custom_call_target="tpu_custom_call" | custom-call | tf_op jit(solution)/shard_map/pallas_call | solution.py:139
Async XLA Ops:
  0.6 0.9 %copy-start = (bf16[1,64,1024]{2,1,0:T(8,128)(2,1)S(1)}, bf16[1,64,1024]{2,1,0:T(8,128)(2,1)}, u32[]{:S(2)}) copy-start(bf16[1,64,1024]{2,1,0:T(8,128)(2,1)} %feats_ref.3) | copy-start | bytes 393220
  1.5 0.7 %copy-start.1 = (f32[1,1024]{1,0:T(1,128)S(1)}, f32[1,1024]{1,0:T(1,128)}, u32[]{:S(2)}) copy-start(f32[1,1024]{1,0:T(1,128)} %weights_ref.3) | copy-start | bytes 12292
  2.2 0.7 %copy-start.2 = (s32[1,4,8]{2,1,0:T(4,128)S(1)}, s32[1,4,8]{2,1,0:T(4,128)}, u32[]{:S(2)}) copy-start(s32[1,4,8]{2,1,0:T(4,128)} %lists_ref.3) | copy-start | bytes 388
  2.9 0.7 %copy-start.3 = (s32[2]{0:T(128)S(1)}, s32[2]{0:T(128)}, u32[]{:S(2)}) copy-start(s32[2]{0:T(128)} %totals_ref.3) | copy-start | bytes 28
  4.2 12.3 %collective-permute-start.6 = (bf16[72,1024]{1,0:T(8,128)(2,1)S(1)}, bf16[72,1024]{1,0:T(8,128)(2,1)S(1)}, u32[]{:S(2)}, u32[]{:S(2)}) collective-permute-start(bf16[72,1024]{1,0:T(8,128)(2,1)S(1)} %shard_map.60), channel_id=1, source_target_pairs={{0,8},{1,9},{2,10},{3,11},{4,12},{5,13},{6,14},{7,15},{8,0},{9,1},... | collective-permute-start | bytes 442376 | tf_op jit(solution)/shard_map/ppermute | solution.py:166
  7.2 9.3 %collective-permute-start.4 = (bf16[72,1024]{1,0:T(8,128)(2,1)S(1)}, bf16[72,1024]{1,0:T(8,128)(2,1)S(1)}, u32[]{:S(2)}, u32[]{:S(2)}) collective-permute-start(bf16[72,1024]{1,0:T(8,128)(2,1)S(1)} %shard_map.60), channel_id=1, source_target_pairs={{0,10},{1,11},{2,8},{3,9},{4,14},{5,15},{6,12},{7,13},{8,2},{9,3},... | collective-permute-start | bytes 442376 | tf_op jit(solution)/shard_map/ppermute | solution.py:166
  8.7 14.5 %collective-permute-start.2 = (bf16[72,1024]{1,0:T(8,128)(2,1)S(1)}, bf16[72,1024]{1,0:T(8,128)(2,1)S(1)}, u32[]{:S(2)}, u32[]{:S(2)}) collective-permute-start(bf16[72,1024]{1,0:T(8,128)(2,1)S(1)} %shard_map.60), channel_id=1, source_target_pairs={{0,12},{1,13},{2,14},{3,15},{4,8},{5,9},{6,10},{7,11},{8,4},{9,5},... | collective-permute-start | bytes 442376 | tf_op jit(solution)/shard_map/ppermute | solution.py:166
  12.2 11.0 %collective-permute-start = (bf16[72,1024]{1,0:T(8,128)(2,1)S(1)}, bf16[72,1024]{1,0:T(8,128)(2,1)S(1)}, u32[]{:S(2)}, u32[]{:S(2)}) collective-permute-start(bf16[72,1024]{1,0:T(8,128)(2,1)S(1)} %shard_map.60), channel_id=1, source_target_pairs={{0,14},{1,15},{2,12},{3,13},{4,10},{5,11},{6,8},{7,9},{8,6},{9,7},... | collective-permute-start | bytes 442376 | tf_op jit(solution)/shard_map/ppermute | solution.py:166
  16.5 7.4 %collective-permute-start.7 = (bf16[72,1024]{1,0:T(8,128)(2,1)S(1)}, bf16[72,1024]{1,0:T(8,128)(2,1)S(1)}, u32[]{:S(2)}, u32[]{:S(2)}) collective-permute-start(bf16[72,1024]{1,0:T(8,128)(2,1)S(1)} %collective-permute-done.6.refs_6_), channel_id=1, source_target_pairs={{0,1},{1,0},{2,3},{3,2},{4,5},{5,4},{6,7},{7,6},{8,9},{9,8},{10,11... | collective-permute-start | bytes 442376 | tf_op jit(solution)/shard_map/ppermute | solution.py:170
  16.5 7.4 %collective-permute-start.5 = (bf16[72,1024]{1,0:T(8,128)(2,1)S(1)}, bf16[72,1024]{1,0:T(8,128)(2,1)S(1)}, u32[]{:S(2)}, u32[]{:S(2)}) collective-permute-start(bf16[72,1024]{1,0:T(8,128)(2,1)S(1)} %collective-permute-done.4.refs_4_), channel_id=1, source_target_pairs={{0,1},{1,0},{2,3},{3,2},{4,5},{5,4},{6,7},{7,6},{8,9},{9,8},{10,11... | collective-permute-start | bytes 442376 | tf_op jit(solution)/shard_map/ppermute | solution.py:170
  23.3 1.4 %collective-permute-start.3 = (bf16[72,1024]{1,0:T(8,128)(2,1)S(1)}, bf16[72,1024]{1,0:T(8,128)(2,1)S(1)}, u32[]{:S(2)}, u32[]{:S(2)}) collective-permute-start(bf16[72,1024]{1,0:T(8,128)(2,1)S(1)} %collective-permute-done.2.refs_2_), channel_id=1, source_target_pairs={{0,1},{1,0},{2,3},{3,2},{4,5},{5,4},{6,7},{7,6},{8,9},{9,8},{10,11... | collective-permute-start | bytes 442376 | tf_op jit(solution)/shard_map/ppermute | solution.py:170
  23.3 1.6 %collective-permute-start.1 = (bf16[72,1024]{1,0:T(8,128)(2,1)S(1)}, bf16[72,1024]{1,0:T(8,128)(2,1)S(1)}, u32[]{:S(2)}, u32[]{:S(2)}) collective-permute-start(bf16[72,1024]{1,0:T(8,128)(2,1)S(1)} %collective-permute-done.refs_0_), channel_id=1, source_target_pairs={{0,1},{1,0},{2,3},{3,2},{4,5},{5,4},{6,7},{7,6},{8,9},{9,8},{10,11... | collective-permute-start | bytes 442376 | tf_op jit(solution)/shard_map/ppermute | solution.py:170

commit v2 on v0

v2 whole, which is shorter than its diff:
```python
import functools
import math

import jax
import jax.numpy as jnp
from jax import lax
from jax.experimental import pallas as pl
from jax.experimental.pallas import tpu as pltpu
from jax.sharding import PartitionSpec as P

spread = 0.5
dead_exponent = -32768.0
vmem_bytes = 32 * 1024 * 1024
lanes = 128
extra_rows = 32
list_rows = 16
bf16 = jnp.bfloat16


def pieces(value):
    high = value.astype(bf16).astype(jnp.float32)
    rest = value - high
    mid = rest.astype(bf16).astype(jnp.float32)
    return high, mid, (rest - mid).astype(bf16).astype(jnp.float32)


def stacked_rows(rows, height, width):
    row_ids = lax.broadcasted_iota(jnp.int32, (height, width), 0)
    block = jnp.zeros((height, width), jnp.float32)
    for place, row in enumerate(rows):
        block = jnp.where(row_ids == place, row, block)
    return block


def lane_blocks(row):
    return jnp.concatenate(
        [row[:, start : start + lanes] for start in range(0, row.shape[1], lanes)], axis=0
    )


def here():
    return lax.axis_index("cells") * lax.axis_size("feat") + lax.axis_index("feat")


def listed_row(lists):
    source_count, list_len = lists.shape
    rows = [lists[place : place + 1] for place in range(source_count)]
    fill = jnp.full((1, lanes - source_count * list_len), -1.0, jnp.float32)
    return jnp.concatenate(rows + [fill], axis=1)


def fetch(sources, targets, sems):
    copies = [
        pltpu.make_async_copy(source, target, sems.at[place])
        for place, (source, target) in enumerate(zip(sources, targets))
    ]
    for copy in copies:
        copy.start()
    for copy in copies:
        copy.wait()


def pack_kernel(
    offset, totals_hbm, feats_hbm, weights_hbm, lists_hbm, out_ref, own_ref, facts_ref, *scratch
):
    totals_ref, feats_ref, weights_ref, lists_ref, sems = scratch
    fetch((feats_hbm, weights_hbm, lists_hbm, totals_hbm), (feats_ref, weights_ref, lists_ref, totals_ref), sems)
    _, feat_count, row_count = feats_ref.shape
    _, source_count, _ = lists_ref.shape
    slabs = row_count // lanes
    feats = feats_ref[0]
    wide = feats.astype(jnp.float32)
    squares = jnp.sum(wide * wide, axis=0, keepdims=True) / (spread * feat_count)
    positions = here() * row_count + lax.broadcasted_iota(jnp.int32, (1, row_count), 1)
    weights = weights_ref[...]
    alive = totals_ref[lax.axis_index("tm")]
    used = (positions < alive) & (weights > 1e-37)
    share = offset - squares + jnp.log(jnp.where(used, weights, 1.0))
    share = lane_blocks(jnp.where(used, share, dead_exponent))
    listed = listed_row(lists_ref[0].astype(jnp.float32))
    fill = jnp.zeros((extra_rows - 3 * slabs, lanes), jnp.float32)
    tail = jnp.concatenate([*pieces(share), fill + listed], axis=0)
    for slab in range(slabs):
        out_ref[slab * feat_count : (slab + 1) * feat_count, :] = feats[:, slab * lanes : (slab + 1) * lanes]
    out_ref[slabs * feat_count :, :] = tail.astype(bf16)
    block = lax.broadcasted_iota(jnp.int32, (1, row_count), 1) // (row_count // source_count)
    cores = lax.axis_size("feat")
    block = block + lax.axis_index("feat") * source_count
    member = [jnp.where(block == place, 1.0, 0.0) for place in range(cores * source_count)]
    own_tail = stacked_rows(
        [1.0, 1.0, 1.0, *pieces(-squares), *member], own_ref.shape[1] - feat_count, row_count
    )
    columns = jnp.concatenate([wide * (2.0 / (spread * feat_count)), own_tail], axis=0)
    own_ref[:row_count, :] = columns.T.astype(bf16)
    own_ref[row_count:, :] = jnp.broadcast_to(listed, (list_rows, lanes)).astype(bf16)
    facts_ref[...] = stacked_rows([weights, alive.astype(jnp.float32)], 8, row_count)


def updated(alive, potentials, message):
    _, row_count = potentials.shape
    positions = here() * row_count + lax.broadcasted_iota(jnp.int32, (1, row_count), 1)
    live = positions.astype(jnp.float32) < alive
    prior = jnp.where(live, potentials * message, 0.0)
    cell_total = row_count * lax.axis_size("cells") * lax.axis_size("feat")
    wanted = cell_total / alive
    scales = potentials * jnp.sqrt(wanted / jnp.where(live, prior, 1.0))
    return jnp.where(live, scales, 0.0), prior


def listed_pairs(values, first, by_sender, list_shape):
    source_count, list_len = list_shape
    lister = lax.broadcasted_iota(jnp.int32, (1, lanes), 1) // list_len
    found = jnp.zeros((1, lanes), jnp.int32)
    for place in range(source_count):
        bit = jnp.where(by_sender, place * source_count + lister, lister * source_count + place)
        hit = values == (first + place).astype(jnp.float32)
        found = found + jnp.where(hit, jnp.left_shift(1, bit), 0)
    return jnp.sum(found)


def add_shard(shard_ref, there, forward, list_shape, owners, totals):
    source_count, _ = list_shape
    cores = lax.axis_size("feat")
    row_count = owners[0][0].shape[0] - list_rows
    slabs = row_count // lanes
    feat_count = (shard_ref.shape[0] - extra_rows) // slabs
    depth = feat_count + 16
    by_sender = lax.axis_index("tm") > 0 if forward is None else jnp.bool_(forward)
    tail = shard_ref[slabs * feat_count :, :].astype(jnp.float32)
    pairs = []
    for own_ref, core in owners:
        lists = own_ref[row_count:, :].astype(jnp.float32)[:1]
        values = jnp.where(by_sender, tail[3 * slabs : 3 * slabs + 1], lists)
        group = lax.axis_index("cells") * cores + core
        first = jnp.where(by_sender, group, there) * source_count
        pairs.append((listed_pairs(values, first, by_sender, list_shape), core))
    cells = [own_ref[:row_count, :depth] for own_ref, _ in owners]
    cells = jnp.concatenate(cells, axis=0) if len(owners) > 1 else cells[0]
    for start in range(0, slabs, 2):
        other = start * source_count // slabs
        shut = []
        for core in range(cores):
            open_here = sum(jnp.where(owner == core, bits, 0) for bits, owner in pairs)
            for place in range(source_count):
                bit = jnp.bitwise_and(jnp.right_shift(open_here, place * source_count + other), 1)
                shut.append(jnp.where(bit == 1, 0.0, dead_exponent))
        columns = []
        for slab in (start, start + 1):
            share = [tail[piece * slabs + slab : piece * slabs + slab + 1] for piece in range(3)]
            rows = stacked_rows([*share, 1.0, 1.0, 1.0, *shut], 16, lanes).astype(bf16)
            feats = shard_ref[slab * feat_count : (slab + 1) * feat_count, :]
            columns.append(jnp.concatenate([feats, rows], axis=0))
        exponents = jnp.dot(
            cells, jnp.concatenate(columns, axis=1), preferred_element_type=jnp.float32
        )
        terms = jnp.exp(exponents)
        terms = terms[:, :lanes] + terms[:, lanes:]
        totals = [
            total + terms[place * row_count : (place + 1) * row_count]
            for place, total in enumerate(totals)
        ]
    return totals


def across(total):
    return jnp.sum(total.T, axis=0, keepdims=True)


def chip_kernel(groups, forward, list_shape, opening, closing, *refs):
    cores = lax.axis_size("feat")
    shards = refs[: len(groups)]
    own_refs = refs[len(groups) : len(groups) + cores]
    refs = refs[len(groups) + cores :]
    core = lax.axis_index("feat")
    owners = [
        (own_ref, lax.rem(core + cores - swap, cores)) for swap, own_ref in enumerate(own_refs)
    ]
    totals = [jnp.zeros((own_refs[0].shape[0] - list_rows, lanes), jnp.float32)] * cores
    if not opening:
        totals, refs = [total_ref[...] for total_ref in refs[:cores]], refs[cores:]
    for shard_ref, group_of in zip(shards, groups):
        totals = add_shard(shard_ref, group_of(), forward, list_shape, owners, totals)
    for out_ref, total in zip(refs, totals):
        out_ref[...] = across(total) if closing else total


def last_kernel(group_of, forward, list_shape, opening, partials, shard_ref, own_ref, *refs):
    total = jnp.zeros((own_ref.shape[0] - list_rows, lanes), jnp.float32)
    if not opening:
        total, refs = refs[0][...], refs[1:]
    owners = [(own_ref, lax.axis_index("feat"))]
    (total,) = add_shard(shard_ref, group_of(), forward, list_shape, owners, [total])
    if partials is None:
        refs[0][...] = total
        return
    message = across(total)
    for partial_ref in refs[:partials]:
        message = message + partial_ref[...]
    refs = refs[partials:]
    if forward is not None:
        refs[0][...] = message
        return
    facts_ref, scales_ref, prior_ref = refs
    scales_ref[...], prior_ref[...] = updated(facts_ref[1:2], facts_ref[0:1], message)


def call(kernel, name, out_shapes, operands, spaces=None, scratch=(), exps=0):
    spaces = spaces or [pltpu.VMEM] * len(operands)
    return pl.pallas_call(
        kernel,
        name=name,
        out_shape=out_shapes,
        in_specs=[pl.BlockSpec(memory_space=space) for space in spaces],
        out_specs=jax.tree.map(lambda _: pl.BlockSpec(memory_space=pltpu.VMEM), out_shapes),
        scratch_shapes=scratch,
        compiler_params=pltpu.CompilerParams(vmem_limit_bytes=vmem_bytes),
        cost_estimate=pl.CostEstimate(flops=160 * exps, bytes_accessed=2**17, transcendentals=exps),
    )(*operands)


def exchange(array, route):
    (moves, shift) = route
    times, count, cores = lax.axis_size("tm"), lax.axis_size("cells"), lax.axis_size("feat")
    pairs = [
        ((time * count + place) * cores + core, ((time + move) * count + shift(place)) * cores + core)
        for time in range(times)
        for move in moves
        if 0 <= time + move < times
        for place in range(count)
        for core in range(cores)
    ]
    return lax.ppermute(array, ("tm", "cells", "feat"), pairs)


def swapped(array, swap):
    cores = lax.axis_size("feat")
    return lax.ppermute(array, "feat", [(core, (core + swap) % cores) for core in range(cores)])


def collected(payload, step):
    count, cores = lax.axis_size("cells"), lax.axis_size("feat")
    moves = (1, -1) if step is None else (step,)
    xor = count & (count - 1) == 0 and count > 1

    def shifted(distance):
        return lambda place: place ^ distance if xor else (place + distance) % count

    def group_of(distance, swap):
        place, core = lax.axis_index("cells"), lax.axis_index("feat")
        source = jnp.bitwise_xor(place, distance) if xor else lax.rem(place + count - distance, count)
        return source * cores + lax.rem(core + cores - swap, cores)

    direct = [d for d in reversed(range(count)) if not xor or d % 2 == 0 or d == 1]
    direct = sorted(direct, key=lambda d: d < 2)
    shards = {d: exchange(payload, (moves, shifted(d))) for d in direct}
    order = sorted(direct, key=lambda d: d >= 2)
    for distance in range(count):
        if distance not in shards:
            shards[distance] = exchange(shards[distance - 1], ((0,), shifted(1)))
            order.append(distance)
    return [(shards[distance], functools.partial(group_of, distance)) for distance in order]


def on_device(principal_coordinates, present_potentials, destination_tiles, living_totals):
    _, feat_count, row_count = principal_coordinates.shape
    _, source_count, list_len = destination_tiles.shape
    block_len = row_count // source_count
    offset = 2.0 / spread - math.log(2 * list_len * block_len)
    times = lax.axis_size("tm")
    row = jax.ShapeDtypeStruct((1, row_count), jnp.float32)
    sums = jax.ShapeDtypeStruct((row_count, lanes), jnp.float32)
    payload_rows = feat_count * row_count // lanes + extra_rows
    smem, vmem = pltpu.SMEM, pltpu.VMEM

    scratch = [
        smem(living_totals.shape, jnp.int32),
        vmem(principal_coordinates.shape, bf16),
        vmem(present_potentials.shape, jnp.float32),
        vmem(destination_tiles.shape, jnp.int32),
        pltpu.SemaphoreType.DMA((4,)),
    ]

    def in_hbm(*arrays):
        return [pltpu.with_memory_space_constraint(array, pltpu.HBM) for array in arrays]

    def packed(weights):
        return call(
            functools.partial(pack_kernel, offset),
            "pack_cells",
            (
                jax.ShapeDtypeStruct((payload_rows, lanes), bf16),
                jax.ShapeDtypeStruct((row_count + list_rows, lanes), bf16),
                jax.ShapeDtypeStruct((8, row_count), jnp.float32),
            ),
            in_hbm(living_totals, principal_coordinates, weights, destination_tiles),
            [pltpu.HBM] * 4,
            scratch,
        )

    def summed(pack, step):
        payload, own, facts = pack
        cores = lax.axis_size("feat")
        list_shape = (source_count, list_len)
        forward = None if step is None else step > 0
        owns = [own] + [swapped(own, swap) for swap in range(1, cores)]
        *early, (last, last_group) = collected(payload, step)
        rows = []
        batches = [early[2:], early[:1], early[1:2]] if len(early) > 2 else [early]
        for place, batch in enumerate(batches):
            closing = place == len(batches) - 1
            rows = call(
                functools.partial(
                    chip_kernel,
                    [functools.partial(group_of, 0) for _, group_of in batch],
                    forward,
                    list_shape,
                    place == 0,
                    closing,
                ),
                "chip_sums",
                (row if closing else sums,) * cores,
                [*(shard for shard, _ in batch), *owns, *rows],
                exps=len(batch) * cores * row_count * row_count,
            )
        partials = [rows[0]] + [swapped(rows[swap], cores - swap) for swap in range(1, cores)]
        last, _ = lax.optimization_barrier((last, rows[0]))
        total = []
        for swap in range(cores):
            shard = swapped(last, swap) if swap else last
            closing = swap == cores - 1
            operands = [shard, own, *total]
            result = sums
            if closing:
                operands += partials
                result = row
                if step is None:
                    operands.append(facts)
                    result = (row, row)
            total = call(
                functools.partial(
                    last_kernel,
                    functools.partial(last_group, swap),
                    forward,
                    list_shape,
                    swap == 0,
                    len(partials) if closing else None,
                ),
                "last_sums",
                result,
                operands,
                exps=row_count * row_count,
            )
            if not closing:
                total = [total]
        return total

    if times == 2:
        return tuple(summed(packed(present_potentials), None))

    time_here = lax.axis_index("tm")

    def advance(_, state):
        forward, backward = state
        pushed = summed(packed(present_potentials * forward), 1)
        pulled = summed(packed(present_potentials * backward), -1)
        return (
            jnp.where(time_here == 0, 1.0, pushed),
            jnp.where(time_here == times - 1, 1.0, pulled),
        )

    unit = jnp.ones((1, row_count), jnp.float32)
    forward, backward = lax.fori_loop(0, times - 1, advance, (unit, unit))
    return updated(living_totals[time_here].astype(jnp.float32), present_potentials, forward * backward)


def solution(mesh):
    in_specs = (
        P(("runs", "tm"), None, ("cells", "feat")),
        P(("runs", "tm"), ("cells", "feat")),
        P(("runs", "tm"), ("cells", "feat"), None),
        P("runs"),
    )
    out_specs = (P(("runs", "tm"), ("cells", "feat")), P(("runs", "tm"), ("cells", "feat")))
    return jax.shard_map(
        on_device, mesh=mesh, in_specs=in_specs, out_specs=out_specs, check_vma=False
    )
```

time: 119 us -> 23.1 us (0.19)
  blocking collectives: 41.5 us -> 0 us
  matrix products: 21.3 us -> 0 us
  waiting for transfers between devices: 20.5 us -> 4.92 us
  between operations: 15.5 us -> 0.69 us
  Pallas kernels: 0 us -> 7.9 us
  other arithmetic: 6.87 us -> 0 us
  local copies, waits for them, and re-layouts: 6.26 us -> 0 us
  starting transfers between devices: 7.16 us -> 9.41 us
    unnamed x1 -> x0, blocking collectives: 27.5 us -> none
    dot_general x5 -> x0, matrix products: 21.3 us -> none  [the longest x1 10.3 us: advance(): jnp.einsum('snij,si->snj', kernel_tiles, running_belief, precision=highest)]
    all_gather x1 -> x0, blocking collectives: 14 us -> none  [advance(): lax.all_gather(neighbours[2, 1], ('cells', 'feat'), axis=0, tiled=True)]
    all_gather x1 -> x0, waiting for transfers between devices: 13.8 us -> none  [on_device(): lax.all_gather(later_shard, ('cells', 'feat'), axis=1, tiled=True)]
    pallas_call x0 -> x6, Pallas kernels: none -> 7.9 us  [call(): pl.pallas_call(kernel, name=name, out_shape=out_shapes, in_specs=[pl.Bloc...]
    reduce_sum x3 -> x0, other arithmetic: 2.47 us -> none  [the longest x1 1.27 us: on_device(): count_here = jnp.sum(jnp.where(time_ids == time_here, living_totals, 0))]
    unnamed x13 -> x0, local copies, waits for them, and re-layouts: 2.44 us -> none
    ppermute x3 -> x7, starting transfers between devices: 7.13 us -> 9.41 us  [the longest x4 8.32 us: exchange(): return lax.ppermute(array, ('tm', 'cells', 'feat'), pairs)]
  transfers between devices with their start and end apart: 4 -> 7, of which waited for: 2 -> 2; matrix products, arithmetic and copies ran while one was open for 16% -> 0% of each run, Pallas kernels for 0% -> 23%
where the time goes in v2:
time: 23.1 us; the launch traced here: 22.9 us
  starting transfers between devices  9.41 us (41%)
  Pallas kernels  7.9 us (34%)
  waiting for transfers between devices  4.92 us (21%)
  between operations  0.69 us (3%)
    ppermute x4, starting transfers between devices, exchange(): return lax.ppermute(array, ('tm', 'cells', 'feat'), pairs)  8.32 us
    pallas_call x6, Pallas kernels, call(): pl.pallas_call(kernel, name=name, out_shape=out_shapes, in_specs=[pl.Bloc...  7.9 us
    ppermute x4, waiting for transfers between devices, exchange(): return lax.ppermute(array, ('tm', 'cells', 'feat'), pairs)  4.91 us
    ppermute x3, starting transfers between devices, swapped(): lax.ppermute(array, 'feat', [(core, (core + swap) % cores) for core in ra...  1.09 us
  transfers between devices with their start and end apart: 7, of which 2 were waited for; matrix products, arithmetic and copies ran while one was open for 0% of the time, Pallas kernels for 23%

profile of v2, /device:TPU:0, one launch (start us, length us, event | category | flops | bytes accessed | tf_op | source)
XLA Modules:
  0.0 22.9 jit_solution(16367511779766044365)
XLA Ops:
  0.6 1.2 %pack_cells.1 = (bf16[544,128]{1,0:T(8,128)(2,1)S(1)}, bf16[1040,128]{1,0:T(8,128)(2,1)S(1)}, f32[8,1024]{1,0:T(8,128)S(1)}) custom-call(s32[2]{0:T(128)} %totals_hbm.1, bf16[1,64,1024]{2,1,0:T(8,128)(2,1)} %feats_hbm.1, f32[1,1024]{1,0:T(1,128)} %weights_hbm.1, s32[1,4,8]{2,1,0:T(4,128)} %lists_hbm.1), custom_call_target="tpu_custom_call" | custom-call | bytes 131072 | tf_op jit(solution)/shard_map/pack_cells/pallas_call | solution.py:209
  1.8 0.5 %collective-permute-start.3 = (bf16[1040,128]{1,0:T(8,128)(2,1)S(1)}, bf16[1040,128]{1,0:T(8,128)(2,1)S(1)}, u32[]{:S(2)}, u32[]{:S(2)}) collective-permute-start(bf16[1040,128]{1,0:T(8,128)(2,1)S(1)} %get-tuple-element.13.refs_1_.own_ref), channel_id=1, source_target_pairs={{0,1},{1,0},{2,3},{3,2},{4,5},{5,4},{6,7},{7,6},{8,9},{9,8},{10,11... | collective-permute-start | bytes 798728 | tf_op jit(solution)/shard_map/ppermute | solution.py:237
  2.3 4.6 %collective-permute-start = (bf16[544,128]{1,0:T(8,128)(2,1)S(1)}, bf16[544,128]{1,0:T(8,128)(2,1)S(1)}, u32[]{:S(2)}, u32[]{:S(2)}) collective-permute-start(bf16[544,128]{1,0:T(8,128)(2,1)S(1)} %get-tuple-element.12), channel_id=1, source_target_pairs={{0,12},{1,13},{2,14},{3,15},{4,8},{5,9},{6,10},{7,11},{8,4},{9,5},... | collective-permute-start | bytes 417800 | tf_op jit(solution)/shard_map/ppermute | solution.py:232
  6.9 1.5 %collective-permute-start.4 = (bf16[544,128]{1,0:T(8,128)(2,1)S(1)}, bf16[544,128]{1,0:T(8,128)(2,1)S(1)}, u32[]{:S(2)}, u32[]{:S(2)}) collective-permute-start(bf16[544,128]{1,0:T(8,128)(2,1)S(1)} %get-tuple-element.12), channel_id=1, source_target_pairs={{0,10},{1,11},{2,8},{3,9},{4,14},{5,15},{6,12},{7,13},{8,2},{9,3},... | collective-permute-start | bytes 417800 | tf_op jit(solution)/shard_map/ppermute | solution.py:232
  8.4 1.5 %collective-permute-start.2 = (bf16[544,128]{1,0:T(8,128)(2,1)S(1)}, bf16[544,128]{1,0:T(8,128)(2,1)S(1)}, u32[]{:S(2)}, u32[]{:S(2)}) collective-permute-start(bf16[544,128]{1,0:T(8,128)(2,1)S(1)} %get-tuple-element.12), channel_id=1, source_target_pairs={{0,8},{1,9},{2,10},{3,11},{4,12},{5,13},{6,14},{7,15},{8,0},{9,1},... | collective-permute-start | bytes 417800 | tf_op jit(solution)/shard_map/ppermute | solution.py:232
  9.9 4.3 %collective-permute-done.refs_0_ = bf16[544,128]{1,0:T(8,128)(2,1)S(1)} collective-permute-done((bf16[544,128]{1,0:T(8,128)(2,1)S(1)}, bf16[544,128]{1,0:T(8,128)(2,1)S(1)}, u32[]{:S(2)}, u32[]{:S(2)}) %collective-permute-start) | collective-permute-done | bytes 139296 | tf_op jit(solution)/shard_map/ppermute | solution.py:232
  14.2 0.7 %collective-permute-start.1 = (bf16[544,128]{1,0:T(8,128)(2,1)S(1)}, bf16[544,128]{1,0:T(8,128)(2,1)S(1)}, u32[]{:S(2)}, u32[]{:S(2)}) collective-permute-start(bf16[544,128]{1,0:T(8,128)(2,1)S(1)} %collective-permute-done.refs_0_), channel_id=1, source_target_pairs={{0,2},{1,3},{2,0},{3,1},{4,6},{5,7},{6,4},{7,5},{8,10},{9,11},{10,... | collective-permute-start | bytes 417800 | tf_op jit(solution)/shard_map/ppermute | solution.py:232
  14.9 0.0 collective-permute-done.3.refs_2_
  14.9 1.4 %chip_sums.3 = (f32[1024,128]{1,0:T(8,128)S(1)}, f32[1024,128]{1,0:T(8,128)S(1)}) custom-call(bf16[544,128]{1,0:T(8,128)(2,1)S(1)} %collective-permute-done.refs_0_, bf16[1040,128]{1,0:T(8,128)(2,1)S(1)} %get-tuple-element.13.refs_1_.own_ref, bf16[1040,128]{1,0:T(8,128)(2,1)S(1)} %collective-permute-done.3.refs_2_), custom_call_target="tpu_custom_call" | custom-call | flops 335544320 | bytes 131072 | tf_op jit(solution)/shard_map/chip_sums/pallas_call | solution.py:209
  16.3 0.0 collective-permute-done.4.refs_0_
  16.3 1.4 %chip_sums.4 = (f32[1024,128]{1,0:T(8,128)S(1)}, f32[1024,128]{1,0:T(8,128)S(1)}) custom-call(bf16[544,128]{1,0:T(8,128)(2,1)S(1)} %collective-permute-done.4.refs_0_, bf16[1040,128]{1,0:T(8,128)(2,1)S(1)} %get-tuple-element.13.refs_1_.own_ref, bf16[1040,128]{1,0:T(8,128)(2,1)S(1)} %collective-permute-done.3.refs_2_, ...), custom_call_target="tpu_custom_call" | custom-call | flops 335544320 | bytes 131072 | tf_op jit(solution)/shard_map/chip_sums/pallas_call | solution.py:209
  17.7 0.6 %collective-permute-done.2.refs_0_ = bf16[544,128]{1,0:T(8,128)(2,1)S(1)} collective-permute-done((bf16[544,128]{1,0:T(8,128)(2,1)S(1)}, bf16[544,128]{1,0:T(8,128)(2,1)S(1)}, u32[]{:S(2)}, u32[]{:S(2)}) %collective-permute-start.2) | collective-permute-done | bytes 139296 | tf_op jit(solution)/shard_map/ppermute | solution.py:232
  18.4 1.5 %chip_sums.5 = (f32[1,1024]{1,0:T(1,128)S(1)}, f32[1,1024]{1,0:T(1,128)S(1)}) custom-call(bf16[544,128]{1,0:T(8,128)(2,1)S(1)} %collective-permute-done.2.refs_0_, bf16[1040,128]{1,0:T(8,128)(2,1)S(1)} %get-tuple-element.13.refs_1_.own_ref, bf16[1040,128]{1,0:T(8,128)(2,1)S(1)} %collective-permute-done.3.refs_2_, f32[1024,128]{1,0:T(8,128)S(1)} %get-tuple-element.16.refs_3_, ...), custom_call_target="tpu_custom_call" | custom-call | flops 335544320 | bytes 131072 | tf_op jit(solution)/shard_map/chip_sums/pallas_call | solution.py:209
  19.9 0.0 collective-permute-done.1.shard_ref
  19.9 0.1 collective-permute-start.5
  20.0 0.5 %collective-permute-start.6 = (f32[1,1024]{1,0:T(1,128)S(1)}, f32[1,1024]{1,0:T(1,128)S(1)}, u32[]{:S(2)}, u32[]{:S(2)}) collective-permute-start(f32[1,1024]{1,0:T(1,128)S(1)} %get-tuple-element.20), channel_id=1, source_target_pairs={{0,1},{1,0},{2,3},{3,2},{4,5},{5,4},{6,7},{7,6},{8,9},{9,8},{10,11... | collective-permute-start | bytes 12296 | tf_op jit(solution)/shard_map/ppermute | solution.py:237
  20.5 0.8 %last_sums.2.refs_0_ = f32[1024,128]{1,0:T(8,128)S(1)} custom-call(bf16[544,128]{1,0:T(8,128)(2,1)S(1)} %collective-permute-done.1.shard_ref, bf16[1040,128]{1,0:T(8,128)(2,1)S(1)} %get-tuple-element.13.refs_1_.own_ref), custom_call_target="tpu_custom_call" | custom-call | flops 167772160 | bytes 131072 | tf_op jit(solution)/shard_map/last_sums/pallas_call | solution.py:209
  21.3 0.0 collective-permute-done.6.refs_2_
  21.3 0.0 collective-permute-done.5.shard_ref
  21.3 1.6 %last_sums.3 = (f32[1,1024]{1,0:T(1,128)}, f32[1,1024]{1,0:T(1,128)}) custom-call(bf16[544,128]{1,0:T(8,128)(2,1)S(1)} %collective-permute-done.5.shard_ref, bf16[1040,128]{1,0:T(8,128)(2,1)S(1)} %get-tuple-element.13.refs_1_.own_ref, f32[1024,128]{1,0:T(8,128)S(1)} %last_sums.2.refs_0_, f32[1,1024]{1,0:T(1,128)S(1)} %get-tuple-element.18.refs_1_, ...), custom_call_target="tpu_custom_call" | custom-call | flops 167772160 | bytes 131072 | tf_op jit(solution)/shard_map/last_sums/pallas_call | solution.py:209
Async XLA Ops:
  1.8 13.1 %collective-permute-start.3 = (bf16[1040,128]{1,0:T(8,128)(2,1)S(1)}, bf16[1040,128]{1,0:T(8,128)(2,1)S(1)}, u32[]{:S(2)}, u32[]{:S(2)}) collective-permute-start(bf16[1040,128]{1,0:T(8,128)(2,1)S(1)} %get-tuple-element.13.refs_1_.own_ref), channel_id=1, source_target_pairs={{0,1},{1,0},{2,3},{3,2},{4,5},{5,4},{6,7},{7,6},{8,9},{9,8},{10,11... | collective-permute-start | bytes 798728 | tf_op jit(solution)/shard_map/ppermute | solution.py:237
  2.3 11.9 %collective-permute-start = (bf16[544,128]{1,0:T(8,128)(2,1)S(1)}, bf16[544,128]{1,0:T(8,128)(2,1)S(1)}, u32[]{:S(2)}, u32[]{:S(2)}) collective-permute-start(bf16[544,128]{1,0:T(8,128)(2,1)S(1)} %get-tuple-element.12), channel_id=1, source_target_pairs={{0,12},{1,13},{2,14},{3,15},{4,8},{5,9},{6,10},{7,11},{8,4},{9,5},... | collective-permute-start | bytes 417800 | tf_op jit(solution)/shard_map/ppermute | solution.py:232
  6.9 9.4 %collective-permute-start.4 = (bf16[544,128]{1,0:T(8,128)(2,1)S(1)}, bf16[544,128]{1,0:T(8,128)(2,1)S(1)}, u32[]{:S(2)}, u32[]{:S(2)}) collective-permute-start(bf16[544,128]{1,0:T(8,128)(2,1)S(1)} %get-tuple-element.12), channel_id=1, source_target_pairs={{0,10},{1,11},{2,8},{3,9},{4,14},{5,15},{6,12},{7,13},{8,2},{9,3},... | collective-permute-start | bytes 417800 | tf_op jit(solution)/shard_map/ppermute | solution.py:232
  8.4 9.9 %collective-permute-start.2 = (bf16[544,128]{1,0:T(8,128)(2,1)S(1)}, bf16[544,128]{1,0:T(8,128)(2,1)S(1)}, u32[]{:S(2)}, u32[]{:S(2)}) collective-permute-start(bf16[544,128]{1,0:T(8,128)(2,1)S(1)} %get-tuple-element.12), channel_id=1, source_target_pairs={{0,8},{1,9},{2,10},{3,11},{4,12},{5,13},{6,14},{7,15},{8,0},{9,1},... | collective-permute-start | bytes 417800 | tf_op jit(solution)/shard_map/ppermute | solution.py:232
  14.2 5.7 %collective-permute-start.1 = (bf16[544,128]{1,0:T(8,128)(2,1)S(1)}, bf16[544,128]{1,0:T(8,128)(2,1)S(1)}, u32[]{:S(2)}, u32[]{:S(2)}) collective-permute-start(bf16[544,128]{1,0:T(8,128)(2,1)S(1)} %collective-permute-done.refs_0_), channel_id=1, source_target_pairs={{0,2},{1,3},{2,0},{3,1},{4,6},{5,7},{6,4},{7,5},{8,10},{9,11},{10,... | collective-permute-start | bytes 417800 | tf_op jit(solution)/shard_map/ppermute | solution.py:232
  19.9 1.4 %collective-permute-start.5 = (bf16[544,128]{1,0:T(8,128)(2,1)S(1)}, bf16[544,128]{1,0:T(8,128)(2,1)S(1)}, u32[]{:S(2)}, u32[]{:S(2)}) collective-permute-start(bf16[544,128]{1,0:T(8,128)(2,1)S(1)} %collective-permute-done.1.shard_ref), channel_id=1, source_target_pairs={{0,1},{1,0},{2,3},{3,2},{4,5},{5,4},{6,7},{7,6},{8,9},{9,8},{10,11... | collective-permute-start | bytes 417800 | tf_op jit(solution)/shard_map/ppermute | solution.py:237
  20.0 1.3 %collective-permute-start.6 = (f32[1,1024]{1,0:T(1,128)S(1)}, f32[1,1024]{1,0:T(1,128)S(1)}, u32[]{:S(2)}, u32[]{:S(2)}) collective-permute-start(f32[1,1024]{1,0:T(1,128)S(1)} %get-tuple-element.20), channel_id=1, source_target_pairs={{0,1},{1,0},{2,3},{3,2},{4,5},{5,4},{6,7},{7,6},{8,9},{9,8},{10,11... | collective-permute-start | bytes 12296 | tf_op jit(solution)/shard_map/ppermute | solution.py:237

commit v3 on v2

--- a/solution.py
+++ b/solution.py
@@ -61,7 +61,7 @@
 
 
 def pack_kernel(
-    offset, totals_hbm, feats_hbm, weights_hbm, lists_hbm, out_ref, own_ref, facts_ref, *scratch
+    offset, totals_hbm, feats_hbm, weights_hbm, lists_hbm, out_ref, facts_ref, *scratch
 ):
     totals_ref, feats_ref, weights_ref, lists_ref, sems = scratch
     fetch((feats_hbm, weights_hbm, lists_hbm, totals_hbm), (feats_ref, weights_ref, lists_ref, totals_ref), sems)
@@ -83,17 +83,28 @@
     for slab in range(slabs):
         out_ref[slab * feat_count : (slab + 1) * feat_count, :] = feats[:, slab * lanes : (slab + 1) * lanes]
     out_ref[slabs * feat_count :, :] = tail.astype(bf16)
+    facts_ref[...] = stacked_rows([weights, alive.astype(jnp.float32)], 8, row_count)
+
+
+def own_kernel(source_count, payload_ref, own_ref):
+    row_count = own_ref.shape[0] - list_rows
+    slabs = row_count // lanes
+    feat_count = (payload_ref.shape[0] - extra_rows) // slabs
+    feats = [payload_ref[slab * feat_count : (slab + 1) * feat_count, :] for slab in range(slabs)]
+    wide = jnp.concatenate(feats, axis=1).astype(jnp.float32)
+    squares = jnp.sum(wide * wide, axis=0, keepdims=True) / (spread * feat_count)
+    cores = lax.axis_size("feat")
     block = lax.broadcasted_iota(jnp.int32, (1, row_count), 1) // (row_count // source_count)
-    cores = lax.axis_size("feat")
     block = block + lax.axis_index("feat") * source_count
     member = [jnp.where(block == place, 1.0, 0.0) for place in range(cores * source_count)]
     own_tail = stacked_rows(
-        [1.0, 1.0, 1.0, *pieces(-squares), *member], own_ref.shape[1] - feat_count, row_count
+        [1.0, 1.0, 1.0, *pieces(-squares), 0.0, 0.0, *member], lanes - feat_count, row_count
     )
     columns = jnp.concatenate([wide * (2.0 / (spread * feat_count)), own_tail], axis=0)
     own_ref[:row_count, :] = columns.T.astype(bf16)
+    tail = payload_ref[slabs * feat_count :, :].astype(jnp.float32)
+    listed = tail[3 * slabs : 3 * slabs + 1]
     own_ref[row_count:, :] = jnp.broadcast_to(listed, (list_rows, lanes)).astype(bf16)
-    facts_ref[...] = stacked_rows([weights, alive.astype(jnp.float32)], 8, row_count)
 
 
 def updated(alive, potentials, message):
@@ -107,49 +118,44 @@
     return jnp.where(live, scales, 0.0), prior
 
 
-def listed_pairs(values, first, by_sender, list_shape):
+def closed_pairs(sent, lists, there, forward, list_shape):
     source_count, list_len = list_shape
-    lister = lax.broadcasted_iota(jnp.int32, (1, lanes), 1) // list_len
-    found = jnp.zeros((1, lanes), jnp.int32)
-    for place in range(source_count):
-        bit = jnp.where(by_sender, place * source_count + lister, lister * source_count + place)
-        hit = values == (first + place).astype(jnp.float32)
-        found = found + jnp.where(hit, jnp.left_shift(1, bit), 0)
-    return jnp.sum(found)
+    cores = lax.axis_size("feat")
+    by_sender = lax.axis_index("tm") > 0 if forward is None else jnp.bool_(forward)
+    shape = (source_count * 8, lanes)
+    row_ids = lax.broadcasted_iota(jnp.int32, shape, 0)
+    other, owner = row_ids // 8, row_ids % 8
+    core, block = owner // source_count, owner % source_count
+    lister = lax.broadcasted_iota(jnp.int32, shape, 1) // list_len
+    values = jnp.broadcast_to(sent, shape)
+    for place, own_lists in lists:
+        values = jnp.where((core == place) & jnp.logical_not(by_sender), own_lists, values)
+    group = lax.axis_index("cells") * cores + core
+    wanted = jnp.where(by_sender, group * source_count + block, there * source_count + other)
+    hit = (values == wanted.astype(jnp.float32)) & (lister == jnp.where(by_sender, other, block))
+    found = jnp.max(jnp.where(hit, 1.0, 0.0), axis=1, keepdims=True)
+    return jnp.broadcast_to(jnp.where(found > 0.0, 0.0, dead_exponent), shape)
 
 
 def add_shard(shard_ref, there, forward, list_shape, owners, totals):
     source_count, _ = list_shape
-    cores = lax.axis_size("feat")
     row_count = owners[0][0].shape[0] - list_rows
     slabs = row_count // lanes
     feat_count = (shard_ref.shape[0] - extra_rows) // slabs
     depth = feat_count + 16
-    by_sender = lax.axis_index("tm") > 0 if forward is None else jnp.bool_(forward)
     tail = shard_ref[slabs * feat_count :, :].astype(jnp.float32)
-    pairs = []
-    for own_ref, core in owners:
-        lists = own_ref[row_count:, :].astype(jnp.float32)[:1]
-        values = jnp.where(by_sender, tail[3 * slabs : 3 * slabs + 1], lists)
-        group = lax.axis_index("cells") * cores + core
-        first = jnp.where(by_sender, group, there) * source_count
-        pairs.append((listed_pairs(values, first, by_sender, list_shape), core))
+    lists = [(core, own_ref[row_count:, :].astype(jnp.float32)[:1]) for own_ref, core in owners]
+    closed = closed_pairs(tail[3 * slabs : 3 * slabs + 1], lists, there, forward, list_shape)
     cells = [own_ref[:row_count, :depth] for own_ref, _ in owners]
     cells = jnp.concatenate(cells, axis=0) if len(owners) > 1 else cells[0]
     for start in range(0, slabs, 2):
         other = start * source_count // slabs
-        shut = []
-        for core in range(cores):
-            open_here = sum(jnp.where(owner == core, bits, 0) for bits, owner in pairs)
-            for place in range(source_count):
-                bit = jnp.bitwise_and(jnp.right_shift(open_here, place * source_count + other), 1)
-                shut.append(jnp.where(bit == 1, 0.0, dead_exponent))
         columns = []
         for slab in (start, start + 1):
             share = [tail[piece * slabs + slab : piece * slabs + slab + 1] for piece in range(3)]
-            rows = stacked_rows([*share, 1.0, 1.0, 1.0, *shut], 16, lanes).astype(bf16)
+            rows = [stacked_rows([*share, 1.0, 1.0, 1.0], 8, lanes), closed[other * 8 : other * 8 + 8]]
             feats = shard_ref[slab * feat_count : (slab + 1) * feat_count, :]
-            columns.append(jnp.concatenate([feats, rows], axis=0))
+            columns.append(jnp.concatenate([feats, jnp.concatenate(rows, axis=0).astype(bf16)], axis=0))
         exponents = jnp.dot(
             cells, jnp.concatenate(columns, axis=1), preferred_element_type=jnp.float32
         )
@@ -166,30 +172,37 @@
     return jnp.sum(total.T, axis=0, keepdims=True)
 
 
-def chip_kernel(groups, forward, list_shape, opening, closing, *refs):
+def chip_kernel(groups, jobs, forward, list_shape, started, finished, *refs):
     cores = lax.axis_size("feat")
-    shards = refs[: len(groups)]
-    own_refs = refs[len(groups) : len(groups) + cores]
-    refs = refs[len(groups) + cores :]
+    owner_count = 1 + max(max(swaps) for _, swaps in jobs)
+    shards, refs = refs[: len(groups)], refs[len(groups) :]
+    own_refs, refs = refs[:owner_count], refs[owner_count:]
     core = lax.axis_index("feat")
     owners = [
         (own_ref, lax.rem(core + cores - swap, cores)) for swap, own_ref in enumerate(own_refs)
     ]
-    totals = [jnp.zeros((own_refs[0].shape[0] - list_rows, lanes), jnp.float32)] * cores
-    if not opening:
-        totals, refs = [total_ref[...] for total_ref in refs[:cores]], refs[cores:]
-    for shard_ref, group_of in zip(shards, groups):
-        totals = add_shard(shard_ref, group_of(), forward, list_shape, owners, totals)
-    for out_ref, total in zip(refs, totals):
-        out_ref[...] = across(total) if closing else total
-
-
-def last_kernel(group_of, forward, list_shape, opening, partials, shard_ref, own_ref, *refs):
-    total = jnp.zeros((own_ref.shape[0] - list_rows, lanes), jnp.float32)
-    if not opening:
-        total, refs = refs[0][...], refs[1:]
+    row_count = own_refs[0].shape[0] - list_rows
+    totals = [total_ref[...] for total_ref in refs[:started]]
+    totals += [jnp.zeros((row_count, lanes), jnp.float32)] * (owner_count - started)
+    refs = refs[started:]
+    for place, swaps in jobs:
+        added = add_shard(
+            shards[place],
+            groups[place](),
+            forward,
+            list_shape,
+            [owners[swap] for swap in swaps],
+            [totals[swap] for swap in swaps],
+        )
+        for swap, total in zip(swaps, added):
+            totals[swap] = total
+    for swap, (out_ref, total) in enumerate(zip(refs, totals)):
+        out_ref[...] = across(total) if finished and swap else total
+
+
+def last_kernel(group_of, forward, list_shape, partials, shard_ref, own_ref, total_ref, *refs):
     owners = [(own_ref, lax.axis_index("feat"))]
-    (total,) = add_shard(shard_ref, group_of(), forward, list_shape, owners, [total])
+    (total,) = add_shard(shard_ref, group_of(), forward, list_shape, owners, [total_ref[...]])
     if partials is None:
         refs[0][...] = total
         return
@@ -289,7 +302,6 @@
             "pack_cells",
             (
                 jax.ShapeDtypeStruct((payload_rows, lanes), bf16),
-                jax.ShapeDtypeStruct((row_count + list_rows, lanes), bf16),
                 jax.ShapeDtypeStruct((8, row_count), jnp.float32),
             ),
             in_hbm(living_totals, principal_coordinates, weights, destination_tiles),
@@ -298,37 +310,51 @@
         )
 
     def summed(pack, step):
-        payload, own, facts = pack
+        payload, facts = pack
+        own = call(
+            functools.partial(own_kernel, source_count),
+            "own_rows",
+            jax.ShapeDtypeStruct((row_count + list_rows, lanes), bf16),
+            (payload,),
+        )
         cores = lax.axis_size("feat")
         list_shape = (source_count, list_len)
         forward = None if step is None else step > 0
         owns = [own] + [swapped(own, swap) for swap in range(1, cores)]
         *early, (last, last_group) = collected(payload, step)
-        rows = []
-        batches = [early[2:], early[:1], early[1:2]] if len(early) > 2 else [early]
+        mine, everyone, others = (0,), tuple(range(cores)), tuple(range(1, cores))
+        if len(early) > 2:
+            first = [(shard, mine) for shard in early[2:]]
+            second = [(shard, others) for shard in early[2:]]
+            batches = [first, [(early[0], everyone), *second], [(early[1], everyone)]]
+        else:
+            batches = [[(shard, everyone) for shard in early]]
+        totals = []
         for place, batch in enumerate(batches):
-            closing = place == len(batches) - 1
-            rows = call(
+            finished = place == len(batches) - 1
+            owner_count = 1 + max(max(swaps) for _, swaps in batch)
+            totals = call(
                 functools.partial(
                     chip_kernel,
-                    [functools.partial(group_of, 0) for _, group_of in batch],
+                    [functools.partial(group_of, 0) for (_, group_of), _ in batch],
+                    [(job, swaps) for job, (_, swaps) in enumerate(batch)],
                     forward,
                     list_shape,
-                    place == 0,
-                    closing,
+                    len(totals),
+                    finished,
                 ),
                 "chip_sums",
-                (row if closing else sums,) * cores,
-                [*(shard for shard, _ in batch), *owns, *rows],
-                exps=len(batch) * cores * row_count * row_count,
+                tuple(row if finished and swap else sums for swap in range(owner_count)),
+                [*(shard for (shard, _), _ in batch), *owns[:owner_count], *totals],
+                exps=row_count * row_count * sum(len(swaps) for _, swaps in batch),
             )
-        partials = [rows[0]] + [swapped(rows[swap], cores - swap) for swap in range(1, cores)]
-        last, _ = lax.optimization_barrier((last, rows[0]))
-        total = []
+        partials = [swapped(totals[swap], cores - swap) for swap in range(1, cores)]
+        last, _ = lax.optimization_barrier((last, totals[0]))
+        total = totals[0]
         for swap in range(cores):
             shard = swapped(last, swap) if swap else last
             closing = swap == cores - 1
-            operands = [shard, own, *total]
+            operands = [shard, own, total]
             result = sums
             if closing:
                 operands += partials
@@ -342,7 +368,6 @@
                     functools.partial(last_group, swap),
                     forward,
                     list_shape,
-                    swap == 0,
                     len(partials) if closing else None,
                 ),
                 "last_sums",
@@ -350,8 +375,6 @@
                 operands,
                 exps=row_count * row_count,
             )
-            if not closing:
-                total = [total]
         return total
 
     if times == 2:

time: 23.1 us -> 23 us (level)
  Pallas kernels: 7.9 us -> 7.58 us
    pallas_call x6 -> x7, Pallas kernels: 7.9 us -> 7.58 us  [call(): pl.pallas_call(kernel, name=name, out_shape=out_shapes, in_specs=[pl.Bloc...]
  transfers between devices with their start and end apart: 7 -> 7, of which waited for: 2 -> 3; matrix products, arithmetic and copies ran while one was open for 0% -> 0% of each run, Pallas kernels for 23% -> 21%
where the time goes in v3:
time: 23 us; the launch traced here: 22.8 us
  starting transfers between devices  9.41 us (41%)
  Pallas kernels  7.58 us (33%)
  waiting for transfers between devices  5.13 us (22%)
  between operations  0.69 us (3%)
    ppermute x4, starting transfers between devices, exchange(): return lax.ppermute(array, ('tm', 'cells', 'feat'), pairs)  8.32 us
    pallas_call x7, Pallas kernels, call(): pl.pallas_call(kernel, name=name, out_shape=out_shapes, in_specs=[pl.Bloc...  7.58 us
    ppermute x4, waiting for transfers between devices, exchange(): return lax.ppermute(array, ('tm', 'cells', 'feat'), pairs)  5.05 us
    ppermute x3, starting transfers between devices, swapped(): lax.ppermute(array, 'feat', [(core, (core + swap) % cores) for core in ra...  1.09 us
  transfers between devices with their start and end apart: 7, of which 3 were waited for; matrix products, arithmetic and copies ran while one was open for 0% of the time, Pallas kernels for 21%

profile of v3, /device:TPU:0, one launch (start us, length us, event | category | flops | bytes accessed | tf_op | source)
XLA Modules:
  0.0 22.8 jit_solution(4613697044470611040)
XLA Ops:
  0.6 1.0 %pack_cells.1 = (bf16[544,128]{1,0:T(8,128)(2,1)S(1)}, f32[8,1024]{1,0:T(8,128)S(1)}) custom-call(s32[2]{0:T(128)} %totals_hbm.1, bf16[1,64,1024]{2,1,0:T(8,128)(2,1)} %feats_hbm.1, f32[1,1024]{1,0:T(1,128)} %weights_hbm.1, s32[1,4,8]{2,1,0:T(4,128)} %lists_hbm.1), custom_call_target="tpu_custom_call" | custom-call | bytes 131072 | tf_op jit(solution)/shard_map/pack_cells/pallas_call | solution.py:222
  1.7 0.2 own_rows.1.refs_1_.refs_2_.own_ref
  1.9 0.5 %collective-permute-start.3 = (bf16[1040,128]{1,0:T(8,128)(2,1)S(1)}, bf16[1040,128]{1,0:T(8,128)(2,1)S(1)}, u32[]{:S(2)}, u32[]{:S(2)}) collective-permute-start(bf16[1040,128]{1,0:T(8,128)(2,1)S(1)} %own_rows.1.refs_1_.refs_2_.own_ref), channel_id=1, source_target_pairs={{0,1},{1,0},{2,3},{3,2},{4,5},{5,4},{6,7},{7,6},{8,9},{9,8},{10,11... | collective-permute-start | bytes 798728 | tf_op jit(solution)/shard_map/ppermute | solution.py:250
  2.4 4.6 %collective-permute-start = (bf16[544,128]{1,0:T(8,128)(2,1)S(1)}, bf16[544,128]{1,0:T(8,128)(2,1)S(1)}, u32[]{:S(2)}, u32[]{:S(2)}) collective-permute-start(bf16[544,128]{1,0:T(8,128)(2,1)S(1)} %get-tuple-element.9.payload_ref), channel_id=1, source_target_pairs={{0,12},{1,13},{2,14},{3,15},{4,8},{5,9},{6,10},{7,11},{8,4},{9,5},... | collective-permute-start | bytes 417800 | tf_op jit(solution)/shard_map/ppermute | solution.py:245
  7.0 1.5 %collective-permute-start.4 = (bf16[544,128]{1,0:T(8,128)(2,1)S(1)}, bf16[544,128]{1,0:T(8,128)(2,1)S(1)}, u32[]{:S(2)}, u32[]{:S(2)}) collective-permute-start(bf16[544,128]{1,0:T(8,128)(2,1)S(1)} %get-tuple-element.9.payload_ref), channel_id=1, source_target_pairs={{0,10},{1,11},{2,8},{3,9},{4,14},{5,15},{6,12},{7,13},{8,2},{9,3},... | collective-permute-start | bytes 417800 | tf_op jit(solution)/shard_map/ppermute | solution.py:245
  8.5 1.5 %collective-permute-start.2 = (bf16[544,128]{1,0:T(8,128)(2,1)S(1)}, bf16[544,128]{1,0:T(8,128)(2,1)S(1)}, u32[]{:S(2)}, u32[]{:S(2)}) collective-permute-start(bf16[544,128]{1,0:T(8,128)(2,1)S(1)} %get-tuple-element.9.payload_ref), channel_id=1, source_target_pairs={{0,8},{1,9},{2,10},{3,11},{4,12},{5,13},{6,14},{7,15},{8,0},{9,1},... | collective-permute-start | bytes 417800 | tf_op jit(solution)/shard_map/ppermute | solution.py:245
  10.0 4.3 %collective-permute-done.refs_0_.refs_1_ = bf16[544,128]{1,0:T(8,128)(2,1)S(1)} collective-permute-done((bf16[544,128]{1,0:T(8,128)(2,1)S(1)}, bf16[544,128]{1,0:T(8,128)(2,1)S(1)}, u32[]{:S(2)}, u32[]{:S(2)}) %collective-permute-start) | collective-permute-done | bytes 139296 | tf_op jit(solution)/shard_map/ppermute | solution.py:245
  14.3 0.7 %collective-permute-start.1 = (bf16[544,128]{1,0:T(8,128)(2,1)S(1)}, bf16[544,128]{1,0:T(8,128)(2,1)S(1)}, u32[]{:S(2)}, u32[]{:S(2)}) collective-permute-start(bf16[544,128]{1,0:T(8,128)(2,1)S(1)} %collective-permute-done.refs_0_.refs_1_), channel_id=1, source_target_pairs={{0,2},{1,3},{2,0},{3,1},{4,6},{5,7},{6,4},{7,5},{8,10},{9,11},{10,... | collective-permute-start | bytes 417800 | tf_op jit(solution)/shard_map/ppermute | solution.py:245
  15.0 0.8 %chip_sums.3.refs_4_ = f32[1024,128]{1,0:T(8,128)S(1)} custom-call(bf16[544,128]{1,0:T(8,128)(2,1)S(1)} %collective-permute-done.refs_0_.refs_1_, bf16[1040,128]{1,0:T(8,128)(2,1)S(1)} %own_rows.1.refs_1_.refs_2_.own_ref), custom_call_target="tpu_custom_call" | custom-call | flops 167772160 | bytes 131072 | tf_op jit(solution)/shard_map/chip_sums/pallas_call | solution.py:222
  15.8 0.0 collective-permute-done.4.refs_0_
  15.8 0.0 collective-permute-done.3.refs_3_.refs_2_
  15.8 1.9 %chip_sums.4 = (f32[1024,128]{1,0:T(8,128)S(1)}, f32[1024,128]{1,0:T(8,128)S(1)}) custom-call(bf16[544,128]{1,0:T(8,128)(2,1)S(1)} %collective-permute-done.4.refs_0_, bf16[544,128]{1,0:T(8,128)(2,1)S(1)} %collective-permute-done.refs_0_.refs_1_, bf16[1040,128]{1,0:T(8,128)(2,1)S(1)} %own_rows.1.refs_1_.refs_2_.own_ref, ...), custom_call_target="tpu_custom_call" | custom-call | flops 503316480 | bytes 131072 | tf_op jit(solution)/shard_map/chip_sums/pallas_call | solution.py:222
  17.6 0.8 %collective-permute-done.2.refs_0_ = bf16[544,128]{1,0:T(8,128)(2,1)S(1)} collective-permute-done((bf16[544,128]{1,0:T(8,128)(2,1)S(1)}, bf16[544,128]{1,0:T(8,128)(2,1)S(1)}, u32[]{:S(2)}, u32[]{:S(2)}) %collective-permute-start.2) | collective-permute-done | bytes 139296 | tf_op jit(solution)/shard_map/ppermute | solution.py:245
  18.4 1.4 %chip_sums.5 = (f32[1024,128]{1,0:T(8,128)S(1)}, f32[1,1024]{1,0:T(1,128)S(1)}) custom-call(bf16[544,128]{1,0:T(8,128)(2,1)S(1)} %collective-permute-done.2.refs_0_, bf16[1040,128]{1,0:T(8,128)(2,1)S(1)} %own_rows.1.refs_1_.refs_2_.own_ref, bf16[1040,128]{1,0:T(8,128)(2,1)S(1)} %collective-permute-done.3.refs_3_.refs_2_, ...), custom_call_target="tpu_custom_call" | custom-call | flops 335544320 | bytes 131072 | tf_op jit(solution)/shard_map/chip_sums/pallas_call | solution.py:222
  19.9 0.0 collective-permute-done.1.shard_ref
  19.9 0.1 collective-permute-start.5
  19.9 0.5 %collective-permute-start.6 = (f32[1,1024]{1,0:T(1,128)S(1)}, f32[1,1024]{1,0:T(1,128)S(1)}, u32[]{:S(2)}, u32[]{:S(2)}) collective-permute-start(f32[1,1024]{1,0:T(1,128)S(1)} %get-tuple-element.14), channel_id=1, source_target_pairs={{0,1},{1,0},{2,3},{3,2},{4,5},{5,4},{6,7},{7,6},{8,9},{9,8},{10,11... | collective-permute-start | bytes 12296 | tf_op jit(solution)/shard_map/ppermute | solution.py:250
  20.4 0.8 %last_sums.2.total_ref = f32[1024,128]{1,0:T(8,128)S(1)} custom-call(bf16[544,128]{1,0:T(8,128)(2,1)S(1)} %collective-permute-done.1.shard_ref, bf16[1040,128]{1,0:T(8,128)(2,1)S(1)} %own_rows.1.refs_1_.refs_2_.own_ref, f32[1024,128]{1,0:T(8,128)S(1)} %get-tuple-element.12.total_ref), custom_call_target="tpu_custom_call" | custom-call | flops 167772160 | bytes 131072 | tf_op jit(solution)/shard_map/last_sums/pallas_call | solution.py:222
  21.2 0.1 collective-permute-done.6.refs_0_
  21.3 0.0 collective-permute-done.5.shard_ref
  21.3 1.5 %last_sums.3 = (f32[1,1024]{1,0:T(1,128)}, f32[1,1024]{1,0:T(1,128)}) custom-call(bf16[544,128]{1,0:T(8,128)(2,1)S(1)} %collective-permute-done.5.shard_ref, bf16[1040,128]{1,0:T(8,128)(2,1)S(1)} %own_rows.1.refs_1_.refs_2_.own_ref, f32[1024,128]{1,0:T(8,128)S(1)} %last_sums.2.total_ref, f32[1,1024]{1,0:T(1,128)S(1)} %collective-permute-done.6.refs_0_, ...), custom_call_target="tpu_custom_call" | custom-call | flops 167772160 | bytes 131072 | tf_op jit(solution)/shard_map/last_sums/pallas_call | solution.py:222
Async XLA Ops:
  1.9 13.9 %collective-permute-start.3 = (bf16[1040,128]{1,0:T(8,128)(2,1)S(1)}, bf16[1040,128]{1,0:T(8,128)(2,1)S(1)}, u32[]{:S(2)}, u32[]{:S(2)}) collective-permute-start(bf16[1040,128]{1,0:T(8,128)(2,1)S(1)} %own_rows.1.refs_1_.refs_2_.own_ref), channel_id=1, source_target_pairs={{0,1},{1,0},{2,3},{3,2},{4,5},{5,4},{6,7},{7,6},{8,9},{9,8},{10,11... | collective-permute-start | bytes 798728 | tf_op jit(solution)/shard_map/ppermute | solution.py:250
  2.4 11.9 %collective-permute-start = (bf16[544,128]{1,0:T(8,128)(2,1)S(1)}, bf16[544,128]{1,0:T(8,128)(2,1)S(1)}, u32[]{:S(2)}, u32[]{:S(2)}) collective-permute-start(bf16[544,128]{1,0:T(8,128)(2,1)S(1)} %get-tuple-element.9.payload_ref), channel_id=1, source_target_pairs={{0,12},{1,13},{2,14},{3,15},{4,8},{5,9},{6,10},{7,11},{8,4},{9,5},... | collective-permute-start | bytes 417800 | tf_op jit(solution)/shard_map/ppermute | solution.py:245
  7.0 8.8 %collective-permute-start.4 = (bf16[544,128]{1,0:T(8,128)(2,1)S(1)}, bf16[544,128]{1,0:T(8,128)(2,1)S(1)}, u32[]{:S(2)}, u32[]{:S(2)}) collective-permute-start(bf16[544,128]{1,0:T(8,128)(2,1)S(1)} %get-tuple-element.9.payload_ref), channel_id=1, source_target_pairs={{0,10},{1,11},{2,8},{3,9},{4,14},{5,15},{6,12},{7,13},{8,2},{9,3},... | collective-permute-start | bytes 417800 | tf_op jit(solution)/shard_map/ppermute | solution.py:245
  8.5 9.9 %collective-permute-start.2 = (bf16[544,128]{1,0:T(8,128)(2,1)S(1)}, bf16[544,128]{1,0:T(8,128)(2,1)S(1)}, u32[]{:S(2)}, u32[]{:S(2)}) collective-permute-start(bf16[544,128]{1,0:T(8,128)(2,1)S(1)} %get-tuple-element.9.payload_ref), channel_id=1, source_target_pairs={{0,8},{1,9},{2,10},{3,11},{4,12},{5,13},{6,14},{7,15},{8,0},{9,1},... | collective-permute-start | bytes 417800 | tf_op jit(solution)/shard_map/ppermute | solution.py:245
  14.3 5.6 %collective-permute-start.1 = (bf16[544,128]{1,0:T(8,128)(2,1)S(1)}, bf16[544,128]{1,0:T(8,128)(2,1)S(1)}, u32[]{:S(2)}, u32[]{:S(2)}) collective-permute-start(bf16[544,128]{1,0:T(8,128)(2,1)S(1)} %collective-permute-done.refs_0_.refs_1_), channel_id=1, source_target_pairs={{0,2},{1,3},{2,0},{3,1},{4,6},{5,7},{6,4},{7,5},{8,10},{9,11},{10,... | collective-permute-start | bytes 417800 | tf_op jit(solution)/shard_map/ppermute | solution.py:245
  19.9 1.4 %collective-permute-start.5 = (bf16[544,128]{1,0:T(8,128)(2,1)S(1)}, bf16[544,128]{1,0:T(8,128)(2,1)S(1)}, u32[]{:S(2)}, u32[]{:S(2)}) collective-permute-start(bf16[544,128]{1,0:T(8,128)(2,1)S(1)} %collective-permute-done.1.shard_ref), channel_id=1, source_target_pairs={{0,1},{1,0},{2,3},{3,2},{4,5},{5,4},{6,7},{7,6},{8,9},{9,8},{10,11... | collective-permute-start | bytes 417800 | tf_op jit(solution)/shard_map/ppermute | solution.py:250
  19.9 1.4 %collective-permute-start.6 = (f32[1,1024]{1,0:T(1,128)S(1)}, f32[1,1024]{1,0:T(1,128)S(1)}, u32[]{:S(2)}, u32[]{:S(2)}) collective-permute-start(f32[1,1024]{1,0:T(1,128)S(1)} %get-tuple-element.14), channel_id=1, source_target_pairs={{0,1},{1,0},{2,3},{3,2},{4,5},{5,4},{6,7},{7,6},{8,9},{9,8},{10,11... | collective-permute-start | bytes 12296 | tf_op jit(solution)/shard_map/ppermute | solution.py:250

commit v4 on v3

v4 whole, which is shorter than its diff:
```python
import functools
import math

import jax
import jax.numpy as jnp
from jax import lax
from jax.experimental import pallas as pl
from jax.experimental.pallas import tpu as pltpu
from jax.sharding import PartitionSpec as P

spread = 0.5
dead_exponent = -32768.0
vmem_bytes = 32 * 1024 * 1024
lanes = 128
list_rows = 16
bf16 = jnp.bfloat16


def pieces(value):
    high = value.astype(bf16).astype(jnp.float32)
    rest = value - high
    mid = rest.astype(bf16).astype(jnp.float32)
    return high, mid, (rest - mid).astype(bf16).astype(jnp.float32)


def stacked_rows(rows, height, width):
    row_ids = lax.broadcasted_iota(jnp.int32, (height, width), 0)
    block = jnp.zeros((height, width), jnp.float32)
    for place, row in enumerate(rows):
        block = jnp.where(row_ids == place, row, block)
    return block


def lane_blocks(row):
    return jnp.concatenate(
        [row[:, start : start + lanes] for start in range(0, row.shape[1], lanes)], axis=0
    )


def here():
    return lax.axis_index("cells") * lax.axis_size("feat") + lax.axis_index("feat")


def listed_row(lists):
    source_count, list_len = lists.shape
    rows = [lists[place : place + 1] for place in range(source_count)]
    fill = jnp.full((1, lanes - source_count * list_len), -1.0, jnp.float32)
    return jnp.concatenate(rows + [fill], axis=1)


def fetch(sources, targets, sems):
    copies = [
        pltpu.make_async_copy(source, target, sems.at[place])
        for place, (source, target) in enumerate(zip(sources, targets))
    ]
    for copy in copies:
        copy.start()
    for copy in copies:
        copy.wait()


def pack_kernel(
    offset, totals_hbm, feats_hbm, weights_hbm, lists_hbm, whole_ref, facts_ref, *scratch
):
    totals_ref, feats_ref, weights_ref, lists_ref, sems = scratch
    fetch((feats_hbm, weights_hbm, lists_hbm, totals_hbm), (feats_ref, weights_ref, lists_ref, totals_ref), sems)
    _, feat_count, row_count = feats_ref.shape
    _, source_count, _ = lists_ref.shape
    slabs = row_count // lanes
    feats = feats_ref[0]
    wide = feats.astype(jnp.float32)
    squares = jnp.sum(wide * wide, axis=0, keepdims=True) / (spread * feat_count)
    positions = here() * row_count + lax.broadcasted_iota(jnp.int32, (1, row_count), 1)
    weights = weights_ref[...]
    alive = totals_ref[lax.axis_index("tm")]
    used = (positions < alive) & (weights > 1e-37)
    share = offset - squares + jnp.log(jnp.where(used, weights, 1.0))
    share = lane_blocks(jnp.where(used, share, dead_exponent))
    listed = listed_row(lists_ref[0].astype(jnp.float32))
    shares = pieces(share)
    columns = [feats[:, slab * lanes : (slab + 1) * lanes] for slab in range(slabs)]

    def bundle(first, last):
        rows = [piece[first:last] for piece in shares]
        rows.append(jnp.broadcast_to(listed, (last - first, lanes)))
        tail = jnp.concatenate(rows, axis=0).astype(bf16)
        return jnp.concatenate([*columns[first:last], tail], axis=0)

    whole_ref[...] = bundle(0, slabs)
    facts_ref[...] = stacked_rows([weights, alive.astype(jnp.float32)], 8, row_count)


def rows_kernel(source_count, feat_count, *refs):
    *part_refs, rows_ref = refs
    row_count = rows_ref.shape[0] - list_rows
    slabs = row_count // lanes // len(part_refs)
    feats = [
        part_ref[slab * feat_count : (slab + 1) * feat_count, :]
        for part_ref in part_refs
        for slab in range(slabs)
    ]
    wide = jnp.concatenate(feats, axis=1).astype(jnp.float32)
    squares = jnp.sum(wide * wide, axis=0, keepdims=True) / (spread * feat_count)
    block = lax.broadcasted_iota(jnp.int32, (1, row_count), 1) // (row_count // source_count)
    member = [jnp.where(block == place, 1.0, 0.0) for place in range(source_count)]
    tail = stacked_rows(
        [1.0, 1.0, 1.0, *pieces(-squares), 0.0, 0.0, *member], lanes - feat_count, row_count
    )
    columns = jnp.concatenate([wide * (2.0 / (spread * feat_count)), tail], axis=0)
    rows_ref[:row_count, :] = columns.T.astype(bf16)
    tail = part_refs[0][slabs * feat_count :, :].astype(jnp.float32)
    listed = tail[3 * slabs : 3 * slabs + 1]
    rows_ref[row_count:, :] = jnp.broadcast_to(listed, (list_rows, lanes)).astype(bf16)


def updated(alive, potentials, prior):
    _, row_count = potentials.shape
    positions = here() * row_count + lax.broadcasted_iota(jnp.int32, (1, row_count), 1)
    live = positions.astype(jnp.float32) < alive
    prior = jnp.where(live, prior, 0.0)
    cell_total = row_count * lax.axis_size("cells") * lax.axis_size("feat")
    wanted = cell_total / alive
    scales = potentials * jnp.sqrt(wanted / jnp.where(live, prior, 1.0))
    return jnp.where(live, scales, 0.0), prior


def closed_pairs(sent, own_lists, ours, there, blocks, forward, list_shape):
    source_count, list_len, _ = list_shape
    by_sender = lax.axis_index("tm") > 0 if forward is None else jnp.bool_(forward)
    shape = (len(blocks) * 8, lanes)
    row_ids = lax.broadcasted_iota(jnp.int32, shape, 0)
    other, block = row_ids // 8 + blocks[0], row_ids % 8
    lister = lax.broadcasted_iota(jnp.int32, shape, 1) // list_len
    values = jnp.where(by_sender, sent, own_lists)
    wanted = jnp.where(by_sender, ours * source_count + block, there * source_count + other)
    hit = (values == wanted.astype(jnp.float32)) & (lister == jnp.where(by_sender, other, block))
    found = jnp.max(jnp.where(hit, 1.0, 0.0), axis=1, keepdims=True)
    return jnp.broadcast_to(jnp.where(found > 0.0, 0.0, dead_exponent), shape)


def add_shard(shard_ref, there, part, parts, rows_ref, ours, forward, list_shape, total):
    source_count, _, feat_count = list_shape
    row_count = rows_ref.shape[0] - list_rows
    slabs = row_count // lanes // parts
    blocks = range(source_count // parts * part, source_count // parts * (part + 1))
    tail = shard_ref[slabs * feat_count : slabs * (feat_count + 4), :].astype(jnp.float32)
    own_lists = rows_ref[row_count:, :].astype(jnp.float32)[:1]
    sent = tail[3 * slabs : 3 * slabs + 1]
    closed = closed_pairs(sent, own_lists, ours, there, blocks, forward, list_shape)
    cells = rows_ref[:row_count, : feat_count + 16]
    for start in range(0, slabs, 2):
        other = start * len(blocks) // slabs
        columns = []
        for slab in (start, start + 1):
            share = [tail[piece * slabs + slab : piece * slabs + slab + 1] for piece in range(3)]
            rows = [stacked_rows([*share, 1.0, 1.0, 1.0], 8, lanes), closed[other * 8 : other * 8 + 8]]
            feats = shard_ref[slab * feat_count : (slab + 1) * feat_count, :]
            columns.append(jnp.concatenate([feats, jnp.concatenate(rows, axis=0).astype(bf16)], axis=0))
        exponents = jnp.dot(
            cells, jnp.concatenate(columns, axis=1), preferred_element_type=jnp.float32
        )
        terms = jnp.exp(exponents)
        total = total + terms[:, :lanes] + terms[:, lanes:]
    return total


def sum_kernel(jobs, ours, forward, list_shape, started, finished, *refs):
    shards, (rows_ref, *refs) = refs[: len(jobs)], refs[len(jobs) :]
    total = jnp.zeros((rows_ref.shape[0] - list_rows, lanes), jnp.float32)
    if started:
        total, refs = refs[0][...], refs[1:]
    for shard_ref, (there, part, parts) in zip(shards, jobs):
        total = add_shard(
            shard_ref, there(), part, parts, rows_ref, ours(), forward, list_shape, total
        )
    refs[0][...] = jnp.sum(total.T, axis=0, keepdims=True) if finished else total


def end_kernel(parts, facts_ref, *refs):
    message = refs[0][...]
    for part_ref in refs[1:parts]:
        message = message + part_ref[...]
    scales_ref, prior_ref = refs[parts:]
    potentials = facts_ref[0:1]
    scales_ref[...], prior_ref[...] = updated(facts_ref[1:2], potentials, potentials * message)


def call(kernel, name, out_shapes, operands, spaces=None, scratch=(), exps=0):
    spaces = spaces or [pltpu.VMEM] * len(operands)
    return pl.pallas_call(
        kernel,
        name=name,
        out_shape=out_shapes,
        in_specs=[pl.BlockSpec(memory_space=space) for space in spaces],
        out_specs=jax.tree.map(lambda _: pl.BlockSpec(memory_space=pltpu.VMEM), out_shapes),
        scratch_shapes=scratch,
        compiler_params=pltpu.CompilerParams(vmem_limit_bytes=vmem_bytes),
        cost_estimate=pl.CostEstimate(flops=160 * exps, bytes_accessed=2**17, transcendentals=exps),
    )(*operands)


def exchange(array, route):
    (moves, shift) = route
    times, count, cores = lax.axis_size("tm"), lax.axis_size("cells"), lax.axis_size("feat")
    pairs = [
        ((time * count + place) * cores + core, ((time + move) * count + shift(place)) * cores + core)
        for time in range(times)
        for move in moves
        if 0 <= time + move < times
        for place in range(count)
        for core in range(cores)
    ]
    return lax.ppermute(array, ("tm", "cells", "feat"), pairs)


def swapped(array, swap):
    cores = lax.axis_size("feat")
    return lax.ppermute(array, "feat", [(core, (core + swap) % cores) for core in range(cores)])


def on_device(principal_coordinates, present_potentials, destination_tiles, living_totals):
    _, feat_count, row_count = principal_coordinates.shape
    _, source_count, list_len = destination_tiles.shape
    block_len = row_count // source_count
    offset = 2.0 / spread - math.log(2 * list_len * block_len)
    times = lax.axis_size("tm")
    row = jax.ShapeDtypeStruct((1, row_count), jnp.float32)
    sums = jax.ShapeDtypeStruct((row_count, lanes), jnp.float32)
    payload_rows = (feat_count + 4) * row_count // lanes
    smem, vmem = pltpu.SMEM, pltpu.VMEM

    scratch = [
        smem(living_totals.shape, jnp.int32),
        vmem(principal_coordinates.shape, bf16),
        vmem(present_potentials.shape, jnp.float32),
        vmem(destination_tiles.shape, jnp.int32),
        pltpu.SemaphoreType.DMA((4,)),
    ]

    def in_hbm(*arrays):
        return [pltpu.with_memory_space_constraint(array, pltpu.HBM) for array in arrays]

    def packed(weights):
        return call(
            functools.partial(pack_kernel, offset),
            "pack_cells",
            (
                jax.ShapeDtypeStruct((payload_rows, lanes), bf16),
                jax.ShapeDtypeStruct((8, row_count), jnp.float32),
            ),
            in_hbm(living_totals, principal_coordinates, weights, destination_tiles),
            [pltpu.HBM] * 4,
            scratch,
        )

    count, cores = lax.axis_size("cells"), lax.axis_size("feat")
    xor = count > 1 and count & (count - 1) == 0

    def shifted(distance):
        return lambda place: place ^ distance if xor else (place + distance) % count

    def group_of(distance, swap=0):
        place, core = lax.axis_index("cells"), lax.axis_index("feat")
        source = jnp.bitwise_xor(place, distance) if xor else lax.rem(place + count - distance, count)
        return source * cores + lax.rem(core + cores - swap, cores)

    def cell_rows(parts):
        return call(
            functools.partial(rows_kernel, source_count, feat_count),
            "cell_rows",
            jax.ShapeDtypeStruct((row_count + list_rows, lanes), bf16),
            parts,
        )

    def summed(pack, step):
        payload, _ = pack
        forward = None if step is None else step > 0
        moves = (1, -1) if step is None else (step,)
        *distances, far = range(0, count, 2 if xor else 1)
        far_shard = exchange(payload, (moves, shifted(far)))
        shards = {distance: exchange(payload, (moves, shifted(distance))) for distance in distances}

        def added(jobs, rows, ours, total, finished):
            return call(
                functools.partial(
                    sum_kernel,
                    [place for _, place in jobs],
                    ours,
                    forward,
                    (source_count, list_len, feat_count),
                    total is not None,
                    finished,
                ),
                "sum_tiles",
                row if finished else sums,
                [*(shard for shard, _ in jobs), rows] + ([] if total is None else [total]),
                exps=len(jobs) * row_count * row_count,
            )

        def job(shard, distance, swap, part=0, parts=1):
            here_now = swapped(shard, swap) if swap else shard
            return here_now, (functools.partial(group_of, distance, swap), part, parts)

        def batch(swap):
            return [job(shard, distance, swap) for distance, shard in shards.items()]

        if not xor:
            jobs = [one for swap in range(cores) for one in batch(swap)]
            jobs += [job(far_shard, far, swap) for swap in range(cores)]
            return [added(jobs, cell_rows([payload]), group_of_own, None, True)]

        near = cell_rows([exchange(payload, ((0,), shifted(1)))])
        near_group = functools.partial(group_of, 1)
        own = cell_rows([payload])
        far_job = job(far_shard, far, 0)
        direct = [far_job, *batch(0)]
        crossed = [job(far_shard, far, swap) for swap in range(1, cores)]
        crossed += [one for swap in range(1, cores) for one in batch(swap)]
        total = added(direct, near, near_group, None, False)
        total = added(crossed, near, near_group, total, True)
        own, _ = lax.optimization_barrier((own, total))
        return [
            exchange(total, ((0,), shifted(1))),
            added([*direct, *crossed], own, group_of_own, None, True),
        ]

    group_of_own = functools.partial(group_of, 0)

    if times == 2:
        pack = packed(present_potentials)
        parts = summed(pack, None)
        return tuple(
            call(functools.partial(end_kernel, len(parts)), "end", (row, row), [pack[1], *parts])
        )

    time_here = lax.axis_index("tm")

    def advance(_, state):
        forward, backward = state
        pushed = sum(summed(packed(present_potentials * forward), 1))
        pulled = sum(summed(packed(present_potentials * backward), -1))
        return (
            jnp.where(time_here == 0, 1.0, pushed),
            jnp.where(time_here == times - 1, 1.0, pulled),
        )

    unit = jnp.ones((1, row_count), jnp.float32)
    forward, backward = lax.fori_loop(0, times - 1, advance, (unit, unit))
    return updated(living_totals[time_here].astype(jnp.float32), present_potentials, present_potentials * forward * backward)


def solution(mesh):
    in_specs = (
        P(("runs", "tm"), None, ("cells", "feat")),
        P(("runs", "tm"), ("cells", "feat")),
        P(("runs", "tm"), ("cells", "feat"), None),
        P("runs"),
    )
    out_specs = (P(("runs", "tm"), ("cells", "feat")), P(("runs", "tm"), ("cells", "feat")))
    return jax.shard_map(
        on_device, mesh=mesh, in_specs=in_specs, out_specs=out_specs, check_vma=False
    )
```

time: 23 us -> 21.6 us (0.939)
  starting transfers between devices: 9.41 us -> 8.59 us
  Pallas kernels: 7.58 us -> 7.24 us
    ppermute x3 -> x2, starting transfers between devices: 1.09 us -> 0.35 us  [swapped(): lax.ppermute(array, 'feat', [(core, (core + swap) % cores) for core in ra...]
    pallas_call x7, Pallas kernels: 7.58 us -> 7.24 us  [call(): pl.pallas_call(kernel, name=name, out_shape=out_shapes, in_specs=[pl.Bloc...]
  transfers between devices with their start and end apart: 7 -> 6, of which waited for: 3 -> 3; matrix products, arithmetic and copies ran while one was open for 0% -> 0% of each run, Pallas kernels for 21% -> 19%
where the time goes in v4:
time: 21.6 us; the launch traced here: 21.5 us
  starting transfers between devices  8.59 us (40%)
  Pallas kernels  7.24 us (34%)
  waiting for transfers between devices  4.94 us (23%)
  between operations  0.69 us (3%)
    ppermute x4, starting transfers between devices, exchange(): return lax.ppermute(array, ('tm', 'cells', 'feat'), pairs)  8.23 us
    pallas_call x7, Pallas kernels, call(): pl.pallas_call(kernel, name=name, out_shape=out_shapes, in_specs=[pl.Bloc...  7.24 us
    ppermute x4, waiting for transfers between devices, exchange(): return lax.ppermute(array, ('tm', 'cells', 'feat'), pairs)  4.93 us
  transfers between devices with their start and end apart: 6, of which 3 were waited for; matrix products, arithmetic and copies ran while one was open for 0% of the time, Pallas kernels for 19%

profile of v4, /device:TPU:0, one launch (start us, length us, event | category | flops | bytes accessed | tf_op | source)
XLA Modules:
  0.0 21.5 jit_solution(4420519255644332444)
XLA Ops:
  0.6 1.0 %pack_cells.1 = (bf16[544,128]{1,0:T(8,128)(2,1)S(1)}, f32[8,1024]{1,0:T(8,128)S(1)}) custom-call(s32[2]{0:T(128)} %totals_hbm.1, bf16[1,64,1024]{2,1,0:T(8,128)(2,1)} %feats_hbm.1, f32[1,1024]{1,0:T(1,128)} %weights_hbm.1, s32[1,4,8]{2,1,0:T(4,128)} %lists_hbm.1), custom_call_target="tpu_custom_call" | custom-call | bytes 131072 | tf_op jit(solution)/shard_map/pack_cells/pallas_call | solution.py:190
  1.7 5.0 %collective-permute-start = (bf16[544,128]{1,0:T(8,128)(2,1)S(1)}, bf16[544,128]{1,0:T(8,128)(2,1)S(1)}, u32[]{:S(2)}, u32[]{:S(2)}) collective-permute-start(bf16[544,128]{1,0:T(8,128)(2,1)S(1)} %get-tuple-element.6.refs_0_), channel_id=1, source_target_pairs={{0,12},{1,13},{2,14},{3,15},{4,8},{5,9},{6,10},{7,11},{8,4},{9,5},... | collective-permute-start | bytes 417800 | tf_op jit(solution)/shard_map/ppermute | solution.py:213
  6.7 0.5 %collective-permute-start.2 = (bf16[544,128]{1,0:T(8,128)(2,1)S(1)}, bf16[544,128]{1,0:T(8,128)(2,1)S(1)}, u32[]{:S(2)}, u32[]{:S(2)}) collective-permute-start(bf16[544,128]{1,0:T(8,128)(2,1)S(1)} %get-tuple-element.6.refs_0_), channel_id=1, source_target_pairs={{0,8},{1,9},{2,10},{3,11},{4,12},{5,13},{6,14},{7,15},{8,0},{9,1},... | collective-permute-start | bytes 417800 | tf_op jit(solution)/shard_map/ppermute | solution.py:213
  7.2 1.6 %collective-permute-start.4 = (bf16[544,128]{1,0:T(8,128)(2,1)S(1)}, bf16[544,128]{1,0:T(8,128)(2,1)S(1)}, u32[]{:S(2)}, u32[]{:S(2)}) collective-permute-start(bf16[544,128]{1,0:T(8,128)(2,1)S(1)} %get-tuple-element.6.refs_0_), channel_id=1, source_target_pairs={{0,2},{1,3},{2,0},{3,1},{4,6},{5,7},{6,4},{7,5},{8,10},{9,11},{10,... | collective-permute-start | bytes 417800 | tf_op jit(solution)/shard_map/ppermute | solution.py:213
  8.8 4.7 %collective-permute-done.refs_0_ = bf16[544,128]{1,0:T(8,128)(2,1)S(1)} collective-permute-done((bf16[544,128]{1,0:T(8,128)(2,1)S(1)}, bf16[544,128]{1,0:T(8,128)(2,1)S(1)}, u32[]{:S(2)}, u32[]{:S(2)}) %collective-permute-start) | collective-permute-done | bytes 139296 | tf_op jit(solution)/shard_map/ppermute | solution.py:213
  13.5 0.0 collective-permute-start.1
  13.5 0.2 collective-permute-done.2.refs_1_
  13.7 0.3 %collective-permute-start.3 = (bf16[544,128]{1,0:T(8,128)(2,1)S(1)}, bf16[544,128]{1,0:T(8,128)(2,1)S(1)}, u32[]{:S(2)}, u32[]{:S(2)}) collective-permute-start(bf16[544,128]{1,0:T(8,128)(2,1)S(1)} %collective-permute-done.2.refs_1_), channel_id=1, source_target_pairs={{0,1},{1,0},{2,3},{3,2},{4,5},{5,4},{6,7},{7,6},{8,9},{9,8},{10,11... | collective-permute-start | bytes 417800 | tf_op jit(solution)/shard_map/ppermute | solution.py:218
  14.0 0.2 cell_rows.3.refs_4_
  14.2 0.0 collective-permute-done.4.refs_0_
  14.2 0.2 cell_rows.2.refs_2_
  14.4 1.3 %sum_tiles.3.refs_3_ = f32[1024,128]{1,0:T(8,128)S(1)} custom-call(bf16[544,128]{1,0:T(8,128)(2,1)S(1)} %collective-permute-done.refs_0_, bf16[544,128]{1,0:T(8,128)(2,1)S(1)} %collective-permute-done.2.refs_1_, bf16[1040,128]{1,0:T(8,128)(2,1)S(1)} %cell_rows.2.refs_2_), custom_call_target="tpu_custom_call" | custom-call | flops 335544320 | bytes 131072 | tf_op jit(solution)/shard_map/sum_tiles/pallas_call | solution.py:190
  15.7 0.0 collective-permute-done.1.refs_0_.refs_2_
  15.7 0.0 collective-permute-done.3.refs_1_.refs_3_
  15.7 1.4 %sum_tiles.4 = f32[1,1024]{1,0:T(1,128)S(1)} custom-call(bf16[544,128]{1,0:T(8,128)(2,1)S(1)} %collective-permute-done.1.refs_0_.refs_2_, bf16[544,128]{1,0:T(8,128)(2,1)S(1)} %collective-permute-done.3.refs_1_.refs_3_, bf16[1040,128]{1,0:T(8,128)(2,1)S(1)} %cell_rows.2.refs_2_, f32[1024,128]{1,0:T(8,128)S(1)} %sum_tiles.3.refs_3_), custom_call_target="tpu_custom_call" | custom-call | flops 335544320 | bytes 131072 | tf_op jit(solution)/shard_map/sum_tiles/pallas_call | solution.py:190
  17.1 1.1 %collective-permute-start.5 = (f32[1,1024]{1,0:T(1,128)S(1)}, f32[1,1024]{1,0:T(1,128)S(1)}, u32[]{:S(2)}, u32[]{:S(2)}) collective-permute-start(f32[1,1024]{1,0:T(1,128)S(1)} %sum_tiles.4), channel_id=1, source_target_pairs={{0,2},{1,3},{2,0},{3,1},{4,6},{5,7},{6,4},{7,5},{8,10},{9,11},{10,... | collective-permute-start | bytes 12296 | tf_op jit(solution)/shard_map/ppermute | solution.py:213
  18.2 2.5 %sum_tiles.5.refs_1_ = f32[1,1024]{1,0:T(1,128)S(1)} custom-call(bf16[544,128]{1,0:T(8,128)(2,1)S(1)} %collective-permute-done.refs_0_, bf16[544,128]{1,0:T(8,128)(2,1)S(1)} %collective-permute-done.2.refs_1_, bf16[544,128]{1,0:T(8,128)(2,1)S(1)} %collective-permute-done.1.refs_0_.refs_2_, bf16[544,128]{1,0:T(8,128)(2,1)S(1)} %collective-permute-done.3.refs_1_.refs_3_, ...), custom_call_target="tpu_custom_call" | custom-call | flops 671088640 | bytes 131072 | tf_op jit(solution)/shard_map/sum_tiles/pallas_call | solution.py:190
  20.8 0.1 collective-permute-done.5.refs_0_
  20.8 0.6 %end.1 = (f32[1,1024]{1,0:T(1,128)}, f32[1,1024]{1,0:T(1,128)}) custom-call(f32[8,1024]{1,0:T(8,128)S(1)} %get-tuple-element.5.facts_ref, f32[1,1024]{1,0:T(1,128)S(1)} %collective-permute-done.5.refs_0_, f32[1,1024]{1,0:T(1,128)S(1)} %sum_tiles.5.refs_1_), custom_call_target="tpu_custom_call" | custom-call | bytes 131072 | tf_op jit(solution)/shard_map/end/pallas_call | solution.py:190
Async XLA Ops:
  1.7 11.8 %collective-permute-start = (bf16[544,128]{1,0:T(8,128)(2,1)S(1)}, bf16[544,128]{1,0:T(8,128)(2,1)S(1)}, u32[]{:S(2)}, u32[]{:S(2)}) collective-permute-start(bf16[544,128]{1,0:T(8,128)(2,1)S(1)} %get-tuple-element.6.refs_0_), channel_id=1, source_target_pairs={{0,12},{1,13},{2,14},{3,15},{4,8},{5,9},{6,10},{7,11},{8,4},{9,5},... | collective-permute-start | bytes 417800 | tf_op jit(solution)/shard_map/ppermute | solution.py:213
  6.7 7.0 %collective-permute-start.2 = (bf16[544,128]{1,0:T(8,128)(2,1)S(1)}, bf16[544,128]{1,0:T(8,128)(2,1)S(1)}, u32[]{:S(2)}, u32[]{:S(2)}) collective-permute-start(bf16[544,128]{1,0:T(8,128)(2,1)S(1)} %get-tuple-element.6.refs_0_), channel_id=1, source_target_pairs={{0,8},{1,9},{2,10},{3,11},{4,12},{5,13},{6,14},{7,15},{8,0},{9,1},... | collective-permute-start | bytes 417800 | tf_op jit(solution)/shard_map/ppermute | solution.py:213
  7.2 7.0 %collective-permute-start.4 = (bf16[544,128]{1,0:T(8,128)(2,1)S(1)}, bf16[544,128]{1,0:T(8,128)(2,1)S(1)}, u32[]{:S(2)}, u32[]{:S(2)}) collective-permute-start(bf16[544,128]{1,0:T(8,128)(2,1)S(1)} %get-tuple-element.6.refs_0_), channel_id=1, source_target_pairs={{0,2},{1,3},{2,0},{3,1},{4,6},{5,7},{6,4},{7,5},{8,10},{9,11},{10,... | collective-permute-start | bytes 417800 | tf_op jit(solution)/shard_map/ppermute | solution.py:213
  13.5 2.2 %collective-permute-start.1 = (bf16[544,128]{1,0:T(8,128)(2,1)S(1)}, bf16[544,128]{1,0:T(8,128)(2,1)S(1)}, u32[]{:S(2)}, u32[]{:S(2)}) collective-permute-start(bf16[544,128]{1,0:T(8,128)(2,1)S(1)} %collective-permute-done.refs_0_), channel_id=1, source_target_pairs={{0,1},{1,0},{2,3},{3,2},{4,5},{5,4},{6,7},{7,6},{8,9},{9,8},{10,11... | collective-permute-start | bytes 417800 | tf_op jit(solution)/shard_map/ppermute | solution.py:218
  13.7 2.0 %collective-permute-start.3 = (bf16[544,128]{1,0:T(8,128)(2,1)S(1)}, bf16[544,128]{1,0:T(8,128)(2,1)S(1)}, u32[]{:S(2)}, u32[]{:S(2)}) collective-permute-start(bf16[544,128]{1,0:T(8,128)(2,1)S(1)} %collective-permute-done.2.refs_1_), channel_id=1, source_target_pairs={{0,1},{1,0},{2,3},{3,2},{4,5},{5,4},{6,7},{7,6},{8,9},{9,8},{10,11... | collective-permute-start | bytes 417800 | tf_op jit(solution)/shard_map/ppermute | solution.py:218
  17.1 3.7 %collective-permute-start.5 = (f32[1,1024]{1,0:T(1,128)S(1)}, f32[1,1024]{1,0:T(1,128)S(1)}, u32[]{:S(2)}, u32[]{:S(2)}) collective-permute-start(f32[1,1024]{1,0:T(1,128)S(1)} %sum_tiles.4), channel_id=1, source_target_pairs={{0,2},{1,3},{2,0},{3,1},{4,6},{5,7},{6,4},{7,5},{8,10},{9,11},{10,... | collective-permute-start | bytes 12296 | tf_op jit(solution)/shard_map/ppermute | solution.py:213

commit v5 on v4

--- a/solution.py
+++ b/solution.py
@@ -60,7 +60,7 @@
 
 
 def pack_kernel(
-    offset, totals_hbm, feats_hbm, weights_hbm, lists_hbm, whole_ref, facts_ref, *scratch
+    offset, totals_hbm, feats_hbm, weights_hbm, lists_hbm, payload_ref, facts_ref, *scratch
 ):
     totals_ref, feats_ref, weights_ref, lists_ref, sems = scratch
     fetch((feats_hbm, weights_hbm, lists_hbm, totals_hbm), (feats_ref, weights_ref, lists_ref, totals_ref), sems)
@@ -69,36 +69,27 @@
     slabs = row_count // lanes
     feats = feats_ref[0]
     wide = feats.astype(jnp.float32)
-    squares = jnp.sum(wide * wide, axis=0, keepdims=True) / (spread * feat_count)
-    positions = here() * row_count + lax.broadcasted_iota(jnp.int32, (1, row_count), 1)
-    weights = weights_ref[...]
+    squares = lane_blocks(jnp.sum(wide * wide, axis=0, keepdims=True)) / (spread * feat_count)
+    shape = (slabs, lanes)
+    positions = here() * row_count + lanes * lax.broadcasted_iota(jnp.int32, shape, 0)
+    positions = positions + lax.broadcasted_iota(jnp.int32, shape, 1)
+    weights = lane_blocks(weights_ref[...])
     alive = totals_ref[lax.axis_index("tm")]
     used = (positions < alive) & (weights > 1e-37)
     share = offset - squares + jnp.log(jnp.where(used, weights, 1.0))
-    share = lane_blocks(jnp.where(used, share, dead_exponent))
-    listed = listed_row(lists_ref[0].astype(jnp.float32))
-    shares = pieces(share)
+    share = jnp.where(used, share, dead_exponent)
+    listed = jnp.broadcast_to(listed_row(lists_ref[0].astype(jnp.float32)), shape)
+    tail = jnp.concatenate([*pieces(share), listed], axis=0).astype(bf16)
     columns = [feats[:, slab * lanes : (slab + 1) * lanes] for slab in range(slabs)]
-
-    def bundle(first, last):
-        rows = [piece[first:last] for piece in shares]
-        rows.append(jnp.broadcast_to(listed, (last - first, lanes)))
-        tail = jnp.concatenate(rows, axis=0).astype(bf16)
-        return jnp.concatenate([*columns[first:last], tail], axis=0)
-
-    whole_ref[...] = bundle(0, slabs)
-    facts_ref[...] = stacked_rows([weights, alive.astype(jnp.float32)], 8, row_count)
-
-
-def rows_kernel(source_count, feat_count, *refs):
-    *part_refs, rows_ref = refs
+    payload_ref[...] = jnp.concatenate([*columns, tail], axis=0)
+    facts_ref[...] = stacked_rows([weights_ref[...], alive.astype(jnp.float32)], 8, row_count)
+
+
+def rows_kernel(list_shape, payload_ref, rows_ref):
+    source_count, _, feat_count = list_shape
     row_count = rows_ref.shape[0] - list_rows
-    slabs = row_count // lanes // len(part_refs)
-    feats = [
-        part_ref[slab * feat_count : (slab + 1) * feat_count, :]
-        for part_ref in part_refs
-        for slab in range(slabs)
-    ]
+    slabs = row_count // lanes
+    feats = [payload_ref[slab * feat_count : (slab + 1) * feat_count, :] for slab in range(slabs)]
     wide = jnp.concatenate(feats, axis=1).astype(jnp.float32)
     squares = jnp.sum(wide * wide, axis=0, keepdims=True) / (spread * feat_count)
     block = lax.broadcasted_iota(jnp.int32, (1, row_count), 1) // (row_count // source_count)
@@ -108,7 +99,7 @@
     )
     columns = jnp.concatenate([wide * (2.0 / (spread * feat_count)), tail], axis=0)
     rows_ref[:row_count, :] = columns.T.astype(bf16)
-    tail = part_refs[0][slabs * feat_count :, :].astype(jnp.float32)
+    tail = payload_ref[slabs * feat_count :, :].astype(jnp.float32)
     listed = tail[3 * slabs : 3 * slabs + 1]
     rows_ref[row_count:, :] = jnp.broadcast_to(listed, (list_rows, lanes)).astype(bf16)
 
@@ -124,12 +115,12 @@
     return jnp.where(live, scales, 0.0), prior
 
 
-def closed_pairs(sent, own_lists, ours, there, blocks, forward, list_shape):
+def closed_pairs(sent, own_lists, ours, there, forward, list_shape):
     source_count, list_len, _ = list_shape
     by_sender = lax.axis_index("tm") > 0 if forward is None else jnp.bool_(forward)
-    shape = (len(blocks) * 8, lanes)
+    shape = (source_count * 8, lanes)
     row_ids = lax.broadcasted_iota(jnp.int32, shape, 0)
-    other, block = row_ids // 8 + blocks[0], row_ids % 8
+    other, block = row_ids // 8, row_ids % 8
     lister = lax.broadcasted_iota(jnp.int32, shape, 1) // list_len
     values = jnp.where(by_sender, sent, own_lists)
     wanted = jnp.where(by_sender, ours * source_count + block, there * source_count + other)
@@ -138,18 +129,17 @@
     return jnp.broadcast_to(jnp.where(found > 0.0, 0.0, dead_exponent), shape)
 
 
-def add_shard(shard_ref, there, part, parts, rows_ref, ours, forward, list_shape, total):
+def add_shard(shard_ref, there, rows_ref, ours, forward, list_shape, total):
     source_count, _, feat_count = list_shape
     row_count = rows_ref.shape[0] - list_rows
-    slabs = row_count // lanes // parts
-    blocks = range(source_count // parts * part, source_count // parts * (part + 1))
-    tail = shard_ref[slabs * feat_count : slabs * (feat_count + 4), :].astype(jnp.float32)
+    slabs = row_count // lanes
+    tail = shard_ref[slabs * feat_count :, :].astype(jnp.float32)
     own_lists = rows_ref[row_count:, :].astype(jnp.float32)[:1]
     sent = tail[3 * slabs : 3 * slabs + 1]
-    closed = closed_pairs(sent, own_lists, ours, there, blocks, forward, list_shape)
+    closed = closed_pairs(sent, own_lists, ours, there, forward, list_shape)
     cells = rows_ref[:row_count, : feat_count + 16]
     for start in range(0, slabs, 2):
-        other = start * len(blocks) // slabs
+        other = start * source_count // slabs
         columns = []
         for slab in (start, start + 1):
             share = [tail[piece * slabs + slab : piece * slabs + slab + 1] for piece in range(3)]
@@ -164,15 +154,17 @@
     return total
 
 
-def sum_kernel(jobs, ours, forward, list_shape, started, finished, *refs):
-    shards, (rows_ref, *refs) = refs[: len(jobs)], refs[len(jobs) :]
+def sum_kernel(groups, ours, forward, list_shape, built, started, finished, *refs):
+    shards, (cells_ref, *refs) = refs[: len(groups)], refs[len(groups) :]
+    rows_ref = cells_ref
+    if built:
+        rows_ref, *refs = refs
+        rows_kernel(list_shape, cells_ref, rows_ref)
     total = jnp.zeros((rows_ref.shape[0] - list_rows, lanes), jnp.float32)
     if started:
         total, refs = refs[0][...], refs[1:]
-    for shard_ref, (there, part, parts) in zip(shards, jobs):
-        total = add_shard(
-            shard_ref, there(), part, parts, rows_ref, ours(), forward, list_shape, total
-        )
+    for shard_ref, there in zip(shards, groups):
+        total = add_shard(shard_ref, there(), rows_ref, ours(), forward, list_shape, total)
     refs[0][...] = jnp.sum(total.T, axis=0, keepdims=True) if finished else total
 
 
@@ -264,13 +256,11 @@
         source = jnp.bitwise_xor(place, distance) if xor else lax.rem(place + count - distance, count)
         return source * cores + lax.rem(core + cores - swap, cores)
 
-    def cell_rows(parts):
-        return call(
-            functools.partial(rows_kernel, source_count, feat_count),
-            "cell_rows",
-            jax.ShapeDtypeStruct((row_count + list_rows, lanes), bf16),
-            parts,
-        )
+    list_shape = (source_count, list_len, feat_count)
+    rows_shape = jax.ShapeDtypeStruct((row_count + list_rows, lanes), bf16)
+
+    def cell_rows(payload):
+        return call(functools.partial(rows_kernel, list_shape), "cell_rows", rows_shape, [payload])
 
     def summed(pack, step):
         payload, _ = pack
@@ -280,48 +270,49 @@
         far_shard = exchange(payload, (moves, shifted(far)))
         shards = {distance: exchange(payload, (moves, shifted(distance))) for distance in distances}
 
-        def added(jobs, rows, ours, total, finished):
+        def added(jobs, cells, ours, total=None, finished=False, built=False):
+            result = row if finished else sums
             return call(
                 functools.partial(
                     sum_kernel,
-                    [place for _, place in jobs],
+                    [there for _, there in jobs],
                     ours,
                     forward,
-                    (source_count, list_len, feat_count),
+                    list_shape,
+                    built,
                     total is not None,
                     finished,
                 ),
                 "sum_tiles",
-                row if finished else sums,
-                [*(shard for shard, _ in jobs), rows] + ([] if total is None else [total]),
+                (rows_shape, result) if built else result,
+                [*(shard for shard, _ in jobs), cells] + ([] if total is None else [total]),
                 exps=len(jobs) * row_count * row_count,
             )
 
-        def job(shard, distance, swap, part=0, parts=1):
-            here_now = swapped(shard, swap) if swap else shard
-            return here_now, (functools.partial(group_of, distance, swap), part, parts)
+        def job(shard, distance, swap):
+            return swapped(shard, swap) if swap else shard, functools.partial(group_of, distance, swap)
 
         def batch(swap):
             return [job(shard, distance, swap) for distance, shard in shards.items()]
 
+        own = cell_rows(payload)
         if not xor:
             jobs = [one for swap in range(cores) for one in batch(swap)]
             jobs += [job(far_shard, far, swap) for swap in range(cores)]
-            return [added(jobs, cell_rows([payload]), group_of_own, None, True)]
-
-        near = cell_rows([exchange(payload, ((0,), shifted(1)))])
+            return [added(jobs, own, group_of_own, finished=True)]
+
         near_group = functools.partial(group_of, 1)
-        own = cell_rows([payload])
-        far_job = job(far_shard, far, 0)
-        direct = [far_job, *batch(0)]
-        crossed = [job(far_shard, far, swap) for swap in range(1, cores)]
+        near = exchange(payload, ((0,), shifted(1)))
+        ready, _ = lax.optimization_barrier((far_shard, own))
+        direct = [job(far_shard, far, 0), *batch(0)]
+        crossed = [job(ready, far, swap) for swap in range(1, cores)]
         crossed += [one for swap in range(1, cores) for one in batch(swap)]
-        total = added(direct, near, near_group, None, False)
-        total = added(crossed, near, near_group, total, True)
+        near, total = added(direct, near, near_group, built=True)
+        total = added(crossed, near, near_group, total, finished=True)
         own, _ = lax.optimization_barrier((own, total))
         return [
             exchange(total, ((0,), shifted(1))),
-            added([*direct, *crossed], own, group_of_own, None, True),
+            added([*direct, *crossed], own, group_of_own, finished=True),
         ]
 
     group_of_own = functools.partial(group_of, 0)

time: 21.6 us -> 21.3 us (0.986)
  waiting for transfers between devices: 4.94 us -> 4.72 us
    ppermute x4, waiting for transfers between devices: 4.93 us -> 4.71 us  [exchange(): return lax.ppermute(array, ('tm', 'cells', 'feat'), pairs)]
    pallas_call x7 -> x6, Pallas kernels: 7.24 us -> 7.12 us  [call(): pl.pallas_call(kernel, name=name, out_shape=out_shapes, in_specs=[pl.Bloc...]
  transfers between devices with their start and end apart: 6 -> 6, of which waited for: 3 -> 2; matrix products, arithmetic and copies ran while one was open for 0% -> 0% of each run, Pallas kernels for 19% -> 19%
where the time goes in v5:
time: 21.3 us; the launch traced here: 21.2 us
  starting transfers between devices  8.65 us (41%)
  Pallas kernels  7.12 us (33%)
  waiting for transfers between devices  4.72 us (22%)
  between operations  0.68 us (3%)
    ppermute x4, starting transfers between devices, exchange(): return lax.ppermute(array, ('tm', 'cells', 'feat'), pairs)  8.29 us
    pallas_call x6, Pallas kernels, call(): pl.pallas_call(kernel, name=name, out_shape=out_shapes, in_specs=[pl.Bloc...  7.12 us
    ppermute x4, waiting for transfers between devices, exchange(): return lax.ppermute(array, ('tm', 'cells', 'feat'), pairs)  4.71 us
  transfers between devices with their start and end apart: 6, of which 2 were waited for; matrix products, arithmetic and copies ran while one was open for 0% of the time, Pallas kernels for 19%

profile of v5, /device:TPU:0, one launch (start us, length us, event | category | flops | bytes accessed | tf_op | source)
XLA Modules:
  0.0 21.2 jit_solution(4839899162064588749)
XLA Ops:
  0.6 1.0 %pack_cells.1 = (bf16[544,128]{1,0:T(8,128)(2,1)S(1)}, f32[8,1024]{1,0:T(8,128)S(1)}) custom-call(s32[2]{0:T(128)} %totals_hbm.1, bf16[1,64,1024]{2,1,0:T(8,128)(2,1)} %feats_hbm.1, f32[1,1024]{1,0:T(1,128)} %weights_hbm.1, s32[1,4,8]{2,1,0:T(4,128)} %lists_hbm.1), custom_call_target="tpu_custom_call" | custom-call | bytes 131072 | tf_op jit(solution)/shard_map/pack_cells/pallas_call | solution.py:182
  1.7 5.0 %collective-permute-start = (bf16[544,128]{1,0:T(8,128)(2,1)S(1)}, bf16[544,128]{1,0:T(8,128)(2,1)S(1)}, u32[]{:S(2)}, u32[]{:S(2)}) collective-permute-start(bf16[544,128]{1,0:T(8,128)(2,1)S(1)} %get-tuple-element.9.payload_ref), channel_id=1, source_target_pairs={{0,12},{1,13},{2,14},{3,15},{4,8},{5,9},{6,10},{7,11},{8,4},{9,5},... | collective-permute-start | bytes 417800 | tf_op jit(solution)/shard_map/ppermute | solution.py:205
  6.7 0.5 %collective-permute-start.2 = (bf16[544,128]{1,0:T(8,128)(2,1)S(1)}, bf16[544,128]{1,0:T(8,128)(2,1)S(1)}, u32[]{:S(2)}, u32[]{:S(2)}) collective-permute-start(bf16[544,128]{1,0:T(8,128)(2,1)S(1)} %get-tuple-element.9.payload_ref), channel_id=1, source_target_pairs={{0,8},{1,9},{2,10},{3,11},{4,12},{5,13},{6,14},{7,15},{8,0},{9,1},... | collective-permute-start | bytes 417800 | tf_op jit(solution)/shard_map/ppermute | solution.py:205
  7.2 1.6 %collective-permute-start.4 = (bf16[544,128]{1,0:T(8,128)(2,1)S(1)}, bf16[544,128]{1,0:T(8,128)(2,1)S(1)}, u32[]{:S(2)}, u32[]{:S(2)}) collective-permute-start(bf16[544,128]{1,0:T(8,128)(2,1)S(1)} %get-tuple-element.9.payload_ref), channel_id=1, source_target_pairs={{0,2},{1,3},{2,0},{3,1},{4,6},{5,7},{6,4},{7,5},{8,10},{9,11},{10,... | collective-permute-start | bytes 417800 | tf_op jit(solution)/shard_map/ppermute | solution.py:205
  8.8 0.2 cell_rows.1.refs_4_
  9.0 4.5 %collective-permute-done.refs_0_ = bf16[544,128]{1,0:T(8,128)(2,1)S(1)} collective-permute-done((bf16[544,128]{1,0:T(8,128)(2,1)S(1)}, bf16[544,128]{1,0:T(8,128)(2,1)S(1)}, u32[]{:S(2)}, u32[]{:S(2)}) %collective-permute-start) | collective-permute-done | bytes 139296 | tf_op jit(solution)/shard_map/ppermute | solution.py:205
  13.5 0.0 collective-permute-start.1
  13.5 0.2 collective-permute-done.2.refs_1_
  13.7 0.3 %collective-permute-start.3 = (bf16[544,128]{1,0:T(8,128)(2,1)S(1)}, bf16[544,128]{1,0:T(8,128)(2,1)S(1)}, u32[]{:S(2)}, u32[]{:S(2)}) collective-permute-start(bf16[544,128]{1,0:T(8,128)(2,1)S(1)} %collective-permute-done.2.refs_1_), channel_id=1, source_target_pairs={{0,1},{1,0},{2,3},{3,2},{4,5},{5,4},{6,7},{7,6},{8,9},{9,8},{10,11... | collective-permute-start | bytes 417800 | tf_op jit(solution)/shard_map/ppermute | solution.py:210
  14.0 0.0 collective-permute-done.4.refs_2_
  14.0 1.4 %sum_tiles.3 = (bf16[1040,128]{1,0:T(8,128)(2,1)S(1)}, f32[1024,128]{1,0:T(8,128)S(1)}) custom-call(bf16[544,128]{1,0:T(8,128)(2,1)S(1)} %collective-permute-done.refs_0_, bf16[544,128]{1,0:T(8,128)(2,1)S(1)} %collective-permute-done.2.refs_1_, bf16[544,128]{1,0:T(8,128)(2,1)S(1)} %collective-permute-done.4.refs_2_), custom_call_target="tpu_custom_call" | custom-call | flops 335544320 | bytes 131072 | tf_op jit(solution)/shard_map/sum_tiles/pallas_call | solution.py:182
  15.4 0.0 collective-permute-done.1.refs_0_.refs_2_
  15.4 0.0 collective-permute-done.3.refs_1_.refs_3_
  15.4 1.4 %sum_tiles.4 = f32[1,1024]{1,0:T(1,128)S(1)} custom-call(bf16[544,128]{1,0:T(8,128)(2,1)S(1)} %collective-permute-done.1.refs_0_.refs_2_, bf16[544,128]{1,0:T(8,128)(2,1)S(1)} %collective-permute-done.3.refs_1_.refs_3_, bf16[1040,128]{1,0:T(8,128)(2,1)S(1)} %get-tuple-element.11.refs_2_, f32[1024,128]{1,0:T(8,128)S(1)} %get-tuple-element.12.refs_3_), custom_call_target="tpu_custom_call" | custom-call | flops 335544320 | bytes 131072 | tf_op jit(solution)/shard_map/sum_tiles/pallas_call | solution.py:182
  16.8 1.2 %collective-permute-start.5 = (f32[1,1024]{1,0:T(1,128)S(1)}, f32[1,1024]{1,0:T(1,128)S(1)}, u32[]{:S(2)}, u32[]{:S(2)}) collective-permute-start(f32[1,1024]{1,0:T(1,128)S(1)} %sum_tiles.4), channel_id=1, source_target_pairs={{0,2},{1,3},{2,0},{3,1},{4,6},{5,7},{6,4},{7,5},{8,10},{9,11},{10,... | collective-permute-start | bytes 12296 | tf_op jit(solution)/shard_map/ppermute | solution.py:205
  18.0 2.5 %sum_tiles.5.refs_1_ = f32[1,1024]{1,0:T(1,128)S(1)} custom-call(bf16[544,128]{1,0:T(8,128)(2,1)S(1)} %collective-permute-done.refs_0_, bf16[544,128]{1,0:T(8,128)(2,1)S(1)} %collective-permute-done.2.refs_1_, bf16[544,128]{1,0:T(8,128)(2,1)S(1)} %collective-permute-done.1.refs_0_.refs_2_, bf16[544,128]{1,0:T(8,128)(2,1)S(1)} %collective-permute-done.3.refs_1_.refs_3_, ...), custom_call_target="tpu_custom_call" | custom-call | flops 671088640 | bytes 131072 | tf_op jit(solution)/shard_map/sum_tiles/pallas_call | solution.py:182
  20.5 0.0 collective-permute-done.5.refs_0_
  20.5 0.6 %end.1 = (f32[1,1024]{1,0:T(1,128)}, f32[1,1024]{1,0:T(1,128)}) custom-call(f32[8,1024]{1,0:T(8,128)S(1)} %get-tuple-element.8.facts_ref, f32[1,1024]{1,0:T(1,128)S(1)} %collective-permute-done.5.refs_0_, f32[1,1024]{1,0:T(1,128)S(1)} %sum_tiles.5.refs_1_), custom_call_target="tpu_custom_call" | custom-call | bytes 131072 | tf_op jit(solution)/shard_map/end/pallas_call | solution.py:182
Async XLA Ops:
  1.7 11.8 %collective-permute-start = (bf16[544,128]{1,0:T(8,128)(2,1)S(1)}, bf16[544,128]{1,0:T(8,128)(2,1)S(1)}, u32[]{:S(2)}, u32[]{:S(2)}) collective-permute-start(bf16[544,128]{1,0:T(8,128)(2,1)S(1)} %get-tuple-element.9.payload_ref), channel_id=1, source_target_pairs={{0,12},{1,13},{2,14},{3,15},{4,8},{5,9},{6,10},{7,11},{8,4},{9,5},... | collective-permute-start | bytes 417800 | tf_op jit(solution)/shard_map/ppermute | solution.py:205
  6.7 7.0 %collective-permute-start.2 = (bf16[544,128]{1,0:T(8,128)(2,1)S(1)}, bf16[544,128]{1,0:T(8,128)(2,1)S(1)}, u32[]{:S(2)}, u32[]{:S(2)}) collective-permute-start(bf16[544,128]{1,0:T(8,128)(2,1)S(1)} %get-tuple-element.9.payload_ref), channel_id=1, source_target_pairs={{0,8},{1,9},{2,10},{3,11},{4,12},{5,13},{6,14},{7,15},{8,0},{9,1},... | collective-permute-start | bytes 417800 | tf_op jit(solution)/shard_map/ppermute | solution.py:205
  7.2 6.8 %collective-permute-start.4 = (bf16[544,128]{1,0:T(8,128)(2,1)S(1)}, bf16[544,128]{1,0:T(8,128)(2,1)S(1)}, u32[]{:S(2)}, u32[]{:S(2)}) collective-permute-start(bf16[544,128]{1,0:T(8,128)(2,1)S(1)} %get-tuple-element.9.payload_ref), channel_id=1, source_target_pairs={{0,2},{1,3},{2,0},{3,1},{4,6},{5,7},{6,4},{7,5},{8,10},{9,11},{10,... | collective-permute-start | bytes 417800 | tf_op jit(solution)/shard_map/ppermute | solution.py:205
  13.5 1.9 %collective-permute-start.1 = (bf16[544,128]{1,0:T(8,128)(2,1)S(1)}, bf16[544,128]{1,0:T(8,128)(2,1)S(1)}, u32[]{:S(2)}, u32[]{:S(2)}) collective-permute-start(bf16[544,128]{1,0:T(8,128)(2,1)S(1)} %collective-permute-done.refs_0_), channel_id=1, source_target_pairs={{0,1},{1,0},{2,3},{3,2},{4,5},{5,4},{6,7},{7,6},{8,9},{9,8},{10,11... | collective-permute-start | bytes 417800 | tf_op jit(solution)/shard_map/ppermute | solution.py:210
  13.7 1.7 %collective-permute-start.3 = (bf16[544,128]{1,0:T(8,128)(2,1)S(1)}, bf16[544,128]{1,0:T(8,128)(2,1)S(1)}, u32[]{:S(2)}, u32[]{:S(2)}) collective-permute-start(bf16[544,128]{1,0:T(8,128)(2,1)S(1)} %collective-permute-done.2.refs_1_), channel_id=1, source_target_pairs={{0,1},{1,0},{2,3},{3,2},{4,5},{5,4},{6,7},{7,6},{8,9},{9,8},{10,11... | collective-permute-start | bytes 417800 | tf_op jit(solution)/shard_map/ppermute | solution.py:210
  16.8 3.7 %collective-permute-start.5 = (f32[1,1024]{1,0:T(1,128)S(1)}, f32[1,1024]{1,0:T(1,128)S(1)}, u32[]{:S(2)}, u32[]{:S(2)}) collective-permute-start(f32[1,1024]{1,0:T(1,128)S(1)} %sum_tiles.4), channel_id=1, source_target_pairs={{0,2},{1,3},{2,0},{3,1},{4,6},{5,7},{6,4},{7,5},{8,10},{9,11},{10,... | collective-permute-start | bytes 12296 | tf_op jit(solution)/shard_map/ppermute | solution.py:205

commit v6 on v5

--- a/solution.py
+++ b/solution.py
@@ -13,6 +13,8 @@
 vmem_bytes = 32 * 1024 * 1024
 lanes = 128
 list_rows = 16
+pairs_at_once = 6
+feat_copies = 4
 bf16 = jnp.bfloat16
 
 
@@ -63,8 +65,14 @@
     offset, totals_hbm, feats_hbm, weights_hbm, lists_hbm, payload_ref, facts_ref, *scratch
 ):
     totals_ref, feats_ref, weights_ref, lists_ref, sems = scratch
-    fetch((feats_hbm, weights_hbm, lists_hbm, totals_hbm), (feats_ref, weights_ref, lists_ref, totals_ref), sems)
     _, feat_count, row_count = feats_ref.shape
+    share = feat_count // feat_copies
+    parts = [pl.ds(start, share) for start in range(0, feat_count, share)]
+    fetch(
+        [*(feats_hbm.at[:, part, :] for part in parts), weights_hbm, lists_hbm, totals_hbm],
+        [*(feats_ref.at[:, part, :] for part in parts), weights_ref, lists_ref, totals_ref],
+        sems,
+    )
     _, source_count, _ = lists_ref.shape
     slabs = row_count // lanes
     feats = feats_ref[0]
@@ -115,56 +123,96 @@
     return jnp.where(live, scales, 0.0), prior
 
 
-def closed_pairs(sent, own_lists, ours, there, forward, list_shape):
+def listed_pairs(tails, own_lists, ours, groups, forward, list_shape):
     source_count, list_len, _ = list_shape
     by_sender = lax.axis_index("tm") > 0 if forward is None else jnp.bool_(forward)
-    shape = (source_count * 8, lanes)
-    row_ids = lax.broadcasted_iota(jnp.int32, shape, 0)
-    other, block = row_ids // 8, row_ids % 8
-    lister = lax.broadcasted_iota(jnp.int32, shape, 1) // list_len
-    values = jnp.where(by_sender, sent, own_lists)
-    wanted = jnp.where(by_sender, ours * source_count + block, there * source_count + other)
-    hit = (values == wanted.astype(jnp.float32)) & (lister == jnp.where(by_sender, other, block))
-    found = jnp.max(jnp.where(hit, 1.0, 0.0), axis=1, keepdims=True)
-    return jnp.broadcast_to(jnp.where(found > 0.0, 0.0, dead_exponent), shape)
-
-
-def add_shard(shard_ref, there, rows_ref, ours, forward, list_shape, total):
+    lister = lax.broadcasted_iota(jnp.int32, (1, lanes), 1) // list_len
+    found = jnp.zeros((1, lanes), jnp.int32)
+    for shard, (sent, there) in enumerate(zip(tails, groups)):
+        values = jnp.where(by_sender, sent, own_lists)
+        first = jnp.where(by_sender, ours, there) * source_count
+        for place in range(source_count):
+            bit = jnp.where(by_sender, place * source_count + lister, lister * source_count + place)
+            bit = bit + shard * source_count**2
+            hit = values == (first + place).astype(jnp.float32)
+            found = found + jnp.where(hit, jnp.left_shift(1, bit), 0)
+    return jnp.sum(found)
+
+
+def sum_pairs(shards, groups, rows_ref, ours, forward, list_shape, list_ref, tiles_ref, total_ref):
     source_count, _, feat_count = list_shape
     row_count = rows_ref.shape[0] - list_rows
+    block_len = row_count // source_count
     slabs = row_count // lanes
-    tail = shard_ref[slabs * feat_count :, :].astype(jnp.float32)
+    depth = feat_count + 16
     own_lists = rows_ref[row_count:, :].astype(jnp.float32)[:1]
-    sent = tail[3 * slabs : 3 * slabs + 1]
-    closed = closed_pairs(sent, own_lists, ours, there, forward, list_shape)
-    cells = rows_ref[:row_count, : feat_count + 16]
-    for start in range(0, slabs, 2):
-        other = start * source_count // slabs
-        columns = []
-        for slab in (start, start + 1):
+    tails = []
+    for place, shard_ref in enumerate(shards):
+        tail = shard_ref[slabs * feat_count :, :].astype(jnp.float32)
+        tails.append(tail[3 * slabs : 3 * slabs + 1])
+        for slab in range(slabs):
             share = [tail[piece * slabs + slab : piece * slabs + slab + 1] for piece in range(3)]
-            rows = [stacked_rows([*share, 1.0, 1.0, 1.0], 8, lanes), closed[other * 8 : other * 8 + 8]]
+            rows = stacked_rows([*share, 1.0, 1.0, 1.0], 16, lanes).astype(bf16)
             feats = shard_ref[slab * feat_count : (slab + 1) * feat_count, :]
-            columns.append(jnp.concatenate([feats, jnp.concatenate(rows, axis=0).astype(bf16)], axis=0))
-        exponents = jnp.dot(
-            cells, jnp.concatenate(columns, axis=1), preferred_element_type=jnp.float32
-        )
-        terms = jnp.exp(exponents)
-        total = total + terms[:, :lanes] + terms[:, lanes:]
-    return total
+            start = (place * slabs + slab) * depth
+            tiles_ref[start : start + depth, :] = jnp.concatenate([feats, rows], axis=0)
+    square = source_count**2
+    at_once = 32 // square
+    count = jnp.int32(0)
+    for first in range(0, len(shards), at_once):
+        last = min(first + at_once, len(shards))
+        bits = listed_pairs(tails[first:last], own_lists, ours, groups[first:last], forward, list_shape)
+        for place in range((last - first) * square):
+            list_ref[count] = jnp.int32(first * square + place)
+            count = count + jnp.bitwise_and(jnp.right_shift(bits, place), 1)
+    pair_total = len(shards) * square
+    for place in range(pairs_at_once - 1):
+        list_ref[count + place] = jnp.int32(pair_total)
+
+    def step(index, carry):
+        sums = []
+        for place in range(pairs_at_once):
+            listed = list_ref[index * pairs_at_once + place]
+            pair = jnp.minimum(listed, pair_total - 1)
+            block, other = lax.rem(pair // source_count, source_count), lax.rem(pair, source_count)
+            row = pl.multiple_of(block * block_len, block_len)
+            tile = (pair // square * source_count + other) * (slabs // source_count) * depth
+            columns = [
+                tiles_ref[pl.ds(pl.multiple_of(tile + slab * depth, 16), depth), :]
+                for slab in range(slabs // source_count)
+            ]
+            exponents = jnp.dot(
+                rows_ref[pl.ds(row, block_len), :depth],
+                jnp.concatenate(columns, axis=1),
+                preferred_element_type=jnp.float32,
+            )
+            terms = jnp.exp(exponents)
+            added = terms[:, :lanes]
+            for start in range(lanes, block_len, lanes):
+                added = added + terms[:, start : start + lanes]
+            sums.append((jnp.where(listed < pair_total, row, row_count), added))
+        for row, added in sums:
+            total_ref[pl.ds(pl.multiple_of(row, block_len), block_len), :] += added
+        return carry
+
+    lax.fori_loop(0, (count + pairs_at_once - 1) // pairs_at_once, step, 0)
 
 
 def sum_kernel(groups, ours, forward, list_shape, built, started, finished, *refs):
+    *refs, list_ref, tiles_ref, total_ref = refs
     shards, (cells_ref, *refs) = refs[: len(groups)], refs[len(groups) :]
     rows_ref = cells_ref
     if built:
         rows_ref, *refs = refs
         rows_kernel(list_shape, cells_ref, rows_ref)
-    total = jnp.zeros((rows_ref.shape[0] - list_rows, lanes), jnp.float32)
+    row_count = rows_ref.shape[0] - list_rows
     if started:
-        total, refs = refs[0][...], refs[1:]
-    for shard_ref, there in zip(shards, groups):
-        total = add_shard(shard_ref, there(), rows_ref, ours(), forward, list_shape, total)
+        total_ref[:row_count, :], refs = refs[0][...], refs[1:]
+    else:
+        total_ref[:row_count, :] = jnp.zeros((row_count, lanes), jnp.float32)
+    theres = [there() for there in groups]
+    sum_pairs(shards, theres, rows_ref, ours(), forward, list_shape, list_ref, tiles_ref, total_ref)
+    total = total_ref[:row_count, :]
     refs[0][...] = jnp.sum(total.T, axis=0, keepdims=True) if finished else total
 
 
@@ -226,7 +274,7 @@
         vmem(principal_coordinates.shape, bf16),
         vmem(present_potentials.shape, jnp.float32),
         vmem(destination_tiles.shape, jnp.int32),
-        pltpu.SemaphoreType.DMA((4,)),
+        pltpu.SemaphoreType.DMA((feat_copies + 3,)),
     ]
 
     def in_hbm(*arrays):
@@ -286,6 +334,11 @@
                 "sum_tiles",
                 (rows_shape, result) if built else result,
                 [*(shard for shard, _ in jobs), cells] + ([] if total is None else [total]),
+                scratch=[
+                    smem((len(jobs) * source_count**2 + pairs_at_once,), jnp.int32),
+                    vmem((len(jobs) * (feat_count + 16) * row_count // lanes, lanes), bf16),
+                    vmem((row_count + block_len, lanes), jnp.float32),
+                ],
                 exps=len(jobs) * row_count * row_count,
             )
 

time: 21.3 us -> 21.1 us (level)
  Pallas kernels: 7.12 us -> 6.43 us
  waiting for transfers between devices: 4.72 us -> 5.27 us
    pallas_call x6, Pallas kernels: 7.12 us -> 6.43 us  [call(): pl.pallas_call(kernel, name=name, out_shape=out_shapes, in_specs=[pl.Bloc...]
    ppermute x4, waiting for transfers between devices: 4.71 us -> 5.13 us  [exchange(): return lax.ppermute(array, ('tm', 'cells', 'feat'), pairs)]
  transfers between devices with their start and end apart: 6 -> 6, of which waited for: 2 -> 4; matrix products, arithmetic and copies ran while one was open for 0% -> 0% of each run, Pallas kernels for 19% -> 16%
where the time goes in v6:
time: 21.1 us; the launch traced here: 20.9 us
  starting transfers between devices  8.51 us (40%)
  Pallas kernels  6.43 us (30%)
  waiting for transfers between devices  5.27 us (25%)
  between operations  0.68 us (3%)
    ppermute x4, starting transfers between devices, exchange(): return lax.ppermute(array, ('tm', 'cells', 'feat'), pairs)  8.16 us
    pallas_call x6, Pallas kernels, call(): pl.pallas_call(kernel, name=name, out_shape=out_shapes, in_specs=[pl.Bloc...  6.43 us
    ppermute x4, waiting for transfers between devices, exchange(): return lax.ppermute(array, ('tm', 'cells', 'feat'), pairs)  5.13 us
  transfers between devices with their start and end apart: 6, of which 4 were waited for; matrix products, arithmetic and copies ran while one was open for 0% of the time, Pallas kernels for 16%

profile of v6, /device:TPU:0, one launch (start us, length us, event | category | flops | bytes accessed | tf_op | source)
XLA Modules:
  0.0 20.9 jit_solution(3488446189284977455)
XLA Ops:
  0.6 1.0 %pack_cells.1 = (bf16[544,128]{1,0:T(8,128)(2,1)S(1)}, f32[8,1024]{1,0:T(8,128)S(1)}) custom-call(s32[2]{0:T(128)} %totals_hbm.1, bf16[1,64,1024]{2,1,0:T(8,128)(2,1)} %feats_hbm.1, f32[1,1024]{1,0:T(1,128)} %weights_hbm.1, s32[1,4,8]{2,1,0:T(4,128)} %lists_hbm.1), custom_call_target="tpu_custom_call" | custom-call | bytes 131072 | tf_op jit(solution)/shard_map/pack_cells/pallas_call | solution.py:230
  1.6 5.0 %collective-permute-start = (bf16[544,128]{1,0:T(8,128)(2,1)S(1)}, bf16[544,128]{1,0:T(8,128)(2,1)S(1)}, u32[]{:S(2)}, u32[]{:S(2)}) collective-permute-start(bf16[544,128]{1,0:T(8,128)(2,1)S(1)} %get-tuple-element.9.payload_ref), channel_id=1, source_target_pairs={{0,12},{1,13},{2,14},{3,15},{4,8},{5,9},{6,10},{7,11},{8,4},{9,5},... | collective-permute-start | bytes 417800 | tf_op jit(solution)/shard_map/ppermute | solution.py:253
  6.6 0.5 %collective-permute-start.2 = (bf16[544,128]{1,0:T(8,128)(2,1)S(1)}, bf16[544,128]{1,0:T(8,128)(2,1)S(1)}, u32[]{:S(2)}, u32[]{:S(2)}) collective-permute-start(bf16[544,128]{1,0:T(8,128)(2,1)S(1)} %get-tuple-element.9.payload_ref), channel_id=1, source_target_pairs={{0,8},{1,9},{2,10},{3,11},{4,12},{5,13},{6,14},{7,15},{8,0},{9,1},... | collective-permute-start | bytes 417800 | tf_op jit(solution)/shard_map/ppermute | solution.py:253
  7.2 1.6 %collective-permute-start.4 = (bf16[544,128]{1,0:T(8,128)(2,1)S(1)}, bf16[544,128]{1,0:T(8,128)(2,1)S(1)}, u32[]{:S(2)}, u32[]{:S(2)}) collective-permute-start(bf16[544,128]{1,0:T(8,128)(2,1)S(1)} %get-tuple-element.9.payload_ref), channel_id=1, source_target_pairs={{0,2},{1,3},{2,0},{3,1},{4,6},{5,7},{6,4},{7,5},{8,10},{9,11},{10,... | collective-permute-start | bytes 417800 | tf_op jit(solution)/shard_map/ppermute | solution.py:253
  8.7 0.2 cell_rows.1.refs_4_
  8.9 4.5 %collective-permute-done.refs_0_ = bf16[544,128]{1,0:T(8,128)(2,1)S(1)} collective-permute-done((bf16[544,128]{1,0:T(8,128)(2,1)S(1)}, bf16[544,128]{1,0:T(8,128)(2,1)S(1)}, u32[]{:S(2)}, u32[]{:S(2)}) %collective-permute-start) | collective-permute-done | bytes 139296 | tf_op jit(solution)/shard_map/ppermute | solution.py:253
  13.4 0.0 collective-permute-start.1
  13.4 0.2 collective-permute-done.2.refs_1_
  13.6 0.3 %collective-permute-start.3 = (bf16[544,128]{1,0:T(8,128)(2,1)S(1)}, bf16[544,128]{1,0:T(8,128)(2,1)S(1)}, u32[]{:S(2)}, u32[]{:S(2)}) collective-permute-start(bf16[544,128]{1,0:T(8,128)(2,1)S(1)} %collective-permute-done.2.refs_1_), channel_id=1, source_target_pairs={{0,1},{1,0},{2,3},{3,2},{4,5},{5,4},{6,7},{7,6},{8,9},{9,8},{10,11... | collective-permute-start | bytes 417800 | tf_op jit(solution)/shard_map/ppermute | solution.py:258
  14.0 0.0 collective-permute-done.4.refs_2_
  14.0 0.9 %sum_tiles.3 = (bf16[1040,128]{1,0:T(8,128)(2,1)S(1)}, f32[1024,128]{1,0:T(8,128)S(1)}) custom-call(bf16[544,128]{1,0:T(8,128)(2,1)S(1)} %collective-permute-done.refs_0_, bf16[544,128]{1,0:T(8,128)(2,1)S(1)} %collective-permute-done.2.refs_1_, bf16[544,128]{1,0:T(8,128)(2,1)S(1)} %collective-permute-done.4.refs_2_), custom_call_target="tpu_custom_call" | custom-call | flops 335544320 | bytes 131072 | tf_op jit(solution)/shard_map/sum_tiles/pallas_call | solution.py:230
  14.8 0.0 collective-permute-done.1.refs_0_.refs_2_
  14.9 0.1 collective-permute-done.3.refs_1_.refs_3_
  15.0 1.6 %sum_tiles.4 = f32[1,1024]{1,0:T(1,128)S(1)} custom-call(bf16[544,128]{1,0:T(8,128)(2,1)S(1)} %collective-permute-done.1.refs_0_.refs_2_, bf16[544,128]{1,0:T(8,128)(2,1)S(1)} %collective-permute-done.3.refs_1_.refs_3_, bf16[1040,128]{1,0:T(8,128)(2,1)S(1)} %get-tuple-element.11.refs_2_, f32[1024,128]{1,0:T(8,128)S(1)} %get-tuple-element.12.refs_3_), custom_call_target="tpu_custom_call" | custom-call | flops 335544320 | bytes 131072 | tf_op jit(solution)/shard_map/sum_tiles/pallas_call | solution.py:230
  16.6 1.0 %collective-permute-start.5 = (f32[1,1024]{1,0:T(1,128)S(1)}, f32[1,1024]{1,0:T(1,128)S(1)}, u32[]{:S(2)}, u32[]{:S(2)}) collective-permute-start(f32[1,1024]{1,0:T(1,128)S(1)} %sum_tiles.4), channel_id=1, source_target_pairs={{0,2},{1,3},{2,0},{3,1},{4,6},{5,7},{6,4},{7,5},{8,10},{9,11},{10,... | collective-permute-start | bytes 12296 | tf_op jit(solution)/shard_map/ppermute | solution.py:253
  17.6 2.2 %sum_tiles.5.refs_1_ = f32[1,1024]{1,0:T(1,128)S(1)} custom-call(bf16[544,128]{1,0:T(8,128)(2,1)S(1)} %collective-permute-done.refs_0_, bf16[544,128]{1,0:T(8,128)(2,1)S(1)} %collective-permute-done.2.refs_1_, bf16[544,128]{1,0:T(8,128)(2,1)S(1)} %collective-permute-done.1.refs_0_.refs_2_, bf16[544,128]{1,0:T(8,128)(2,1)S(1)} %collective-permute-done.3.refs_1_.refs_3_, ...), custom_call_target="tpu_custom_call" | custom-call | flops 671088640 | bytes 131072 | tf_op jit(solution)/shard_map/sum_tiles/pallas_call | solution.py:230
  19.8 0.4 %collective-permute-done.5.refs_0_ = f32[1,1024]{1,0:T(1,128)S(1)} collective-permute-done((f32[1,1024]{1,0:T(1,128)S(1)}, f32[1,1024]{1,0:T(1,128)S(1)}, u32[]{:S(2)}, u32[]{:S(2)}) %collective-permute-start.5) | collective-permute-done | bytes 4128 | tf_op jit(solution)/shard_map/ppermute | solution.py:253
  20.3 0.6 %end.1 = (f32[1,1024]{1,0:T(1,128)}, f32[1,1024]{1,0:T(1,128)}) custom-call(f32[8,1024]{1,0:T(8,128)S(1)} %get-tuple-element.8.facts_ref, f32[1,1024]{1,0:T(1,128)S(1)} %collective-permute-done.5.refs_0_, f32[1,1024]{1,0:T(1,128)S(1)} %sum_tiles.5.refs_1_), custom_call_target="tpu_custom_call" | custom-call | bytes 131072 | tf_op jit(solution)/shard_map/end/pallas_call | solution.py:230
Async XLA Ops:
  1.6 11.8 %collective-permute-start = (bf16[544,128]{1,0:T(8,128)(2,1)S(1)}, bf16[544,128]{1,0:T(8,128)(2,1)S(1)}, u32[]{:S(2)}, u32[]{:S(2)}) collective-permute-start(bf16[544,128]{1,0:T(8,128)(2,1)S(1)} %get-tuple-element.9.payload_ref), channel_id=1, source_target_pairs={{0,12},{1,13},{2,14},{3,15},{4,8},{5,9},{6,10},{7,11},{8,4},{9,5},... | collective-permute-start | bytes 417800 | tf_op jit(solution)/shard_map/ppermute | solution.py:253
  6.6 7.0 %collective-permute-start.2 = (bf16[544,128]{1,0:T(8,128)(2,1)S(1)}, bf16[544,128]{1,0:T(8,128)(2,1)S(1)}, u32[]{:S(2)}, u32[]{:S(2)}) collective-permute-start(bf16[544,128]{1,0:T(8,128)(2,1)S(1)} %get-tuple-element.9.payload_ref), channel_id=1, source_target_pairs={{0,8},{1,9},{2,10},{3,11},{4,12},{5,13},{6,14},{7,15},{8,0},{9,1},... | collective-permute-start | bytes 417800 | tf_op jit(solution)/shard_map/ppermute | solution.py:253
  7.2 6.8 %collective-permute-start.4 = (bf16[544,128]{1,0:T(8,128)(2,1)S(1)}, bf16[544,128]{1,0:T(8,128)(2,1)S(1)}, u32[]{:S(2)}, u32[]{:S(2)}) collective-permute-start(bf16[544,128]{1,0:T(8,128)(2,1)S(1)} %get-tuple-element.9.payload_ref), channel_id=1, source_target_pairs={{0,2},{1,3},{2,0},{3,1},{4,6},{5,7},{6,4},{7,5},{8,10},{9,11},{10,... | collective-permute-start | bytes 417800 | tf_op jit(solution)/shard_map/ppermute | solution.py:253
  13.4 1.4 %collective-permute-start.1 = (bf16[544,128]{1,0:T(8,128)(2,1)S(1)}, bf16[544,128]{1,0:T(8,128)(2,1)S(1)}, u32[]{:S(2)}, u32[]{:S(2)}) collective-permute-start(bf16[544,128]{1,0:T(8,128)(2,1)S(1)} %collective-permute-done.refs_0_), channel_id=1, source_target_pairs={{0,1},{1,0},{2,3},{3,2},{4,5},{5,4},{6,7},{7,6},{8,9},{9,8},{10,11... | collective-permute-start | bytes 417800 | tf_op jit(solution)/shard_map/ppermute | solution.py:258
  13.6 1.4 %collective-permute-start.3 = (bf16[544,128]{1,0:T(8,128)(2,1)S(1)}, bf16[544,128]{1,0:T(8,128)(2,1)S(1)}, u32[]{:S(2)}, u32[]{:S(2)}) collective-permute-start(bf16[544,128]{1,0:T(8,128)(2,1)S(1)} %collective-permute-done.2.refs_1_), channel_id=1, source_target_pairs={{0,1},{1,0},{2,3},{3,2},{4,5},{5,4},{6,7},{7,6},{8,9},{9,8},{10,11... | collective-permute-start | bytes 417800 | tf_op jit(solution)/shard_map/ppermute | solution.py:258
  16.6 3.7 %collective-permute-start.5 = (f32[1,1024]{1,0:T(1,128)S(1)}, f32[1,1024]{1,0:T(1,128)S(1)}, u32[]{:S(2)}, u32[]{:S(2)}) collective-permute-start(f32[1,1024]{1,0:T(1,128)S(1)} %sum_tiles.4), channel_id=1, source_target_pairs={{0,2},{1,3},{2,0},{3,1},{4,6},{5,7},{6,4},{7,5},{8,10},{9,11},{10,... | collective-permute-start | bytes 12296 | tf_op jit(solution)/shard_map/ppermute | solution.py:253

commit v7 on v6

--- a/solution.py
+++ b/solution.py
@@ -169,10 +169,10 @@
     for place in range(pairs_at_once - 1):
         list_ref[count + place] = jnp.int32(pair_total)
 
-    def step(index, carry):
+    def step(taken, size):
         sums = []
-        for place in range(pairs_at_once):
-            listed = list_ref[index * pairs_at_once + place]
+        for place in range(size):
+            listed = list_ref[taken + place]
             pair = jnp.minimum(listed, pair_total - 1)
             block, other = lax.rem(pair // source_count, source_count), lax.rem(pair, source_count)
             row = pl.multiple_of(block * block_len, block_len)
@@ -193,9 +193,18 @@
             sums.append((jnp.where(listed < pair_total, row, row_count), added))
         for row, added in sums:
             total_ref[pl.ds(pl.multiple_of(row, block_len), block_len), :] += added
+
+    def whole_step(index, carry):
+        step(index * pairs_at_once, pairs_at_once)
         return carry
 
-    lax.fori_loop(0, (count + pairs_at_once - 1) // pairs_at_once, step, 0)
+    half = pairs_at_once // 2
+    whole_steps = (count + pairs_at_once - 1 - half) // pairs_at_once
+    lax.fori_loop(0, whole_steps, whole_step, 0)
+
+    @pl.when(count > whole_steps * pairs_at_once)
+    def _():
+        step(whole_steps * pairs_at_once, half)
 
 
 def sum_kernel(groups, ours, forward, list_shape, built, started, finished, *refs):

time: 21.1 us -> 21.1 us (level); the launches traced: 20.9 us -> 21.2 us
  Pallas kernels: 6.43 us -> 7.13 us
  waiting for transfers between devices: 5.27 us -> 4.72 us
    pallas_call x6, Pallas kernels: 6.43 us -> 7.13 us  [call(): pl.pallas_call(kernel, name=name, out_shape=out_shapes, in_specs=[pl.Bloc...]
    ppermute x4, waiting for transfers between devices: 5.13 us -> 4.71 us  [exchange(): return lax.ppermute(array, ('tm', 'cells', 'feat'), pairs)]
  transfers between devices with their start and end apart: 6 -> 6, of which waited for: 4 -> 2; matrix products, arithmetic and copies ran while one was open for 0% -> 0% of each run, Pallas kernels for 16% -> 20%
where the time goes in v7:
time: 21.1 us; the launch traced here: 21.2 us
  starting transfers between devices  8.67 us (41%)
  Pallas kernels  7.13 us (34%)
  waiting for transfers between devices  4.72 us (22%)
  between operations  0.69 us (3%)
    ppermute x4, starting transfers between devices, exchange(): return lax.ppermute(array, ('tm', 'cells', 'feat'), pairs)  8.32 us
    pallas_call x6, Pallas kernels, call(): pl.pallas_call(kernel, name=name, out_shape=out_shapes, in_specs=[pl.Bloc...  7.13 us
    ppermute x4, waiting for transfers between devices, exchange(): return lax.ppermute(array, ('tm', 'cells', 'feat'), pairs)  4.71 us
  transfers between devices with their start and end apart: 6, of which 2 were waited for; matrix products, arithmetic and copies ran while one was open for 0% of the time, Pallas kernels for 20%

profile of v7, /device:TPU:0, one launch (start us, length us, event | category | flops | bytes accessed | tf_op | source)
XLA Modules:
  0.0 21.2 jit_solution(952732856557624381)
XLA Ops:
  0.6 1.0 %pack_cells.1 = (bf16[544,128]{1,0:T(8,128)(2,1)S(1)}, f32[8,1024]{1,0:T(8,128)S(1)}) custom-call(s32[2]{0:T(128)} %totals_hbm.1, bf16[1,64,1024]{2,1,0:T(8,128)(2,1)} %feats_hbm.1, f32[1,1024]{1,0:T(1,128)} %weights_hbm.1, s32[1,4,8]{2,1,0:T(4,128)} %lists_hbm.1), custom_call_target="tpu_custom_call" | custom-call | bytes 131072 | tf_op jit(solution)/shard_map/pack_cells/pallas_call | solution.py:239
  1.6 5.0 %collective-permute-start = (bf16[544,128]{1,0:T(8,128)(2,1)S(1)}, bf16[544,128]{1,0:T(8,128)(2,1)S(1)}, u32[]{:S(2)}, u32[]{:S(2)}) collective-permute-start(bf16[544,128]{1,0:T(8,128)(2,1)S(1)} %get-tuple-element.9.payload_ref), channel_id=1, source_target_pairs={{0,12},{1,13},{2,14},{3,15},{4,8},{5,9},{6,10},{7,11},{8,4},{9,5},... | collective-permute-start | bytes 417800 | tf_op jit(solution)/shard_map/ppermute | solution.py:262
  6.6 0.5 %collective-permute-start.2 = (bf16[544,128]{1,0:T(8,128)(2,1)S(1)}, bf16[544,128]{1,0:T(8,128)(2,1)S(1)}, u32[]{:S(2)}, u32[]{:S(2)}) collective-permute-start(bf16[544,128]{1,0:T(8,128)(2,1)S(1)} %get-tuple-element.9.payload_ref), channel_id=1, source_target_pairs={{0,8},{1,9},{2,10},{3,11},{4,12},{5,13},{6,14},{7,15},{8,0},{9,1},... | collective-permute-start | bytes 417800 | tf_op jit(solution)/shard_map/ppermute | solution.py:262
  7.2 1.6 %collective-permute-start.4 = (bf16[544,128]{1,0:T(8,128)(2,1)S(1)}, bf16[544,128]{1,0:T(8,128)(2,1)S(1)}, u32[]{:S(2)}, u32[]{:S(2)}) collective-permute-start(bf16[544,128]{1,0:T(8,128)(2,1)S(1)} %get-tuple-element.9.payload_ref), channel_id=1, source_target_pairs={{0,2},{1,3},{2,0},{3,1},{4,6},{5,7},{6,4},{7,5},{8,10},{9,11},{10,... | collective-permute-start | bytes 417800 | tf_op jit(solution)/shard_map/ppermute | solution.py:262
  8.7 0.2 cell_rows.1.refs_4_
  8.9 4.5 %collective-permute-done.refs_0_ = bf16[544,128]{1,0:T(8,128)(2,1)S(1)} collective-permute-done((bf16[544,128]{1,0:T(8,128)(2,1)S(1)}, bf16[544,128]{1,0:T(8,128)(2,1)S(1)}, u32[]{:S(2)}, u32[]{:S(2)}) %collective-permute-start) | collective-permute-done | bytes 139296 | tf_op jit(solution)/shard_map/ppermute | solution.py:262
  13.4 0.0 collective-permute-start.1
  13.4 0.2 collective-permute-done.2.refs_1_
  13.6 0.3 %collective-permute-start.3 = (bf16[544,128]{1,0:T(8,128)(2,1)S(1)}, bf16[544,128]{1,0:T(8,128)(2,1)S(1)}, u32[]{:S(2)}, u32[]{:S(2)}) collective-permute-start(bf16[544,128]{1,0:T(8,128)(2,1)S(1)} %collective-permute-done.2.refs_1_), channel_id=1, source_target_pairs={{0,1},{1,0},{2,3},{3,2},{4,5},{5,4},{6,7},{7,6},{8,9},{9,8},{10,11... | collective-permute-start | bytes 417800 | tf_op jit(solution)/shard_map/ppermute | solution.py:267
  14.0 0.0 collective-permute-done.4.refs_2_
  14.0 1.2 %sum_tiles.3 = (bf16[1040,128]{1,0:T(8,128)(2,1)S(1)}, f32[1024,128]{1,0:T(8,128)S(1)}) custom-call(bf16[544,128]{1,0:T(8,128)(2,1)S(1)} %collective-permute-done.refs_0_, bf16[544,128]{1,0:T(8,128)(2,1)S(1)} %collective-permute-done.2.refs_1_, bf16[544,128]{1,0:T(8,128)(2,1)S(1)} %collective-permute-done.4.refs_2_), custom_call_target="tpu_custom_call" | custom-call | flops 335544320 | bytes 131072 | tf_op jit(solution)/shard_map/sum_tiles/pallas_call | solution.py:239
  15.2 0.0 collective-permute-done.1.refs_0_.refs_2_
  15.2 0.0 collective-permute-done.3.refs_1_.refs_3_
  15.2 1.3 %sum_tiles.4 = f32[1,1024]{1,0:T(1,128)S(1)} custom-call(bf16[544,128]{1,0:T(8,128)(2,1)S(1)} %collective-permute-done.1.refs_0_.refs_2_, bf16[544,128]{1,0:T(8,128)(2,1)S(1)} %collective-permute-done.3.refs_1_.refs_3_, bf16[1040,128]{1,0:T(8,128)(2,1)S(1)} %get-tuple-element.11.refs_2_, f32[1024,128]{1,0:T(8,128)S(1)} %get-tuple-element.12.refs_3_), custom_call_target="tpu_custom_call" | custom-call | flops 335544320 | bytes 131072 | tf_op jit(solution)/shard_map/sum_tiles/pallas_call | solution.py:239
  16.6 1.2 %collective-permute-start.5 = (f32[1,1024]{1,0:T(1,128)S(1)}, f32[1,1024]{1,0:T(1,128)S(1)}, u32[]{:S(2)}, u32[]{:S(2)}) collective-permute-start(f32[1,1024]{1,0:T(1,128)S(1)} %sum_tiles.4), channel_id=1, source_target_pairs={{0,2},{1,3},{2,0},{3,1},{4,6},{5,7},{6,4},{7,5},{8,10},{9,11},{10,... | collective-permute-start | bytes 12296 | tf_op jit(solution)/shard_map/ppermute | solution.py:262
  17.7 2.8 %sum_tiles.5.refs_1_ = f32[1,1024]{1,0:T(1,128)S(1)} custom-call(bf16[544,128]{1,0:T(8,128)(2,1)S(1)} %collective-permute-done.refs_0_, bf16[544,128]{1,0:T(8,128)(2,1)S(1)} %collective-permute-done.2.refs_1_, bf16[544,128]{1,0:T(8,128)(2,1)S(1)} %collective-permute-done.1.refs_0_.refs_2_, bf16[544,128]{1,0:T(8,128)(2,1)S(1)} %collective-permute-done.3.refs_1_.refs_3_, ...), custom_call_target="tpu_custom_call" | custom-call | flops 671088640 | bytes 131072 | tf_op jit(solution)/shard_map/sum_tiles/pallas_call | solution.py:239
  20.6 0.0 collective-permute-done.5.refs_0_
  20.6 0.6 %end.1 = (f32[1,1024]{1,0:T(1,128)}, f32[1,1024]{1,0:T(1,128)}) custom-call(f32[8,1024]{1,0:T(8,128)S(1)} %get-tuple-element.8.facts_ref, f32[1,1024]{1,0:T(1,128)S(1)} %collective-permute-done.5.refs_0_, f32[1,1024]{1,0:T(1,128)S(1)} %sum_tiles.5.refs_1_), custom_call_target="tpu_custom_call" | custom-call | bytes 131072 | tf_op jit(solution)/shard_map/end/pallas_call | solution.py:239
Async XLA Ops:
  1.6 11.8 %collective-permute-start = (bf16[544,128]{1,0:T(8,128)(2,1)S(1)}, bf16[544,128]{1,0:T(8,128)(2,1)S(1)}, u32[]{:S(2)}, u32[]{:S(2)}) collective-permute-start(bf16[544,128]{1,0:T(8,128)(2,1)S(1)} %get-tuple-element.9.payload_ref), channel_id=1, source_target_pairs={{0,12},{1,13},{2,14},{3,15},{4,8},{5,9},{6,10},{7,11},{8,4},{9,5},... | collective-permute-start | bytes 417800 | tf_op jit(solution)/shard_map/ppermute | solution.py:262
  6.6 7.0 %collective-permute-start.2 = (bf16[544,128]{1,0:T(8,128)(2,1)S(1)}, bf16[544,128]{1,0:T(8,128)(2,1)S(1)}, u32[]{:S(2)}, u32[]{:S(2)}) collective-permute-start(bf16[544,128]{1,0:T(8,128)(2,1)S(1)} %get-tuple-element.9.payload_ref), channel_id=1, source_target_pairs={{0,8},{1,9},{2,10},{3,11},{4,12},{5,13},{6,14},{7,15},{8,0},{9,1},... | collective-permute-start | bytes 417800 | tf_op jit(solution)/shard_map/ppermute | solution.py:262
  7.2 6.8 %collective-permute-start.4 = (bf16[544,128]{1,0:T(8,128)(2,1)S(1)}, bf16[544,128]{1,0:T(8,128)(2,1)S(1)}, u32[]{:S(2)}, u32[]{:S(2)}) collective-permute-start(bf16[544,128]{1,0:T(8,128)(2,1)S(1)} %get-tuple-element.9.payload_ref), channel_id=1, source_target_pairs={{0,2},{1,3},{2,0},{3,1},{4,6},{5,7},{6,4},{7,5},{8,10},{9,11},{10,... | collective-permute-start | bytes 417800 | tf_op jit(solution)/shard_map/ppermute | solution.py:262
  13.4 1.8 %collective-permute-start.1 = (bf16[544,128]{1,0:T(8,128)(2,1)S(1)}, bf16[544,128]{1,0:T(8,128)(2,1)S(1)}, u32[]{:S(2)}, u32[]{:S(2)}) collective-permute-start(bf16[544,128]{1,0:T(8,128)(2,1)S(1)} %collective-permute-done.refs_0_), channel_id=1, source_target_pairs={{0,1},{1,0},{2,3},{3,2},{4,5},{5,4},{6,7},{7,6},{8,9},{9,8},{10,11... | collective-permute-start | bytes 417800 | tf_op jit(solution)/shard_map/ppermute | solution.py:267
  13.6 1.6 %collective-permute-start.3 = (bf16[544,128]{1,0:T(8,128)(2,1)S(1)}, bf16[544,128]{1,0:T(8,128)(2,1)S(1)}, u32[]{:S(2)}, u32[]{:S(2)}) collective-permute-start(bf16[544,128]{1,0:T(8,128)(2,1)S(1)} %collective-permute-done.2.refs_1_), channel_id=1, source_target_pairs={{0,1},{1,0},{2,3},{3,2},{4,5},{5,4},{6,7},{7,6},{8,9},{9,8},{10,11... | collective-permute-start | bytes 417800 | tf_op jit(solution)/shard_map/ppermute | solution.py:267
  16.6 4.0 %collective-permute-start.5 = (f32[1,1024]{1,0:T(1,128)S(1)}, f32[1,1024]{1,0:T(1,128)S(1)}, u32[]{:S(2)}, u32[]{:S(2)}) collective-permute-start(f32[1,1024]{1,0:T(1,128)S(1)} %sum_tiles.4), channel_id=1, source_target_pairs={{0,2},{1,3},{2,0},{3,1},{4,6},{5,7},{6,4},{7,5},{8,10},{9,11},{10,... | collective-permute-start | bytes 12296 | tf_op jit(solution)/shard_map/ppermute | solution.py:262

commit v8 on v6

--- a/solution.py
+++ b/solution.py
@@ -62,7 +62,7 @@
 
 
 def pack_kernel(
-    offset, totals_hbm, feats_hbm, weights_hbm, lists_hbm, payload_ref, facts_ref, *scratch
+    offset, totals_hbm, feats_hbm, weights_hbm, lists_hbm, payload_ref, near_ref, facts_ref, *scratch
 ):
     totals_ref, feats_ref, weights_ref, lists_ref, sems = scratch
     _, feat_count, row_count = feats_ref.shape
@@ -90,6 +90,8 @@
     tail = jnp.concatenate([*pieces(share), listed], axis=0).astype(bf16)
     columns = [feats[:, slab * lanes : (slab + 1) * lanes] for slab in range(slabs)]
     payload_ref[...] = jnp.concatenate([*columns, tail], axis=0)
+    near_tail = jnp.broadcast_to(listed[:1], (list_rows, lanes)).astype(bf16)
+    near_ref[...] = jnp.concatenate([*columns, near_tail], axis=0)
     facts_ref[...] = stacked_rows([weights_ref[...], alive.astype(jnp.float32)], 8, row_count)
 
 
@@ -107,8 +109,8 @@
     )
     columns = jnp.concatenate([wide * (2.0 / (spread * feat_count)), tail], axis=0)
     rows_ref[:row_count, :] = columns.T.astype(bf16)
-    tail = payload_ref[slabs * feat_count :, :].astype(jnp.float32)
-    listed = tail[3 * slabs : 3 * slabs + 1]
+    height = payload_ref.shape[0]
+    listed = payload_ref[height - list_rows :, :].astype(jnp.float32)[list_rows - 1 :]
     rows_ref[row_count:, :] = jnp.broadcast_to(listed, (list_rows, lanes)).astype(bf16)
 
 
@@ -286,6 +288,7 @@
             "pack_cells",
             (
                 jax.ShapeDtypeStruct((payload_rows, lanes), bf16),
+                jax.ShapeDtypeStruct((feat_count * row_count // lanes + list_rows, lanes), bf16),
                 jax.ShapeDtypeStruct((8, row_count), jnp.float32),
             ),
             in_hbm(living_totals, principal_coordinates, weights, destination_tiles),
@@ -311,7 +314,7 @@
         return call(functools.partial(rows_kernel, list_shape), "cell_rows", rows_shape, [payload])
 
     def summed(pack, step):
-        payload, _ = pack
+        payload, near_payload, _ = pack
         forward = None if step is None else step > 0
         moves = (1, -1) if step is None else (step,)
         *distances, far = range(0, count, 2 if xor else 1)
@@ -355,7 +358,7 @@
             return [added(jobs, own, group_of_own, finished=True)]
 
         near_group = functools.partial(group_of, 1)
-        near = exchange(payload, ((0,), shifted(1)))
+        near = exchange(near_payload, ((0,), shifted(1)))
         ready, _ = lax.optimization_barrier((far_shard, own))
         direct = [job(far_shard, far, 0), *batch(0)]
         crossed = [job(ready, far, swap) for swap in range(1, cores)]
@@ -374,7 +377,7 @@
         pack = packed(present_potentials)
         parts = summed(pack, None)
         return tuple(
-            call(functools.partial(end_kernel, len(parts)), "end", (row, row), [pack[1], *parts])
+            call(functools.partial(end_kernel, len(parts)), "end", (row, row), [pack[2], *parts])
         )
 
     time_here = lax.axis_index("tm")

time: 21.1 us -> 21.1 us (level)
  starting transfers between devices: 8.51 us -> 8.9 us
  waiting for transfers between devices: 5.27 us -> 4.88 us
    ppermute x4, waiting for transfers between devices: 5.13 us -> 4.73 us  [exchange(): return lax.ppermute(array, ('tm', 'cells', 'feat'), pairs)]
    ppermute x4, starting transfers between devices: 8.16 us -> 8.55 us  [exchange(): return lax.ppermute(array, ('tm', 'cells', 'feat'), pairs)]
  transfers between devices with their start and end apart: 6 -> 6, of which waited for: 4 -> 3; matrix products, arithmetic and copies ran while one was open for 0% -> 0% of each run, Pallas kernels for 16% -> 16%
where the time goes in v8:
time: 21.1 us; the launch traced here: 20.9 us
  starting transfers between devices  8.9 us (42%)
  Pallas kernels  6.43 us (30%)
  waiting for transfers between devices  4.88 us (23%)
  between operations  0.68 us (3%)
    ppermute x4, starting transfers between devices, exchange(): return lax.ppermute(array, ('tm', 'cells', 'feat'), pairs)  8.55 us
    pallas_call x6, Pallas kernels, call(): pl.pallas_call(kernel, name=name, out_shape=out_shapes, in_specs=[pl.Bloc...  6.43 us
    ppermute x4, waiting for transfers between devices, exchange(): return lax.ppermute(array, ('tm', 'cells', 'feat'), pairs)  4.73 us
  transfers between devices with their start and end apart: 6, of which 3 were waited for; matrix products, arithmetic and copies ran while one was open for 0% of the time, Pallas kernels for 16%

profile of v8, /device:TPU:0, one launch (start us, length us, event | category | flops | bytes accessed | tf_op | source)
XLA Modules:
  0.0 20.9 jit_solution(3853797336443570705)
XLA Ops:
  0.6 1.0 %pack_cells.1 = (bf16[544,128]{1,0:T(8,128)(2,1)S(1)}, bf16[528,128]{1,0:T(8,128)(2,1)S(1)}, f32[8,1024]{1,0:T(8,128)S(1)}) custom-call(s32[2]{0:T(128)} %totals_hbm.1, bf16[1,64,1024]{2,1,0:T(8,128)(2,1)} %feats_hbm.1, f32[1,1024]{1,0:T(1,128)} %weights_hbm.1, s32[1,4,8]{2,1,0:T(4,128)} %lists_hbm.1), custom_call_target="tpu_custom_call" | custom-call | bytes 131072 | tf_op jit(solution)/shard_map/pack_cells/pallas_call | solution.py:232
  1.6 5.0 %collective-permute-start = (bf16[544,128]{1,0:T(8,128)(2,1)S(1)}, bf16[544,128]{1,0:T(8,128)(2,1)S(1)}, u32[]{:S(2)}, u32[]{:S(2)}) collective-permute-start(bf16[544,128]{1,0:T(8,128)(2,1)S(1)} %get-tuple-element.10.payload_ref), channel_id=1, source_target_pairs={{0,12},{1,13},{2,14},{3,15},{4,8},{5,9},{6,10},{7,11},{8,4},{9,5},... | collective-permute-start | bytes 417800 | tf_op jit(solution)/shard_map/ppermute | solution.py:255
  6.6 0.5 %collective-permute-start.2 = (bf16[544,128]{1,0:T(8,128)(2,1)S(1)}, bf16[544,128]{1,0:T(8,128)(2,1)S(1)}, u32[]{:S(2)}, u32[]{:S(2)}) collective-permute-start(bf16[544,128]{1,0:T(8,128)(2,1)S(1)} %get-tuple-element.10.payload_ref), channel_id=1, source_target_pairs={{0,8},{1,9},{2,10},{3,11},{4,12},{5,13},{6,14},{7,15},{8,0},{9,1},... | collective-permute-start | bytes 417800 | tf_op jit(solution)/shard_map/ppermute | solution.py:255
  7.2 1.6 %collective-permute-start.4 = (bf16[528,128]{1,0:T(8,128)(2,1)S(1)}, bf16[528,128]{1,0:T(8,128)(2,1)S(1)}, u32[]{:S(2)}, u32[]{:S(2)}) collective-permute-start(bf16[528,128]{1,0:T(8,128)(2,1)S(1)} %get-tuple-element.12), channel_id=1, source_target_pairs={{0,2},{1,3},{2,0},{3,1},{4,6},{5,7},{6,4},{7,5},{8,10},{9,11},{10,... | collective-permute-start | bytes 405512 | tf_op jit(solution)/shard_map/ppermute | solution.py:255
  8.7 0.2 cell_rows.1.refs_4_
  8.9 4.5 %collective-permute-done.refs_0_ = bf16[544,128]{1,0:T(8,128)(2,1)S(1)} collective-permute-done((bf16[544,128]{1,0:T(8,128)(2,1)S(1)}, bf16[544,128]{1,0:T(8,128)(2,1)S(1)}, u32[]{:S(2)}, u32[]{:S(2)}) %collective-permute-start) | collective-permute-done | bytes 139296 | tf_op jit(solution)/shard_map/ppermute | solution.py:255
  13.4 0.0 collective-permute-start.1
  13.4 0.2 collective-permute-done.2.refs_1_
  13.6 0.3 %collective-permute-start.3 = (bf16[544,128]{1,0:T(8,128)(2,1)S(1)}, bf16[544,128]{1,0:T(8,128)(2,1)S(1)}, u32[]{:S(2)}, u32[]{:S(2)}) collective-permute-start(bf16[544,128]{1,0:T(8,128)(2,1)S(1)} %collective-permute-done.2.refs_1_), channel_id=1, source_target_pairs={{0,1},{1,0},{2,3},{3,2},{4,5},{5,4},{6,7},{7,6},{8,9},{9,8},{10,11... | collective-permute-start | bytes 417800 | tf_op jit(solution)/shard_map/ppermute | solution.py:260
  14.0 0.0 collective-permute-done.4.refs_2_
  14.0 0.9 %sum_tiles.3 = (bf16[1040,128]{1,0:T(8,128)(2,1)S(1)}, f32[1024,128]{1,0:T(8,128)S(1)}) custom-call(bf16[544,128]{1,0:T(8,128)(2,1)S(1)} %collective-permute-done.refs_0_, bf16[544,128]{1,0:T(8,128)(2,1)S(1)} %collective-permute-done.2.refs_1_, bf16[528,128]{1,0:T(8,128)(2,1)S(1)} %collective-permute-done.4.refs_2_), custom_call_target="tpu_custom_call" | custom-call | flops 335544320 | bytes 131072 | tf_op jit(solution)/shard_map/sum_tiles/pallas_call | solution.py:232
  14.8 0.0 collective-permute-done.1.refs_0_.refs_2_
  14.9 0.1 collective-permute-done.3.refs_1_.refs_3_
  15.0 1.6 %sum_tiles.4 = f32[1,1024]{1,0:T(1,128)S(1)} custom-call(bf16[544,128]{1,0:T(8,128)(2,1)S(1)} %collective-permute-done.1.refs_0_.refs_2_, bf16[544,128]{1,0:T(8,128)(2,1)S(1)} %collective-permute-done.3.refs_1_.refs_3_, bf16[1040,128]{1,0:T(8,128)(2,1)S(1)} %get-tuple-element.13.refs_2_, f32[1024,128]{1,0:T(8,128)S(1)} %get-tuple-element.14.refs_3_), custom_call_target="tpu_custom_call" | custom-call | flops 335544320 | bytes 131072 | tf_op jit(solution)/shard_map/sum_tiles/pallas_call | solution.py:232
  16.6 1.4 %collective-permute-start.5 = (f32[1,1024]{1,0:T(1,128)S(1)}, f32[1,1024]{1,0:T(1,128)S(1)}, u32[]{:S(2)}, u32[]{:S(2)}) collective-permute-start(f32[1,1024]{1,0:T(1,128)S(1)} %sum_tiles.4), channel_id=1, source_target_pairs={{0,2},{1,3},{2,0},{3,1},{4,6},{5,7},{6,4},{7,5},{8,10},{9,11},{10,... | collective-permute-start | bytes 12296 | tf_op jit(solution)/shard_map/ppermute | solution.py:255
  18.0 2.2 %sum_tiles.5.refs_1_ = f32[1,1024]{1,0:T(1,128)S(1)} custom-call(bf16[544,128]{1,0:T(8,128)(2,1)S(1)} %collective-permute-done.refs_0_, bf16[544,128]{1,0:T(8,128)(2,1)S(1)} %collective-permute-done.2.refs_1_, bf16[544,128]{1,0:T(8,128)(2,1)S(1)} %collective-permute-done.1.refs_0_.refs_2_, bf16[544,128]{1,0:T(8,128)(2,1)S(1)} %collective-permute-done.3.refs_1_.refs_3_, ...), custom_call_target="tpu_custom_call" | custom-call | flops 671088640 | bytes 131072 | tf_op jit(solution)/shard_map/sum_tiles/pallas_call | solution.py:232
  20.2 0.0 collective-permute-done.5.refs_0_
  20.2 0.6 %end.1 = (f32[1,1024]{1,0:T(1,128)}, f32[1,1024]{1,0:T(1,128)}) custom-call(f32[8,1024]{1,0:T(8,128)S(1)} %get-tuple-element.9.facts_ref, f32[1,1024]{1,0:T(1,128)S(1)} %collective-permute-done.5.refs_0_, f32[1,1024]{1,0:T(1,128)S(1)} %sum_tiles.5.refs_1_), custom_call_target="tpu_custom_call" | custom-call | bytes 131072 | tf_op jit(solution)/shard_map/end/pallas_call | solution.py:232
Async XLA Ops:
  1.6 11.8 %collective-permute-start = (bf16[544,128]{1,0:T(8,128)(2,1)S(1)}, bf16[544,128]{1,0:T(8,128)(2,1)S(1)}, u32[]{:S(2)}, u32[]{:S(2)}) collective-permute-start(bf16[544,128]{1,0:T(8,128)(2,1)S(1)} %get-tuple-element.10.payload_ref), channel_id=1, source_target_pairs={{0,12},{1,13},{2,14},{3,15},{4,8},{5,9},{6,10},{7,11},{8,4},{9,5},... | collective-permute-start | bytes 417800 | tf_op jit(solution)/shard_map/ppermute | solution.py:255
  6.6 7.0 %collective-permute-start.2 = (bf16[544,128]{1,0:T(8,128)(2,1)S(1)}, bf16[544,128]{1,0:T(8,128)(2,1)S(1)}, u32[]{:S(2)}, u32[]{:S(2)}) collective-permute-start(bf16[544,128]{1,0:T(8,128)(2,1)S(1)} %get-tuple-element.10.payload_ref), channel_id=1, source_target_pairs={{0,8},{1,9},{2,10},{3,11},{4,12},{5,13},{6,14},{7,15},{8,0},{9,1},... | collective-permute-start | bytes 417800 | tf_op jit(solution)/shard_map/ppermute | solution.py:255
  7.2 6.8 %collective-permute-start.4 = (bf16[528,128]{1,0:T(8,128)(2,1)S(1)}, bf16[528,128]{1,0:T(8,128)(2,1)S(1)}, u32[]{:S(2)}, u32[]{:S(2)}) collective-permute-start(bf16[528,128]{1,0:T(8,128)(2,1)S(1)} %get-tuple-element.12), channel_id=1, source_target_pairs={{0,2},{1,3},{2,0},{3,1},{4,6},{5,7},{6,4},{7,5},{8,10},{9,11},{10,... | collective-permute-start | bytes 405512 | tf_op jit(solution)/shard_map/ppermute | solution.py:255
  13.4 1.4 %collective-permute-start.1 = (bf16[544,128]{1,0:T(8,128)(2,1)S(1)}, bf16[544,128]{1,0:T(8,128)(2,1)S(1)}, u32[]{:S(2)}, u32[]{:S(2)}) collective-permute-start(bf16[544,128]{1,0:T(8,128)(2,1)S(1)} %collective-permute-done.refs_0_), channel_id=1, source_target_pairs={{0,1},{1,0},{2,3},{3,2},{4,5},{5,4},{6,7},{7,6},{8,9},{9,8},{10,11... | collective-permute-start | bytes 417800 | tf_op jit(solution)/shard_map/ppermute | solution.py:260
  13.6 1.4 %collective-permute-start.3 = (bf16[544,128]{1,0:T(8,128)(2,1)S(1)}, bf16[544,128]{1,0:T(8,128)(2,1)S(1)}, u32[]{:S(2)}, u32[]{:S(2)}) collective-permute-start(bf16[544,128]{1,0:T(8,128)(2,1)S(1)} %collective-permute-done.2.refs_1_), channel_id=1, source_target_pairs={{0,1},{1,0},{2,3},{3,2},{4,5},{5,4},{6,7},{7,6},{8,9},{9,8},{10,11... | collective-permute-start | bytes 417800 | tf_op jit(solution)/shard_map/ppermute | solution.py:260
  16.6 3.7 %collective-permute-start.5 = (f32[1,1024]{1,0:T(1,128)S(1)}, f32[1,1024]{1,0:T(1,128)S(1)}, u32[]{:S(2)}, u32[]{:S(2)}) collective-permute-start(f32[1,1024]{1,0:T(1,128)S(1)} %sum_tiles.4), channel_id=1, source_target_pairs={{0,2},{1,3},{2,0},{3,1},{4,6},{5,7},{6,4},{7,5},{8,10},{9,11},{10,... | collective-permute-start | bytes 12296 | tf_op jit(solution)/shard_map/ppermute | solution.py:255

commit v9 on v8

--- a/solution.py
+++ b/solution.py
@@ -171,10 +171,10 @@
     for place in range(pairs_at_once - 1):
         list_ref[count + place] = jnp.int32(pair_total)
 
-    def step(index, carry):
+    def step(taken, size):
         sums = []
-        for place in range(pairs_at_once):
-            listed = list_ref[index * pairs_at_once + place]
+        for place in range(size):
+            listed = list_ref[taken + place]
             pair = jnp.minimum(listed, pair_total - 1)
             block, other = lax.rem(pair // source_count, source_count), lax.rem(pair, source_count)
             row = pl.multiple_of(block * block_len, block_len)
@@ -195,9 +195,18 @@
             sums.append((jnp.where(listed < pair_total, row, row_count), added))
         for row, added in sums:
             total_ref[pl.ds(pl.multiple_of(row, block_len), block_len), :] += added
+
+    def whole_step(index, carry):
+        step(index * pairs_at_once, pairs_at_once)
         return carry
 
-    lax.fori_loop(0, (count + pairs_at_once - 1) // pairs_at_once, step, 0)
+    half = pairs_at_once // 2
+    whole_steps = (count + pairs_at_once - 1 - half) // pairs_at_once
+    lax.fori_loop(0, whole_steps, whole_step, 0)
+
+    @pl.when(count > whole_steps * pairs_at_once)
+    def _():
+        step(whole_steps * pairs_at_once, half)
 
 
 def sum_kernel(groups, ours, forward, list_shape, built, started, finished, *refs):

time: 21.1 us -> 21.1 us (level); the launches traced: 20.9 us -> 21.2 us
  Pallas kernels: 6.43 us -> 7.01 us
    pallas_call x6, Pallas kernels: 6.43 us -> 7.01 us  [call(): pl.pallas_call(kernel, name=name, out_shape=out_shapes, in_specs=[pl.Bloc...]
  transfers between devices with their start and end apart: 6 -> 6, of which waited for: 3 -> 2; matrix products, arithmetic and copies ran while one was open for 0% -> 0% of each run, Pallas kernels for 16% -> 21%
where the time goes in v9:
time: 21.1 us; the launch traced here: 21.2 us
  starting transfers between devices  8.79 us (42%)
  Pallas kernels  7.01 us (33%)
  waiting for transfers between devices  4.72 us (22%)
  between operations  0.69 us (3%)
    ppermute x4, starting transfers between devices, exchange(): return lax.ppermute(array, ('tm', 'cells', 'feat'), pairs)  8.44 us
    pallas_call x6, Pallas kernels, call(): pl.pallas_call(kernel, name=name, out_shape=out_shapes, in_specs=[pl.Bloc...  7.01 us
    ppermute x4, waiting for transfers between devices, exchange(): return lax.ppermute(array, ('tm', 'cells', 'feat'), pairs)  4.71 us
  transfers between devices with their start and end apart: 6, of which 2 were waited for; matrix products, arithmetic and copies ran while one was open for 0% of the time, Pallas kernels for 21%

profile of v9, /device:TPU:0, one launch (start us, length us, event | category | flops | bytes accessed | tf_op | source)
XLA Modules:
  0.0 21.2 jit_solution(15437289723003031757)
XLA Ops:
  0.6 1.0 %pack_cells.1 = (bf16[544,128]{1,0:T(8,128)(2,1)S(1)}, bf16[528,128]{1,0:T(8,128)(2,1)S(1)}, f32[8,1024]{1,0:T(8,128)S(1)}) custom-call(s32[2]{0:T(128)} %totals_hbm.1, bf16[1,64,1024]{2,1,0:T(8,128)(2,1)} %feats_hbm.1, f32[1,1024]{1,0:T(1,128)} %weights_hbm.1, s32[1,4,8]{2,1,0:T(4,128)} %lists_hbm.1), custom_call_target="tpu_custom_call" | custom-call | bytes 131072 | tf_op jit(solution)/shard_map/pack_cells/pallas_call | solution.py:241
  1.6 5.0 %collective-permute-start = (bf16[544,128]{1,0:T(8,128)(2,1)S(1)}, bf16[544,128]{1,0:T(8,128)(2,1)S(1)}, u32[]{:S(2)}, u32[]{:S(2)}) collective-permute-start(bf16[544,128]{1,0:T(8,128)(2,1)S(1)} %get-tuple-element.10.payload_ref), channel_id=1, source_target_pairs={{0,12},{1,13},{2,14},{3,15},{4,8},{5,9},{6,10},{7,11},{8,4},{9,5},... | collective-permute-start | bytes 417800 | tf_op jit(solution)/shard_map/ppermute | solution.py:264
  6.6 0.5 %collective-permute-start.2 = (bf16[544,128]{1,0:T(8,128)(2,1)S(1)}, bf16[544,128]{1,0:T(8,128)(2,1)S(1)}, u32[]{:S(2)}, u32[]{:S(2)}) collective-permute-start(bf16[544,128]{1,0:T(8,128)(2,1)S(1)} %get-tuple-element.10.payload_ref), channel_id=1, source_target_pairs={{0,8},{1,9},{2,10},{3,11},{4,12},{5,13},{6,14},{7,15},{8,0},{9,1},... | collective-permute-start | bytes 417800 | tf_op jit(solution)/shard_map/ppermute | solution.py:264
  7.2 1.6 %collective-permute-start.4 = (bf16[528,128]{1,0:T(8,128)(2,1)S(1)}, bf16[528,128]{1,0:T(8,128)(2,1)S(1)}, u32[]{:S(2)}, u32[]{:S(2)}) collective-permute-start(bf16[528,128]{1,0:T(8,128)(2,1)S(1)} %get-tuple-element.12), channel_id=1, source_target_pairs={{0,2},{1,3},{2,0},{3,1},{4,6},{5,7},{6,4},{7,5},{8,10},{9,11},{10,... | collective-permute-start | bytes 405512 | tf_op jit(solution)/shard_map/ppermute | solution.py:264
  8.7 0.2 cell_rows.1.refs_4_
  8.9 4.5 %collective-permute-done.refs_0_ = bf16[544,128]{1,0:T(8,128)(2,1)S(1)} collective-permute-done((bf16[544,128]{1,0:T(8,128)(2,1)S(1)}, bf16[544,128]{1,0:T(8,128)(2,1)S(1)}, u32[]{:S(2)}, u32[]{:S(2)}) %collective-permute-start) | collective-permute-done | bytes 139296 | tf_op jit(solution)/shard_map/ppermute | solution.py:264
  13.4 0.0 collective-permute-start.1
  13.4 0.2 collective-permute-done.2.refs_1_
  13.6 0.3 %collective-permute-start.3 = (bf16[544,128]{1,0:T(8,128)(2,1)S(1)}, bf16[544,128]{1,0:T(8,128)(2,1)S(1)}, u32[]{:S(2)}, u32[]{:S(2)}) collective-permute-start(bf16[544,128]{1,0:T(8,128)(2,1)S(1)} %collective-permute-done.2.refs_1_), channel_id=1, source_target_pairs={{0,1},{1,0},{2,3},{3,2},{4,5},{5,4},{6,7},{7,6},{8,9},{9,8},{10,11... | collective-permute-start | bytes 417800 | tf_op jit(solution)/shard_map/ppermute | solution.py:269
  14.0 0.0 collective-permute-done.4.refs_2_
  14.0 1.4 %sum_tiles.3 = (bf16[1040,128]{1,0:T(8,128)(2,1)S(1)}, f32[1024,128]{1,0:T(8,128)S(1)}) custom-call(bf16[544,128]{1,0:T(8,128)(2,1)S(1)} %collective-permute-done.refs_0_, bf16[544,128]{1,0:T(8,128)(2,1)S(1)} %collective-permute-done.2.refs_1_, bf16[528,128]{1,0:T(8,128)(2,1)S(1)} %collective-permute-done.4.refs_2_), custom_call_target="tpu_custom_call" | custom-call | flops 335544320 | bytes 131072 | tf_op jit(solution)/shard_map/sum_tiles/pallas_call | solution.py:241
  15.4 0.0 collective-permute-done.1.refs_0_.refs_2_
  15.4 0.0 collective-permute-done.3.refs_1_.refs_3_
  15.4 1.0 %sum_tiles.4 = f32[1,1024]{1,0:T(1,128)S(1)} custom-call(bf16[544,128]{1,0:T(8,128)(2,1)S(1)} %collective-permute-done.1.refs_0_.refs_2_, bf16[544,128]{1,0:T(8,128)(2,1)S(1)} %collective-permute-done.3.refs_1_.refs_3_, bf16[1040,128]{1,0:T(8,128)(2,1)S(1)} %get-tuple-element.13.refs_2_, f32[1024,128]{1,0:T(8,128)S(1)} %get-tuple-element.14.refs_3_), custom_call_target="tpu_custom_call" | custom-call | flops 335544320 | bytes 131072 | tf_op jit(solution)/shard_map/sum_tiles/pallas_call | solution.py:241
  16.4 1.3 %collective-permute-start.5 = (f32[1,1024]{1,0:T(1,128)S(1)}, f32[1,1024]{1,0:T(1,128)S(1)}, u32[]{:S(2)}, u32[]{:S(2)}) collective-permute-start(f32[1,1024]{1,0:T(1,128)S(1)} %sum_tiles.4), channel_id=1, source_target_pairs={{0,2},{1,3},{2,0},{3,1},{4,6},{5,7},{6,4},{7,5},{8,10},{9,11},{10,... | collective-permute-start | bytes 12296 | tf_op jit(solution)/shard_map/ppermute | solution.py:264
  17.7 2.8 %sum_tiles.5.refs_1_ = f32[1,1024]{1,0:T(1,128)S(1)} custom-call(bf16[544,128]{1,0:T(8,128)(2,1)S(1)} %collective-permute-done.refs_0_, bf16[544,128]{1,0:T(8,128)(2,1)S(1)} %collective-permute-done.2.refs_1_, bf16[544,128]{1,0:T(8,128)(2,1)S(1)} %collective-permute-done.1.refs_0_.refs_2_, bf16[544,128]{1,0:T(8,128)(2,1)S(1)} %collective-permute-done.3.refs_1_.refs_3_, ...), custom_call_target="tpu_custom_call" | custom-call | flops 671088640 | bytes 131072 | tf_op jit(solution)/shard_map/sum_tiles/pallas_call | solution.py:241
  20.6 0.0 collective-permute-done.5.refs_0_
  20.6 0.6 %end.1 = (f32[1,1024]{1,0:T(1,128)}, f32[1,1024]{1,0:T(1,128)}) custom-call(f32[8,1024]{1,0:T(8,128)S(1)} %get-tuple-element.9.facts_ref, f32[1,1024]{1,0:T(1,128)S(1)} %collective-permute-done.5.refs_0_, f32[1,1024]{1,0:T(1,128)S(1)} %sum_tiles.5.refs_1_), custom_call_target="tpu_custom_call" | custom-call | bytes 131072 | tf_op jit(solution)/shard_map/end/pallas_call | solution.py:241
Async XLA Ops:
  1.6 11.8 %collective-permute-start = (bf16[544,128]{1,0:T(8,128)(2,1)S(1)}, bf16[544,128]{1,0:T(8,128)(2,1)S(1)}, u32[]{:S(2)}, u32[]{:S(2)}) collective-permute-start(bf16[544,128]{1,0:T(8,128)(2,1)S(1)} %get-tuple-element.10.payload_ref), channel_id=1, source_target_pairs={{0,12},{1,13},{2,14},{3,15},{4,8},{5,9},{6,10},{7,11},{8,4},{9,5},... | collective-permute-start | bytes 417800 | tf_op jit(solution)/shard_map/ppermute | solution.py:264
  6.6 7.0 %collective-permute-start.2 = (bf16[544,128]{1,0:T(8,128)(2,1)S(1)}, bf16[544,128]{1,0:T(8,128)(2,1)S(1)}, u32[]{:S(2)}, u32[]{:S(2)}) collective-permute-start(bf16[544,128]{1,0:T(8,128)(2,1)S(1)} %get-tuple-element.10.payload_ref), channel_id=1, source_target_pairs={{0,8},{1,9},{2,10},{3,11},{4,12},{5,13},{6,14},{7,15},{8,0},{9,1},... | collective-permute-start | bytes 417800 | tf_op jit(solution)/shard_map/ppermute | solution.py:264
  7.2 6.8 %collective-permute-start.4 = (bf16[528,128]{1,0:T(8,128)(2,1)S(1)}, bf16[528,128]{1,0:T(8,128)(2,1)S(1)}, u32[]{:S(2)}, u32[]{:S(2)}) collective-permute-start(bf16[528,128]{1,0:T(8,128)(2,1)S(1)} %get-tuple-element.12), channel_id=1, source_target_pairs={{0,2},{1,3},{2,0},{3,1},{4,6},{5,7},{6,4},{7,5},{8,10},{9,11},{10,... | collective-permute-start | bytes 405512 | tf_op jit(solution)/shard_map/ppermute | solution.py:264
  13.4 2.0 %collective-permute-start.1 = (bf16[544,128]{1,0:T(8,128)(2,1)S(1)}, bf16[544,128]{1,0:T(8,128)(2,1)S(1)}, u32[]{:S(2)}, u32[]{:S(2)}) collective-permute-start(bf16[544,128]{1,0:T(8,128)(2,1)S(1)} %collective-permute-done.refs_0_), channel_id=1, source_target_pairs={{0,1},{1,0},{2,3},{3,2},{4,5},{5,4},{6,7},{7,6},{8,9},{9,8},{10,11... | collective-permute-start | bytes 417800 | tf_op jit(solution)/shard_map/ppermute | solution.py:269
  13.6 1.8 %collective-permute-start.3 = (bf16[544,128]{1,0:T(8,128)(2,1)S(1)}, bf16[544,128]{1,0:T(8,128)(2,1)S(1)}, u32[]{:S(2)}, u32[]{:S(2)}) collective-permute-start(bf16[544,128]{1,0:T(8,128)(2,1)S(1)} %collective-permute-done.2.refs_1_), channel_id=1, source_target_pairs={{0,1},{1,0},{2,3},{3,2},{4,5},{5,4},{6,7},{7,6},{8,9},{9,8},{10,11... | collective-permute-start | bytes 417800 | tf_op jit(solution)/shard_map/ppermute | solution.py:269
  16.4 4.1 %collective-permute-start.5 = (f32[1,1024]{1,0:T(1,128)S(1)}, f32[1,1024]{1,0:T(1,128)S(1)}, u32[]{:S(2)}, u32[]{:S(2)}) collective-permute-start(f32[1,1024]{1,0:T(1,128)S(1)} %sum_tiles.4), channel_id=1, source_target_pairs={{0,2},{1,3},{2,0},{3,1},{4,6},{5,7},{6,4},{7,5},{8,10},{9,11},{10,... | collective-permute-start | bytes 12296 | tf_op jit(solution)/shard_map/ppermute | solution.py:264
